TPU v7x, 128 devices: a whole 4x4x4 slice. The times are simulated.
128 devices in a mesh: ctx: 16 (over z, y_lo, core), fsdp: 8 (over y_hi, x).
Axes of the slice: x: 4, y: 4 (y_hi: 2, y_lo: 2; y = y_hi * 2 + y_lo), z: 4, core: 2. Of those that a mesh axis runs over, the one named last changes fastest.
Arguments:
- tokens: bfloat16 [8, 2048, 1024], P('fsdp', 'ctx'), may hold values from -6 to 6
- upstream: bfloat16 [8, 2048, 1024], P('fsdp', 'ctx'), may hold values from -6 to 6
- block_pairs: int32 [8, 16], P('fsdp'), may hold values from 0 to 15, as said below
- rotary_place: int32 [8, 2048], P('fsdp', 'ctx'), may hold values from 0 to 2047, as said below
- first_gain: bfloat16 [1024], P('fsdp'), may hold values from 0.25 to 1.75
- first_shift: bfloat16 [1024], P('fsdp'), may hold values from -1.25 to 1.25
- joint_weight: bfloat16 [1024, 3072], P('fsdp'), may hold values from -0.1875 to 0.1875
- joint_bias: bfloat16 [3072], P('fsdp'), may hold values from -1.75 to 1.75
- dense_weight: bfloat16 [1024, 1024], P('fsdp'), may hold values from -3 to 3
- dense_bias: bfloat16 [1024], P('fsdp'), may hold values from -1.75 to 1.75
- second_gain: bfloat16 [1024], P('fsdp'), may hold values from 0.25 to 1.75
- second_shift: bfloat16 [1024], P('fsdp'), may hold values from -1.25 to 1.25
- widen_weight: bfloat16 [1024, 4096], P('fsdp'), may hold values from -0.1875 to 0.1875
- widen_bias: bfloat16 [4096], P('fsdp'), may hold values from -3 to 3
- narrow_weight: bfloat16 [4096, 1024], P('fsdp'), may hold values from -0.09375 to 0.09375
- narrow_bias: bfloat16 [1024], P('fsdp'), may hold values from -1.75 to 1.75
Outputs:
- block_out: bfloat16 [8, 2048, 1024], P('fsdp', 'ctx')
- tokens_grad: float32 [8, 2048, 1024], P('fsdp', 'ctx')
- first_gain_grad: float32 [1024], P('fsdp')
- first_shift_grad: float32 [1024], P('fsdp')
- joint_weight_grad: float32 [1024, 3072], P('fsdp')
- joint_bias_grad: float32 [3072], P('fsdp')
- dense_weight_grad: float32 [1024, 1024], P('fsdp')
- dense_bias_grad: float32 [1024], P('fsdp')
- second_gain_grad: float32 [1024], P('fsdp')
- second_shift_grad: float32 [1024], P('fsdp')
- widen_weight_grad: float32 [1024, 4096], P('fsdp')
- widen_bias_grad: float32 [4096], P('fsdp')
- narrow_weight_grad: float32 [4096, 1024], P('fsdp')
- narrow_bias_grad: float32 [1024], P('fsdp')
Inputs may be any that keep to these rules, and one draw needn't show every extreme that they name: Each row names every value once; in sequence s the rows of ctx index c hold causal blocks p and 31 - p, p = block_pairs[s, c], the lower block first. `rotary_place`: a row's causal place minus the causal place where its document begins; each sequence's first document begins at place 0, the others at places drawn from the seed; one sequence, drawn from the seed, is a single document.
All inputs are finite; a program needn't handle non-finite values.
Results may differ from a plain program's by a relative error of at most 0.024.
Values may be sent and summed in bfloat16 or wider, within the bound.
No kernel may reach another device: no remote copies, remote signals or barrier semaphores. Data moves between devices by JAX's collectives and lax.ppermute only.
A program may use at most 192 MiB of HBM per device.

v0:
```python
import jax
import jax.numpy as jnp
from jax import lax
from jax.experimental import pallas as pl
from jax.experimental.pallas import tpu as pltpu
from jax.sharding import PartitionSpec as P

HEADS = 16
EPSILON = 1e-05
NEGATIVE = -1e30
ROTARY_BASE = 10000.0
N_CTX = 16
N_FSDP = 8
F32 = jnp.float32
BF16 = jnp.bfloat16

OTHER_CORE = [(i ^ 1, i) for i in range(16)]
SAME_CORE = [list(range(0, 16, 2)), list(range(1, 16, 2))]
TURN = [(c * 8 + f, (2 * f + (c & 1)) * 8 + (c >> 1)) for c in range(16) for f in range(8)]


def turn(v):
    return lax.ppermute(v, ("ctx", "fsdp"), TURN)


def dot_tn(a, b):
    return lax.dot_general(a, b, (((0,), (0,)), ((), ())), preferred_element_type=F32)


def dot_nt(a, b):
    return lax.dot_general(a, b, (((1,), (1,)), ((), ())), preferred_element_type=F32)


def dot_nn(a, b):
    return jnp.dot(a, b, preferred_element_type=F32)


def project_kernel(x_ref, up_ref, wj_ref, ww_ref, add_ref, back_ref, xhat_ref, joint_ref, grad_ref, act_ref, wg_ref):
    block, width = x_ref.shape[0] * x_ref.shape[1], x_ref.shape[2]
    x = x_ref[...].reshape(block, width).astype(F32)
    center = x - jnp.mean(x, axis=-1, keepdims=True)
    xhat = (center * lax.rsqrt(jnp.mean(center * center, axis=-1, keepdims=True) + EPSILON)).astype(BF16)
    xhat_ref[...] = xhat
    wide = wj_ref.shape[1]
    joint_ref[...] = dot_nn(xhat, wj_ref[...]) + add_ref[0:1, :wide]
    widened = dot_nn(xhat, ww_ref[...]) + add_ref[0:1, wide:]
    phi = 0.5 * (1.0 + lax.erf(widened * (0.5 ** 0.5)))
    act_ref[...] = (widened * phi).astype(BF16)
    slope = phi + widened * jnp.exp(-0.5 * widened * widened) * 0.3989422804014327
    up = up_ref[...].reshape(block, width)
    hd = back_ref.shape[0] - ww_ref.shape[1]
    grad_ref[...] = dot_nt(up, back_ref[0:hd, :])
    wg_ref[...] = (dot_nt(up, back_ref[hd:, :]) * slope).astype(BF16)


def project(both, wj, ww, add, back):
    slots, _, width = both.shape
    own, per = 128, 2
    rows, block = slots * own, per * own
    wide, ffc = wj.shape[1], ww.shape[1]
    hd = back.shape[0] - ffc
    whole = lambda a: pl.BlockSpec(a.shape, lambda i: (0, 0))
    tall = lambda n: pl.BlockSpec((block, n), lambda i: (i, 0))
    return pl.pallas_call(
        project_kernel,
        grid=(slots // per,),
        in_specs=[
            pl.BlockSpec((per, own, width), lambda i: (i, 0, 0)),
            pl.BlockSpec((per, own, width), lambda i: (i, 1, 0)),
            whole(wj), whole(ww), whole(add), whole(back)],
        out_specs=[tall(width), tall(wide), tall(hd), tall(ffc), tall(ffc)],
        out_shape=[
            jax.ShapeDtypeStruct((rows, width), BF16), jax.ShapeDtypeStruct((rows, wide), F32),
            jax.ShapeDtypeStruct((rows, hd), F32), jax.ShapeDtypeStruct((rows, ffc), BF16),
            jax.ShapeDtypeStruct((rows, ffc), BF16)],
        compiler_params=pltpu.CompilerParams(vmem_limit_bytes=48 * 1024 * 1024),
        cost_estimate=pl.CostEstimate(flops=2 * rows * width * 832, bytes_accessed=20 << 20, transcendentals=rows * 512),
    )(both, both, wj, ww, add, back)


def grads_kernel(xhat_ref, up_ref, mixed_ref, act_ref, wg_ref, out_ref):
    rows = xhat_ref.shape[0]
    n, m, k = xhat_ref.shape[1], mixed_ref.shape[1], act_ref.shape[1]
    hd = m // 4
    xhat = xhat_ref[...]
    up = up_ref[...].reshape(rows, n)
    mixed, act, wg = mixed_ref[...], act_ref[...], wg_ref[...]
    lane = lax.broadcasted_iota(jnp.int32, (n, m), 1)
    out_ref[0, 0:n, 0:m] = jnp.where(lane < 3 * hd, dot_tn(xhat, mixed), dot_tn(up, mixed)).astype(BF16)
    out_ref[0, 0:n, m:m + k] = dot_tn(xhat, wg).astype(BF16)
    out_ref[0, 0:n, m + k:] = dot_tn(up, act).astype(BF16)
    ones = jnp.ones((16, rows), BF16)
    out_ref[0, n:, 0:m] = dot_nn(ones, mixed).astype(BF16)
    out_ref[0, n:, m:m + k] = dot_nn(ones, wg).astype(BF16)
    out_ref[0, n:, m + k:m + k + n] = dot_nn(ones, up).astype(BF16)
    out_ref[0, n:, m + k + n:] = jnp.zeros((16, k - n), BF16)


def grads(xhat, both, mixed, act, wg):
    rows, width = xhat.shape
    n = width // N_FSDP
    total = mixed.shape[1] + act.shape[1] + wg.shape[1]
    whole = lambda a: pl.BlockSpec(a.shape, lambda i: (0, 0))
    return pl.pallas_call(
        grads_kernel,
        grid=(N_FSDP,),
        in_specs=[
            pl.BlockSpec((rows, n), lambda i: (0, i)),
            pl.BlockSpec((both.shape[0], 128, n), lambda i: (0, 1, i)),
            whole(mixed), whole(act), whole(wg)],
        out_specs=pl.BlockSpec((1, n + 16, total), lambda i: (i, 0, 0)),
        out_shape=jax.ShapeDtypeStruct((N_FSDP, n + 16, total), BF16),
        compiler_params=pltpu.CompilerParams(vmem_limit_bytes=48 * 1024 * 1024),
        cost_estimate=pl.CostEstimate(flops=2 * rows * width * 1024, bytes_accessed=14 << 20, transcendentals=0),
    )(xhat, both, mixed, act, wg)


def spread_kernel(core_ref, mixed_ref, wg_ref, act_ref, wj_ref, ww_ref, dense_ref, narrow_ref, mine_ref, other_ref):
    width = wj_ref.shape[0]
    half = mine_ref.shape[1]
    mixed = mixed_ref[...]
    u = (dot_nt(mixed, wj_ref[...]) + dot_nt(wg_ref[...], ww_ref[...])).astype(BF16)
    out = (dot_nn(mixed, dense_ref[...]) + dot_nn(act_ref[...], narrow_ref[...])).astype(BF16)

    def put(low_ref, high_ref):
        for ref, at in ((low_ref, 0), (high_ref, half)):
            ref[0, :, :width] = u[at:at + half]
            ref[0, :, width:] = out[at:at + half]

    @pl.when(core_ref[0] == 0)
    def _():
        put(mine_ref, other_ref)

    @pl.when(core_ref[0] != 0)
    def _():
        put(other_ref, mine_ref)


def spread(core, mixed, wg, act, wj, ww, dense, narrow):
    rows, width = mixed.shape[0], wj.shape[0]
    own = rows // N_CTX
    whole = lambda a: pl.BlockSpec(a.shape, lambda i: (0, 0))
    tall = lambda a: pl.BlockSpec((2 * own, a.shape[1]), lambda i: (i, 0))
    shape = jax.ShapeDtypeStruct((N_CTX // 2, own, 2 * width), BF16)
    return pl.pallas_call(
        spread_kernel,
        grid=(N_CTX // 2,),
        in_specs=[pl.BlockSpec(memory_space=pltpu.SMEM), tall(mixed), tall(wg), tall(act),
                  whole(wj), whole(ww), whole(dense), whole(narrow)],
        out_specs=[pl.BlockSpec((1, own, 2 * width), lambda i: (i, 0, 0))] * 2,
        out_shape=[shape, shape],
        compiler_params=pltpu.CompilerParams(vmem_limit_bytes=48 * 1024 * 1024),
        cost_estimate=pl.CostEstimate(flops=2 * rows * width * 1024, bytes_accessed=14 << 20, transcendentals=0),
    )(core, mixed, wg, act, wj, ww, dense, narrow)


def attention_kernel(order_ref, joint_ref, table_ref, grad_ref, out_ref,
                     joint_s, table_s, grad_s, k_s, v_s, qT_s, kT_s, vT_s, gT_s,
                     oT_s, dqT_s, dkT_s, dvT_s, cosT_s, sinT_s, out_s):
    rows, hd = joint_ref.shape[0], joint_ref.shape[1] // 4
    slots, half, tile = N_CTX, rows // (2 * N_CTX), 256
    last = 2 * slots - 1
    for j in range(slots):
        p = order_ref[j]
        for h in range(2):
            src = pl.ds(j * 2 * half + h * half, half)
            dst = pl.ds(pl.multiple_of((p if h == 0 else last - p) * half, half), half)
            joint_s[dst, :] = joint_ref[src, :]
            table_s[dst, :] = table_ref[src, :]
            grad_s[dst, :] = grad_ref[src, :]
    scale = hd ** -0.5

    def spin(t, c, s):
        return jnp.concatenate([t[0:8] * c - t[8:16] * s, t[8:16] * c + t[0:8] * s, t[16:]], axis=0)

    for i in range(rows // tile):
        at = pl.ds(i * tile, tile)
        jT = joint_s[at, :].T
        tT = table_s[at, :].T
        c, s = tT[0:8], tT[8:16]
        cosT_s[:, at] = c
        sinT_s[:, at] = s
        qT = spin(jT[0:hd], c, s).astype(BF16)
        kT = spin(jT[hd:2 * hd], c, s).astype(BF16)
        vT = jT[2 * hd:3 * hd].astype(BF16)
        qT_s[:, at] = (qT.astype(F32) * scale).astype(BF16)
        kT_s[:, at] = kT
        vT_s[:, at] = vT
        k_s[at, :] = kT.astype(F32).T.astype(BF16)
        v_s[at, :] = vT.astype(F32).T.astype(BF16)
        gT_s[:, at] = grad_s[at, :].T.astype(BF16)
    dkT_s[...] = jnp.zeros_like(dkT_s)
    dvT_s[...] = jnp.zeros_like(dvT_s)
    key_at = lax.broadcasted_iota(jnp.int32, (tile, tile), 0)
    query_at = lax.broadcasted_iota(jnp.int32, (tile, tile), 1)
    seen = key_at <= query_at
    dot = lambda a, b: jnp.dot(a, b, preferred_element_type=F32)
    dot_nt = lambda a, b: lax.dot_general(a, b, (((1,), (1,)), ((), ())), preferred_element_type=F32)
    for i in range(rows // tile):
        at = pl.ds(i * tile, tile)
        span = (i + 1) * tile
        upto = pl.ds(0, span)
        qT, gT = qT_s[:, at], gT_s[:, at]
        sT = dot(k_s[upto, :], qT)
        edge = jnp.where(seen, sT[i * tile:], NEGATIVE)
        sT = edge if i == 0 else jnp.concatenate([sT[:i * tile], edge], axis=0)
        largest = jnp.max(sT, axis=0, keepdims=True)
        e = jnp.exp(sT - largest)
        pT = e * (1.0 / jnp.sum(e, axis=0, keepdims=True))
        pT_low = pT.astype(BF16)
        dpT = dot(v_s[upto, :], gT)
        balance = jnp.sum(dpT * pT, axis=0, keepdims=True)
        dsT = (pT * (dpT - balance)).astype(BF16)
        oT_s[:, at] = dot(vT_s[:, upto], pT_low)
        dqT_s[:, at] = dot(kT_s[:, upto], dsT) * scale
        dkT_s[:, upto] += dot_nt(qT, dsT)
        dvT_s[:, upto] += dot_nt(gT, pT_low)
    for i in range(rows // tile):
        at = pl.ds(i * tile, tile)
        c, s = cosT_s[:, at], -sinT_s[:, at]
        full = jnp.concatenate(
            [spin(dqT_s[:, at], c, s), spin(dkT_s[:, at], c, s), dvT_s[:, at], oT_s[:, at]], axis=0)
        out_s[at, :] = full.T.astype(BF16)
    for j in range(slots):
        p = order_ref[j]
        for h in range(2):
            dst = pl.ds(j * 2 * half + h * half, half)
            src = pl.ds(pl.multiple_of((p if h == 0 else last - p) * half, half), half)
            out_ref[dst, :] = out_s[src, :]


def attention(order, joint, table, grad):
    rows, hd = joint.shape[0], joint.shape[1] // 4
    vmem = pl.BlockSpec(memory_space=pltpu.VMEM)
    return pl.pallas_call(
        attention_kernel,
        out_shape=jax.ShapeDtypeStruct((rows, 4 * hd), BF16),
        in_specs=[pl.BlockSpec(memory_space=pltpu.SMEM), vmem, vmem, vmem],
        out_specs=vmem,
        scratch_shapes=[
            pltpu.VMEM((rows, 4 * hd), F32),
            pltpu.VMEM((rows, 16), F32),
            pltpu.VMEM((rows, hd), F32),
            pltpu.VMEM((rows, hd), BF16),
            pltpu.VMEM((rows, hd), BF16),
            pltpu.VMEM((hd, rows), BF16),
            pltpu.VMEM((hd, rows), BF16),
            pltpu.VMEM((hd, rows), BF16),
            pltpu.VMEM((hd, rows), BF16),
            pltpu.VMEM((hd, rows), F32),
            pltpu.VMEM((hd, rows), F32),
            pltpu.VMEM((hd, rows), F32),
            pltpu.VMEM((hd, rows), F32),
            pltpu.VMEM((8, rows), F32),
            pltpu.VMEM((8, rows), F32),
            pltpu.VMEM((rows, 4 * hd), BF16),
        ],
        compiler_params=pltpu.CompilerParams(vmem_limit_bytes=48 * 1024 * 1024),
        cost_estimate=pl.CostEstimate(flops=7 * rows * rows * hd, bytes_accessed=8 << 20, transcendentals=rows * rows // 2),
    )(order, joint, table, grad)


def shards(
    tokens, upstream, block_pairs, rotary_place,
    first_gain, first_shift, joint_weight, joint_bias, dense_weight, dense_bias,
    second_gain, second_shift, widen_weight, widen_bias, narrow_weight, narrow_bias,
):
    own_rows, width = tokens.shape[1], tokens.shape[2]
    hd = width // HEADS
    ff = widen_weight.shape[1]
    ffc = ff // N_CTX
    rows = own_rows * N_CTX
    c = lax.axis_index("ctx")
    f = lax.axis_index("fsdp")
    own_tokens, own_up = tokens[0], upstream[0]
    d_own = width // N_FSDP

    place = rotary_place[0]
    extra = jnp.concatenate([place // 64, place % 64]).astype(BF16)
    extra = jnp.pad(extra[None, :], ((0, 15), (0, width - 2 * own_rows)))
    both = lax.all_gather(jnp.concatenate([own_tokens, own_up, extra], axis=0), "ctx", axis=0)

    joint_part = lax.dynamic_index_in_dim(joint_weight.reshape(d_own, 3, HEADS, hd), c, 2, keepdims=False)
    vectors = jnp.concatenate(
        [v[:, None] for v in (first_gain, first_shift, second_gain, second_shift, dense_bias, narrow_bias)]
        + [joint_bias.reshape(d_own, 3), widen_bias.reshape(d_own, 4), jnp.zeros((d_own, 51), BF16)], axis=1)
    widen_part = lax.dynamic_slice_in_dim(widen_weight, c * ffc, ffc, axis=1)
    part = jnp.concatenate([joint_part.reshape(d_own, 3 * hd), vectors, widen_part], axis=1)
    slices = lax.all_to_all(jnp.broadcast_to(part[None], (N_FSDP,) + part.shape), "fsdp", 0, 0, tiled=True)
    slices = slices.reshape(width, part.shape[1])
    odd = c % 2
    back_w = turn(jnp.concatenate([
        lax.dynamic_slice_in_dim(dense_weight, odd * hd, hd, axis=0),
        lax.dynamic_slice_in_dim(narrow_weight, odd * ffc, ffc, axis=0)], axis=0))
    dense_w, narrow_w = back_w[:hd], back_w[hd:]

    coded = both[:, 2 * own_rows, :2 * own_rows].astype(F32)
    place_all = (coded[:, :own_rows] * 64.0 + coded[:, own_rows:]).reshape(rows)
    steps = jnp.arange(8, dtype=F32)
    angles = place_all[:, None] * (ROTARY_BASE ** (-2.0 * steps / 16))
    table = jnp.concatenate([jnp.cos(angles), jnp.sin(angles)], axis=1)
    order = block_pairs[0]

    wj = slices[:, :4 * hd].astype(F32)
    ww = slices[:, 4 * hd:].astype(F32)
    vec = slices[:, 3 * hd:4 * hd].astype(F32)
    g1, s1, g2, s2 = vec[:, 0:1], vec[:, 1:2], vec[:, 2:3], vec[:, 3:4]
    dense_b, narrow_b = vec[:, 4], vec[:, 5]
    jb_full = vec[:, 6:9].reshape(3, HEADS, hd)
    wb_full = vec[:, 9:13].reshape(ff)
    jb_own = lax.dynamic_index_in_dim(jb_full, c, 1, keepdims=False).reshape(3 * hd)
    wb_own = lax.dynamic_slice_in_dim(wb_full, c * ffc, ffc)
    wj = jnp.where(jnp.arange(4 * hd)[None, :] < 3 * hd, wj, 0.0)
    wj_g = (g1 * wj).astype(BF16)
    ww_g = (g2 * ww).astype(BF16)
    shifted = jnp.concatenate([
        jnp.sum(s1 * wj, axis=0) + jnp.pad(jb_own, (0, hd)), jnp.sum(s2 * ww, axis=0) + wb_own])[None, :]
    dense_p = jnp.pad(dense_w, ((3 * hd, 0), (0, 0)))

    xhat, joint, att_grad, act, wg = project(both, wj_g, ww_g, shifted, back_w)

    mixed = attention(order, joint, table, att_grad)

    mine, other = spread((c % 2)[None], mixed, wg, act, wj_g, ww_g, dense_p, narrow_w)
    chip = (mine.astype(F32) + lax.ppermute(other, "ctx", OTHER_CORE).astype(F32)).astype(BF16)
    summed = lax.all_to_all(chip, "ctx", 0, 0, tiled=True, axis_index_groups=SAME_CORE)
    summed = jnp.sum(summed.astype(F32), axis=0)
    u_own, out_own = summed[:, :width], summed[:, width:]

    parts = lax.all_to_all(grads(xhat, both, mixed, act, wg), "fsdp", 0, 0, tiled=True)
    parts = jnp.sum(parts.astype(F32), axis=0)
    bias_grad = parts[d_own, 4 * hd + ffc:4 * hd + ffc + d_own]
    low = parts.astype(BF16)
    turned = turn(jnp.concatenate([low[:, 3 * hd:4 * hd], low[:, 4 * hd + ffc:]], axis=1))
    grads_all = lax.all_gather(jnp.concatenate([
        low[:, :3 * hd], turned[:, :hd], low[:, 4 * hd:4 * hd + ffc], turned[:, hd:]], axis=1), "ctx", axis=0)

    own_x = own_tokens.astype(F32)
    block_out = (own_x + out_own + dense_b + narrow_b).astype(BF16)
    own_center = own_x - jnp.mean(own_x, axis=-1, keepdims=True)
    own_rstd = lax.rsqrt(jnp.mean(own_center * own_center, axis=-1, keepdims=True) + EPSILON)
    own_xhat = own_center * own_rstd
    tokens_grad = own_up.astype(F32) + own_rstd * (
        u_own - jnp.mean(u_own, axis=-1, keepdims=True)
        - own_xhat * jnp.mean(u_own * own_xhat, axis=-1, keepdims=True))

    late_all = grads_all[:, :, :4 * hd].astype(F32)
    early_all = grads_all[:, :, 4 * hd:].astype(F32)
    m_w = jnp.transpose(early_all[:, :d_own, :ffc], (1, 0, 2)).reshape(d_own, ff)
    wb_grad = early_all[:, d_own, :ffc].reshape(ff)
    widen_grad = second_gain.astype(F32)[:, None] * m_w + second_shift.astype(F32)[:, None] * wb_grad[None, :]
    widen_f = widen_weight.astype(F32)
    g2_grad = jnp.sum(widen_f * m_w, axis=1)
    s2_grad = jnp.sum(widen_f * wb_grad[None, :], axis=1)
    narrow_grad = jnp.transpose(
        early_all[:, :d_own, ffc:].reshape(N_FSDP, 2, d_own, ffc), (1, 3, 0, 2)).reshape(2 * ffc, width)
    m_j = jnp.transpose(late_all[:, :d_own, :3 * hd].reshape(N_CTX, d_own, 3, hd), (1, 2, 0, 3)).reshape(d_own, 3 * width)
    jb_grad = jnp.transpose(late_all[:, d_own, :3 * hd].reshape(N_CTX, 3, hd), (1, 0, 2)).reshape(3 * width)
    joint_grad = first_gain.astype(F32)[:, None] * m_j + first_shift.astype(F32)[:, None] * jb_grad[None, :]
    joint_f = joint_weight.astype(F32)
    g1_grad = jnp.sum(joint_f * m_j, axis=1)
    s1_grad = jnp.sum(joint_f * jb_grad[None, :], axis=1)
    dense_grad = jnp.transpose(
        late_all[:, :d_own, 3 * hd:].reshape(N_FSDP, 2, d_own, hd), (1, 3, 0, 2)).reshape(2 * hd, width)
    jb_shard = lax.dynamic_slice_in_dim(jb_grad, f * (3 * d_own), 3 * d_own)
    wb_shard = lax.dynamic_slice_in_dim(wb_grad, f * (ff // N_FSDP), ff // N_FSDP)
    return (
        block_out[None], tokens_grad[None], g1_grad, s1_grad, joint_grad, jb_shard,
        dense_grad, bias_grad, g2_grad, s2_grad, widen_grad, wb_shard, narrow_grad, bias_grad,
    )


def solution(mesh):
    rows = P("fsdp", "ctx", None)
    vec, mat = P("fsdp"), P("fsdp", None)
    in_specs = (rows, rows, mat, P("fsdp", "ctx"), vec, vec, mat, vec, mat, vec, vec, vec, mat, vec, mat, vec)
    out_specs = (rows, rows, vec, vec, mat, vec, mat, vec, vec, vec, mat, vec, mat, vec)
    return jax.shard_map(shards, mesh=mesh, in_specs=in_specs, out_specs=out_specs, check_vma=False)
```

profile of v0, /device:TPU:22, one launch (start us, length us, event | category | flops | bytes accessed | tf_op | source)
XLA Modules:
  0.0 317.6 jit_solution(16985327522641115801)
XLA Ops:
  7.3 0.8 fusion.30
  8.1 1.9 pad_maximum_fusion.1
  10.0 0.4 copy.88
  10.6 0.1 copy.90
  10.7 0.1 copy.91
  10.8 0.1 copy.92
  11.0 0.1 copy.93
  11.3 0.1 copy.95
  11.4 0.2 reshape.143
  11.8 0.9 constant_dynamic-slice_fusion.2
  12.6 0.2 concatenate.34
  12.8 1.1 broadcast_in_dim.70
  13.9 7.2 %all-to-all-start = ((bf16[8,128,512]{2,1,0:T(8,128)(2,1)}), bf16[8,128,512]{2,1,0:T(8,128)(2,1)S(1)}, u32[]{:S(2)}, u32[]{:S(2)}) async-start(bf16[8,128,512]{2,1,0:T(8,128)(2,1)} %broadcast_in_dim.70), calls=%async_computation | async-start | bytes 2097152 | tf_op jit(solution)/shard_map/all_to_all | solution.py:289
  21.2 4.7 %collective-permute-start = (bf16[320,1024]{1,0:T(8,128)(2,1)S(1)}, bf16[320,1024]{1,0:T(8,128)(2,1)S(1)}, u32[]{:S(2)}, u32[]{:S(2)}) collective-permute-start(bf16[320,1024]{1,0:T(8,128)(2,1)S(1)} %pad_maximum_fusion), channel_id=1, source_target_pairs={{0,0},{1,16},{2,32},{3,48},{4,64},{5,80},{6,96},{7,112},{8,8},{9,2... | collective-permute-start | bytes 1966088 | tf_op jit(solution)/shard_map/ppermute | solution.py:23
  25.9 39.3 %collective-permute-done.back_ref = bf16[320,1024]{1,0:T(8,128)(2,1)S(1)} collective-permute-done((bf16[320,1024]{1,0:T(8,128)(2,1)S(1)}, bf16[320,1024]{1,0:T(8,128)(2,1)S(1)}, u32[]{:S(2)}, u32[]{:S(2)}) %collective-permute-start) | collective-permute-done | bytes 655392 | tf_op jit(solution)/shard_map/ppermute | solution.py:23
  65.3 0.8 slice.145.narrow_ref
  66.3 1.0 slice.138
  67.3 0.2 slice.140
  67.5 1.4 reshape.146
  69.0 0.3 reshape.148
  69.2 1.6 slice_reduce_fusion.1
  70.8 0.9 multiply_reduce_fusion
  71.8 30.1 %all-gather.5.cloned.1.call-done = bf16[4352,1024]{1,0:T(8,128)(2,1)} async-done(((bf16[272,1024]{1,0:T(8,128)(2,1)}), bf16[4352,1024]{1,0:T(8,128)(2,1)}) %all-gather.5.cloned.1.call-update) | async-done | bytes 8912912 | tf_op jit(solution)/shard_map/all_gather | solution.py:281
  101.9 0.8 slice_convert_fusion.3
  102.8 0.3 multiply_cosine_fusion
  103.1 0.3 copy.96.table_ref
  103.4 10.4 %shard_map.263 = (bf16[2048,1024]{1,0:T(8,128)(2,1)}, f32[2048,256]{1,0:T(8,128)}, f32[2048,64]{1,0:T(8,128)S(1)}, bf16[2048,256]{1,0:T(8,128)(2,1)S(1)}, bf16[2048,256]{1,0:T(8,128)(2,1)S(1)}) custom-call(bf16[16,272,1024]{2,1,0:T(8,128)(2,1)} %bitcast.69, bf16[16,272,1024]{2,1,0:T(8,128)(2,1)} %bitcast.70, ...), custom_call_target="tpu_custom_call" | custom-call | flops 3489660928 | bytes 20971520 | tf_op jit(solution)/shard_map/pallas_call | solution.py:64
  113.8 1.6 copy-done.3
  115.4 12.5 %shard_map.264.mixed_ref = bf16[2048,256]{1,0:T(8,128)(2,1)S(1)} custom-call(s32[16]{0:T(128)S(1)} %bitcast.67, f32[2048,256]{1,0:T(8,128)S(1)} %copy-done.3, f32[2048,16]{1,0:T(8,128)S(1)} %copy.96.table_ref, f32[2048,64]{1,0:T(8,128)S(1)} %get-tuple-element.22.grad_ref), custom_call_target="tpu_custom_call" | custom-call | flops 1879048192 | bytes 8388608 | tf_op jit(solution)/shard_map/pallas_call | solution.py:235
  128.0 8.1 %shard_map.265 = (bf16[8,128,2048]{2,1,0:T(8,128)(2,1)}, bf16[8,128,2048]{2,1,0:T(8,128)(2,1)}) custom-call(s32[1]{0:T(128)} %bitcast.1.core_ref, bf16[2048,256]{1,0:T(8,128)(2,1)S(1)} %shard_map.264.mixed_ref, bf16[2048,256]{1,0:T(8,128)(2,1)S(1)} %get-tuple-element.23.wg_ref, bf16[2048,256]{1,0:T(8,128)(2,1)S(1)} %get-tuple-element.24.act_ref, ...), custom_call_target="tpu_custom_call" | custom-call | flops 4294967296 | bytes 14680064 | tf_op jit(solution)/shard_map/pallas_call | solution.py:145
  136.1 0.2 collective-permute-start.1
  136.3 10.4 %shard_map.266 = bf16[8,144,768]{2,1,0:T(8,128)(2,1)S(1)} custom-call(bf16[2048,1024]{1,0:T(8,128)(2,1)} %get-tuple-element.27.xhat_ref, bf16[16,272,1024]{2,1,0:T(8,128)(2,1)} %bitcast.71, bf16[2048,256]{1,0:T(8,128)(2,1)S(1)} %shard_map.264.mixed_ref, bf16[2048,256]{1,0:T(8,128)(2,1)S(1)} %get-tuple-element.24.act_ref, ...), custom_call_target="tpu_custom_call" | custom-call | flops 4294967296 | bytes 14680064 | tf_op jit(solution)/shard_map/pallas_call | solution.py:104
  146.7 30.2 %all_to_all.15 = bf16[8,144,768]{2,1,0:T(8,128)(2,1)S(1)} all-to-all(bf16[8,144,768]{2,1,0:T(8,128)(2,1)S(1)} %shard_map.266), channel_id=1, replica_groups=mesh['ctx'=16,'fsdp'=8] {'fsdp'}, dimensions={0} | all-to-all | bytes 3538944 | tf_op jit(solution)/shard_map/all_to_all | solution.py:330
  177.0 0.2 convert_reduce_fusion.1
  177.5 9.4 %collective-permute-start.2 = (bf16[144,320]{1,0:T(8,128)(2,1)S(1)}, bf16[144,320]{1,0:T(8,128)(2,1)S(1)}, u32[]{:S(2)}, u32[]{:S(2)}) collective-permute-start(bf16[144,320]{1,0:T(8,128)(2,1)S(1)} %pad_maximum_fusion.4), channel_id=1, source_target_pairs={{0,0},{1,16},{2,32},{3,48},{4,64},{5,80},{6,96},{7,112},{8,8},{9,2... | collective-permute-start | bytes 276488 | tf_op jit(solution)/shard_map/ppermute | solution.py:23
  186.9 4.5 %collective-permute-done.2 = bf16[144,320]{1,0:T(8,128)(2,1)S(1)} collective-permute-done((bf16[144,320]{1,0:T(8,128)(2,1)S(1)}, bf16[144,320]{1,0:T(8,128)(2,1)S(1)}, u32[]{:S(2)}, u32[]{:S(2)}) %collective-permute-start.2) | collective-permute-done | bytes 92192 | tf_op jit(solution)/shard_map/ppermute | solution.py:23
  191.5 0.8 pad_maximum_fusion.2
  192.3 7.7 %add_convert_fusion = bf16[8,128,2048]{2,1,0:T(8,128)(2,1)} fusion(bf16[8,128,2048]{2,1,0:T(8,128)(2,1)} %collective-permute-done.1, bf16[8,128,2048]{2,1,0:T(8,128)(2,1)} %get-tuple-element.25), kind=kLoop, calls=%fused_computation.1 | loop fusion | flops 8388608 | bytes 12582912 | tf_op jit(solution)/shard_map/convert_element_type | solution.py:325
  200.0 4.7 %all-to-all-start.1 = ((bf16[8,128,2048]{2,1,0:T(8,128)(2,1)}), bf16[8,128,2048]{2,1,0:T(8,128)(2,1)}, u32[]{:S(2)}, u32[]{:S(2)}) async-start(bf16[8,128,2048]{2,1,0:T(8,128)(2,1)} %add_convert_fusion), calls=%async_computation.1 | async-start | bytes 8388608 | tf_op jit(solution)/shard_map/all_to_all | solution.py:326
  204.7 1.3 copy.103
  206.2 0.2 fusion.17
  206.5 65.9 %all-to-all-done.1 = bf16[8,128,2048]{2,1,0:T(8,128)(2,1)} async-done(((bf16[8,128,2048]{2,1,0:T(8,128)(2,1)}), bf16[8,128,2048]{2,1,0:T(8,128)(2,1)}, u32[]{:S(2)}, u32[]{:S(2)}) %all-to-all-start.1) | async-done | bytes 4194336 | tf_op jit(solution)/shard_map/all_to_all | solution.py:326
  272.4 3.0 convert_reduce_fusion
  275.4 0.2 slice_reduce_fusion.6
  275.7 1.1 fusion.16
  276.7 2.3 slice_convert_fusion
  279.1 2.6 fusion.31
  281.7 1.5 slice_convert_fusion.1
  283.2 1.5 slice.157
  284.7 1.3 slice.159
  286.1 2.0 copy.104
  288.1 2.4 fusion.1
  290.5 3.0 copy.107
  293.5 1.8 copy.105
  295.3 3.5 %copy.115 = f32[64,8,8,128]{3,1,2,0:T(8,128)} copy(f32[64,8,8,128]{3,2,1,0:T(8,128)} %bitcast.72) | data formatting | bytes 4194304
  298.9 1.7 copy.98
  300.6 1.6 copy.99
  302.3 2.2 fusion.4
  304.5 3.2 copy.106
  307.7 0.7 dynamic_slice.33
  308.4 0.3 copy.102
  308.7 0.9 copy.116
  309.6 0.7 dynamic_slice.32
  310.3 0.5 copy.119
  (99 shorter events, 1.8 us)
Async XLA Ops:
  7.2 13.9 %copy-start = (bf16[512,1024]{1,0:T(8,128)(2,1)S(1)}, bf16[512,1024]{1,0:T(8,128)(2,1)}, u32[]{:S(2)}) copy-start(bf16[512,1024]{1,0:T(8,128)(2,1)} %param.30) | copy-start | bytes 3145732
  7.2 2.8 copy-start.14
  7.2 3.3 %copy-start.22 = (bf16[128]{0:T(256)(128)(2,1)S(1)}, bf16[128]{0:T(256)(128)(2,1)}, u32[]{:S(2)}) copy-start(bf16[128]{0:T(256)(128)(2,1)} %param.20) | copy-start | bytes 772
  7.2 3.5 %copy-start.23 = (bf16[128]{0:T(256)(128)(2,1)S(1)}, bf16[128]{0:T(256)(128)(2,1)}, u32[]{:S(2)}) copy-start(bf16[128]{0:T(256)(128)(2,1)} %param.21) | copy-start | bytes 772
  7.2 3.6 %copy-start.20 = (bf16[128]{0:T(256)(128)(2,1)S(1)}, bf16[128]{0:T(256)(128)(2,1)}, u32[]{:S(2)}) copy-start(bf16[128]{0:T(256)(128)(2,1)} %param.26) | copy-start | bytes 772
  7.2 3.7 %copy-start.21 = (bf16[128]{0:T(256)(128)(2,1)S(1)}, bf16[128]{0:T(256)(128)(2,1)}, u32[]{:S(2)}) copy-start(bf16[128]{0:T(256)(128)(2,1)} %param.27) | copy-start | bytes 772
  7.3 3.9 %copy-start.18 = (bf16[128]{0:T(256)(128)(2,1)S(1)}, bf16[128]{0:T(256)(128)(2,1)}, u32[]{:S(2)}) copy-start(bf16[128]{0:T(256)(128)(2,1)} %param.25) | copy-start | bytes 772
  7.3 4.0 %copy-start.19 = (bf16[128]{0:T(256)(128)(2,1)S(1)}, bf16[128]{0:T(256)(128)(2,1)}, u32[]{:S(2)}) copy-start(bf16[128]{0:T(256)(128)(2,1)} %param.31) | copy-start | bytes 772
  7.3 4.1 %copy-start.16 = (bf16[384]{0:T(512)(128)(2,1)S(1)}, bf16[384]{0:T(512)(128)(2,1)}, u32[]{:S(2)}) copy-start(bf16[384]{0:T(512)(128)(2,1)} %param.23) | copy-start | bytes 2308
  7.3 4.4 %copy-start.17 = (bf16[512]{0:T(512)(128)(2,1)S(1)}, bf16[512]{0:T(512)(128)(2,1)}, u32[]{:S(2)}) copy-start(bf16[512]{0:T(512)(128)(2,1)} %param.29) | copy-start | bytes 3076
  7.3 94.6 %all-gather.5.cloned.1.call-start = ((), (), s32[]{:S(2)}) async-start(), calls=%async_computation.3 | async-start | bytes 9469952 | tf_op jit(solution)/shard_map/all_gather | solution.py:281
  10.4 3.5 %copy-start.10 = (bf16[128,3072]{0,1:T(8,128)(2,1)}, bf16[128,3072]{0,1:T(8,128)(2,1)S(1)}, u32[]{:S(2)}) copy-start(bf16[128,3072]{0,1:T(8,128)(2,1)S(1)} %copy.88) | copy-start | bytes 2359300
  11.0 10.1 %copy-start.15 = (bf16[128,1024]{1,0:T(8,128)(2,1)S(1)}, bf16[128,1024]{1,0:T(8,128)(2,1)}, u32[]{:S(2)}) copy-start(bf16[128,1024]{1,0:T(8,128)(2,1)} %param.24) | copy-start | bytes 786436
  13.9 52.3 %all-to-all-start = ((bf16[8,128,512]{2,1,0:T(8,128)(2,1)}), bf16[8,128,512]{2,1,0:T(8,128)(2,1)S(1)}, u32[]{:S(2)}, u32[]{:S(2)}) async-start(bf16[8,128,512]{2,1,0:T(8,128)(2,1)} %broadcast_in_dim.70), calls=%async_computation | async-start | bytes 2097152 | tf_op jit(solution)/shard_map/all_to_all | solution.py:289
  21.1 255.7 %all-gather.7.cloned.1.call-start = ((), (), s32[]{:S(2)}) async-start(), calls=%async_computation.4 | async-start | bytes 3760128 | tf_op jit(solution)/shard_map/all_gather | solution.py:335
  21.2 44.0 %collective-permute-start = (bf16[320,1024]{1,0:T(8,128)(2,1)S(1)}, bf16[320,1024]{1,0:T(8,128)(2,1)S(1)}, u32[]{:S(2)}, u32[]{:S(2)}) collective-permute-start(bf16[320,1024]{1,0:T(8,128)(2,1)S(1)} %pad_maximum_fusion), channel_id=1, source_target_pairs={{0,0},{1,16},{2,32},{3,48},{4,64},{5,80},{6,96},{7,112},{8,8},{9,2... | collective-permute-start | bytes 1966088 | tf_op jit(solution)/shard_map/ppermute | solution.py:23
  103.4 10.4 %copy-start.4 = (s32[1,16]{1,0:T(1,128)S(1)}, s32[1,16]{1,0:T(1,128)}, u32[]{:S(2)}) copy-start(s32[1,16]{1,0:T(1,128)} %param.18) | copy-start | bytes 196
  113.8 1.6 copy-start.3
  115.4 12.5 %copy-start.2 = (bf16[256,1024]{1,0:T(8,128)(2,1)S(1)}, bf16[256,1024]{1,0:T(8,128)(2,1)}, u32[]{:S(2)}) copy-start(bf16[256,1024]{1,0:T(8,128)(2,1)} %slice.145.narrow_ref) | copy-start | bytes 1572868
  136.1 56.2 %collective-permute-start.1 = (bf16[8,128,2048]{2,1,0:T(8,128)(2,1)}, bf16[8,128,2048]{2,1,0:T(8,128)(2,1)}, u32[]{:S(2)}, u32[]{:S(2)}) collective-permute-start(bf16[8,128,2048]{2,1,0:T(8,128)(2,1)} %get-tuple-element.26), channel_id=1, source_target_pairs={{8,0},{0,8},{24,16},{16,24},{40,32},{32,40},{56,48},{48,56},{72,64... | collective-permute-start | bytes 12582920 | tf_op jit(solution)/shard_map/ppermute | solution.py:325
  177.5 13.9 %collective-permute-start.2 = (bf16[144,320]{1,0:T(8,128)(2,1)S(1)}, bf16[144,320]{1,0:T(8,128)(2,1)S(1)}, u32[]{:S(2)}, u32[]{:S(2)}) collective-permute-start(bf16[144,320]{1,0:T(8,128)(2,1)S(1)} %pad_maximum_fusion.4), channel_id=1, source_target_pairs={{0,0},{1,16},{2,32},{3,48},{4,64},{5,80},{6,96},{7,112},{8,8},{9,2... | collective-permute-start | bytes 276488 | tf_op jit(solution)/shard_map/ppermute | solution.py:23
  200.0 4.7 %copy-start.12 = (bf16[128,4096]{1,0:T(8,128)(2,1)S(1)}, bf16[128,4096]{1,0:T(8,128)(2,1)}, u32[]{:S(2)}) copy-start(bf16[128,4096]{1,0:T(8,128)(2,1)} %param.28) | copy-start | bytes 3145732
  200.0 72.4 %all-to-all-start.1 = ((bf16[8,128,2048]{2,1,0:T(8,128)(2,1)}), bf16[8,128,2048]{2,1,0:T(8,128)(2,1)}, u32[]{:S(2)}, u32[]{:S(2)}) async-start(bf16[8,128,2048]{2,1,0:T(8,128)(2,1)} %add_convert_fusion), calls=%async_computation.1 | async-start | bytes 8388608 | tf_op jit(solution)/shard_map/all_to_all | solution.py:326
  204.7 1.4 copy-start.7
  206.4 103.8 %copy-start.24 = (f32[128]{0:T(128)}, f32[128]{0:T(128)S(1)}, u32[]{:S(2)}) copy-start(f32[128]{0:T(128)S(1)} %slice_bitcast_fusion.1) | copy-start | bytes 1540
  206.5 69.2 %copy-start.13 = (bf16[1,128,1024]{2,1,0:T(8,128)(2,1)S(1)}, bf16[1,128,1024]{2,1,0:T(8,128)(2,1)}, u32[]{:S(2)}) copy-start(bf16[1,128,1024]{2,1,0:T(8,128)(2,1)} %param.17) | copy-start | bytes 786436
  286.0 2.0 copy-start.8
  290.5 3.0 copy-start.6
  295.3 3.5 %copy-start.5 = (f32[16,128,192]{2,1,0:T(8,128)S(1)}, f32[16,128,192]{2,1,0:T(8,128)}, u32[]{:S(2)}) copy-start(f32[16,128,192]{2,1,0:T(8,128)} %slice.157) | copy-start | bytes 4718596
  300.6 1.8 copy-start.11
  304.5 3.8 %copy-start.9 = (f32[16,128,64]{2,1,0:T(8,128)S(1)}, f32[16,128,64]{2,1,0:T(8,128)}, u32[]{:S(2)}) copy-start(f32[16,128,64]{2,1,0:T(8,128)} %slice.159) | copy-start | bytes 1572868
  304.5 6.2 %copy-start.1 = (bf16[512,1024]{1,0:T(8,128)(2,1)S(1)}, bf16[512,1024]{1,0:T(8,128)(2,1)}, u32[]{:S(2)}) copy-start(bf16[512,1024]{1,0:T(8,128)(2,1)} %param.30) | copy-start | bytes 3145732
Sparse Core Ops, SparseCore 0:
  10.4 91.4 all-gather.4
  192.4 78.4 all-gather.6
where the time goes:
time: 322 us; the launch traced here: 318 us
  waiting for transfers between devices  140 us (43%)
  Pallas kernels  41.4 us (13%)
  local copies, waits for them, and re-layouts  38.3 us (12%)
  blocking collectives  30.2 us (9%)
  other arithmetic  26.9 us (8%)
  starting transfers between devices  26.2 us (8%)
  between operations  14.6 us (5%)
    all_to_all x1, waiting for transfers between devices, shards(): lax.all_to_all(chip, 'ctx', 0, 0, tiled=True, axis_index_groups=SAME_CORE)  65.9 us
    ppermute x2, waiting for transfers between devices, turn(): return lax.ppermute(v, ('ctx', 'fsdp'), TURN)  43.8 us
    all_to_all x1, blocking collectives, shards(): lax.all_to_all(grads(xhat, both, mixed, act, wg), 'fsdp', 0, 0, tiled=True)  30.2 us
    all_gather x1, waiting for transfers between devices, shards(): lax.all_gather(jnp.concatenate([own_tokens, own_up, extra], axis=0), 'ctx...  30.1 us
    unnamed x58, local copies, waits for them, and re-layouts  14.5 us
    ppermute x2, starting transfers between devices, turn(): return lax.ppermute(v, ('ctx', 'fsdp'), TURN)  14.1 us
    pallas_call x1, Pallas kernels, attention(): pl.pallas_call(attention_kernel, out_shape=jax.ShapeDtypeStruct((rows, 4...  12.5 us
    pallas_call x1, Pallas kernels, grads(): pl.pallas_call(grads_kernel, grid=(N_FSDP,), in_specs=[pl.BlockSpec((rows...  10.4 us
  transfers between devices with their start and end apart: 7, of which 4 were waited for; matrix products, arithmetic and copies ran while one was open for 8% of the time, Pallas kernels for 3%

commit v1 on v0

v1 whole, which is shorter than its diff:
```python
import jax
import jax.numpy as jnp
from jax import lax
from jax.experimental import pallas as pl
from jax.experimental.pallas import tpu as pltpu
from jax.sharding import PartitionSpec as P

HEADS = 16
EPSILON = 1e-05
NEGATIVE = -1e30
ROTARY_BASE = 10000.0
N_CTX = 16
VMEM = 60 * 1024 * 1024
N_FSDP = 8
F32 = jnp.float32
BF16 = jnp.bfloat16

OTHER_CORE = [(i ^ 1, i) for i in range(16)]
SAME_CORE = [list(range(0, 16, 2)), list(range(1, 16, 2))]
TURN = [(c * 8 + f, (2 * f + (c & 1)) * 8 + (c >> 1)) for c in range(16) for f in range(8)]


def tie(*arrays):
    return lax.optimization_barrier(arrays)


def turn(v):
    return lax.ppermute(v, ("ctx", "fsdp"), TURN)


def gather_chips(own):
    mine = lax.all_to_all(jnp.broadcast_to(own[None], (N_CTX // 2,) + own.shape), "ctx", 0, 0, tiled=True,
                          axis_index_groups=SAME_CORE)
    return mine, lax.ppermute(mine, "ctx", OTHER_CORE)


def dot_tn(a, b):
    return lax.dot_general(a, b, (((0,), (0,)), ((), ())), preferred_element_type=F32)


def dot_nt(a, b):
    return lax.dot_general(a, b, (((1,), (1,)), ((), ())), preferred_element_type=F32)


def dot_nn(a, b):
    return jnp.dot(a, b, preferred_element_type=F32)


def project_kernel(x_ref, up_ref, wj_ref, ww_ref, add_ref, back_ref,
                   xhat_ref, joint_ref, grad_ref, act_ref, wg_ref, early_ref, widen_s, narrow_s, wg_sum_s, up_sum_s):
    block, width = x_ref.shape[0] * x_ref.shape[1], x_ref.shape[2]
    i = pl.program_id(0)

    @pl.when(i == 0)
    def _():
        for ref in (widen_s, narrow_s, wg_sum_s, up_sum_s):
            ref[...] = jnp.zeros_like(ref)

    x = x_ref[...].reshape(block, width).astype(F32)
    center = x - jnp.mean(x, axis=-1, keepdims=True)
    xhat = (center * lax.rsqrt(jnp.mean(center * center, axis=-1, keepdims=True) + EPSILON)).astype(BF16)
    xhat_ref[...] = xhat
    wide = wj_ref.shape[1]
    joint_ref[...] = dot_nn(xhat, wj_ref[...]) + add_ref[0:1, :wide]
    widened = dot_nn(xhat, ww_ref[...]) + add_ref[0:1, wide:]
    phi = 0.5 * (1.0 + lax.erf(widened * (0.5 ** 0.5)))
    act = (widened * phi).astype(BF16)
    act_ref[...] = act
    slope = phi + widened * jnp.exp(-0.5 * widened * widened) * 0.3989422804014327
    up = up_ref[...].reshape(block, width)
    k = ww_ref.shape[1]
    hd = back_ref.shape[0] - k
    grad_ref[...] = dot_nt(up, back_ref[0:hd, :])
    wg = (dot_nt(up, back_ref[hd:, :]) * slope).astype(BF16)
    wg_ref[...] = wg
    widen_s[...] += dot_nn(wg.T, xhat)
    narrow_s[...] += dot_nn(act.T, up)
    ones = jnp.ones((16, block), BF16)
    wg_sum_s[...] += dot_nn(ones, wg)
    up_sum_s[...] += dot_nn(ones, up)

    @pl.when(i == pl.num_programs(0) - 1)
    def _():
        n = early_ref.shape[1] - 16
        per = k // N_FSDP
        for f in range(N_FSDP):
            early_ref[f, 0:n, 0:k] = widen_s[:, f * n:(f + 1) * n].T.astype(BF16)
            for q in range(width // k):
                early_ref[f, q * per:(q + 1) * per, k:] = (
                    narrow_s[f * per:(f + 1) * per, q * k:(q + 1) * k].astype(BF16))
            early_ref[f, n:, 0:k] = wg_sum_s[...].astype(BF16)
            early_ref[f, n:, k:k + n] = up_sum_s[:, f * n:(f + 1) * n].astype(BF16)
            early_ref[f, n:, k + n:] = jnp.zeros((16, k - n), BF16)


def project(both, wj, ww, add, back):
    slots, _, width = both.shape
    own, per = 128, 4
    rows, block = slots * own, per * own
    n = width // N_FSDP
    wide, ffc = wj.shape[1], ww.shape[1]
    hd = back.shape[0] - ffc
    whole = lambda a: pl.BlockSpec(a.shape, lambda i: (0, 0))
    tall = lambda n: pl.BlockSpec((block, n), lambda i: (i, 0))
    payload = (N_FSDP, n + 16, 2 * ffc)
    return pl.pallas_call(
        project_kernel,
        grid=(slots // per,),
        in_specs=[
            pl.BlockSpec((per, own, width), lambda i: (i, 0, 0)),
            pl.BlockSpec((per, own, width), lambda i: (i, 1, 0)),
            whole(wj), whole(ww), whole(add), whole(back)],
        out_specs=[tall(width), tall(wide), tall(hd), tall(ffc), tall(ffc),
                   pl.BlockSpec(payload, lambda i: (0, 0, 0))],
        out_shape=[
            jax.ShapeDtypeStruct((rows, width), BF16), jax.ShapeDtypeStruct((rows, wide), F32),
            jax.ShapeDtypeStruct((rows, hd), F32), jax.ShapeDtypeStruct((rows, ffc), BF16),
            jax.ShapeDtypeStruct((rows, ffc), BF16), jax.ShapeDtypeStruct(payload, BF16)],
        scratch_shapes=[pltpu.VMEM((ffc, width), F32), pltpu.VMEM((ffc, width), F32),
                        pltpu.VMEM((16, ffc), F32), pltpu.VMEM((16, width), F32)],
        compiler_params=pltpu.CompilerParams(vmem_limit_bytes=VMEM),
        cost_estimate=pl.CostEstimate(flops=2 * rows * width * 1344, bytes_accessed=20 << 20, transcendentals=rows * 512),
    )(both, both, wj, ww, add, back)


def late_kernel(xhat_ref, up_ref, mixed_ref, out_ref, mixedT_s, sum_s):
    rows, block = xhat_ref.shape
    m = mixed_ref.shape[1]
    n = out_ref.shape[1] - 16
    hd = m // 4

    @pl.when(pl.program_id(0) == 0)
    def _():
        mixedT_s[...] = mixed_ref[...].T
        sum_s[...] = dot_nn(jnp.ones((16, rows), BF16), mixed_ref[...]).astype(BF16)

    joint = dot_nn(mixedT_s[0:3 * hd, :], xhat_ref[...])
    dense = dot_nn(mixedT_s[3 * hd:, :], up_ref[...].reshape(rows, block))
    full = jnp.concatenate([joint, dense], axis=0).T.astype(BF16)
    for b in range(block // n):
        out_ref[b, 0:n, :] = full[b * n:(b + 1) * n]
        out_ref[b, n:, :] = sum_s[...]


def late_grads(xhat, both, mixed):
    rows, width = xhat.shape
    n, m = width // N_FSDP, mixed.shape[1]
    block = 2 * n
    return pl.pallas_call(
        late_kernel,
        grid=(width // block,),
        in_specs=[
            pl.BlockSpec((rows, block), lambda i: (0, i)),
            pl.BlockSpec((both.shape[0], 128, block), lambda i: (0, 1, i)),
            pl.BlockSpec(mixed.shape, lambda i: (0, 0))],
        out_specs=pl.BlockSpec((2, n + 16, m), lambda i: (i, 0, 0)),
        out_shape=jax.ShapeDtypeStruct((N_FSDP, n + 16, m), BF16),
        scratch_shapes=[pltpu.VMEM((m, rows), BF16), pltpu.VMEM((16, m), BF16)],
        compiler_params=pltpu.CompilerParams(vmem_limit_bytes=VMEM),
        cost_estimate=pl.CostEstimate(flops=2 * rows * width * m, bytes_accessed=10 << 20, transcendentals=0),
    )(xhat, both, mixed)


def spread_kernel(parity_ref, mixed_ref, wg_ref, act_ref, wj_ref, ww_ref, dense_ref, narrow_ref, *refs):
    out_ref = refs[-1]
    width = wj_ref.shape[0]
    chips, own = out_ref.shape[0], out_ref.shape[1]
    flat = lambda ref: ref[...].reshape(chips * own, ref.shape[3])
    mixed = flat(mixed_ref)
    u = dot_nt(mixed, wj_ref[...]) + dot_nt(flat(wg_ref), ww_ref[...])
    out = dot_nn(mixed, dense_ref[...]) + dot_nn(flat(act_ref), narrow_ref[...])
    for q in range(chips):
        rows = slice(q * own, (q + 1) * own)
        for value, at in ((u[rows], slice(0, width)), (out[rows], slice(width, 2 * width))):
            if len(refs) == 2:
                value = value + refs[0][q, :, at].astype(F32)
            out_ref[q, :, at] = value.astype(BF16)


def spread(parity, mixed, wg, act, wj, ww, dense, narrow, got=None):
    rows, width = mixed.shape[0], wj.shape[0]
    own, chips, per = rows // N_CTX, N_CTX // 2, 2
    whole = lambda a: pl.BlockSpec(a.shape, lambda i, parity: (0, 0))
    split = lambda a: a.reshape(chips, 2, own, a.shape[1])
    tall = lambda a: pl.BlockSpec((per, 1, own, a.shape[1]), lambda i, parity: (i, parity[0], 0, 0))
    block = pl.BlockSpec((per, own, 2 * width), lambda i, parity: (i, 0, 0))
    more = [] if got is None else [got]
    return pl.pallas_call(
        spread_kernel,
        grid_spec=pltpu.PrefetchScalarGridSpec(
            num_scalar_prefetch=1,
            grid=(chips // per,),
            in_specs=[tall(mixed), tall(wg), tall(act), whole(wj), whole(ww), whole(dense), whole(narrow)]
            + [block] * len(more),
            out_specs=block),
        out_shape=jax.ShapeDtypeStruct((chips, own, 2 * width), BF16),
        compiler_params=pltpu.CompilerParams(vmem_limit_bytes=VMEM),
        cost_estimate=pl.CostEstimate(flops=rows * width * 1024, bytes_accessed=9 << 20, transcendentals=0),
    )(parity, split(mixed), split(wg), split(act), wj, ww, dense, narrow, *more)


def finish_early_kernel(f_ref, all_ref, weight_ref, gain_ref, shift_ref,
                        widen_ref, narrow_ref, gain_out, shift_out, bias_out, bias_s):
    n, ff = weight_ref.shape
    k = all_ref.shape[2] // 2
    per = k // N_FSDP
    gain, shift = gain_ref[...], shift_ref[...]
    g_sum = jnp.zeros((n, n), F32)
    s_sum = jnp.zeros((n, n), F32)
    for c in range(N_CTX):
        for q in range(narrow_ref.shape[1] // k):
            narrow_ref[c * per:(c + 1) * per, q * k:(q + 1) * k] = all_ref[c, q * per:(q + 1) * per, k:].astype(F32)
    group = n // per
    for h in range(N_CTX // group):
        parts = [all_ref[h * group + i, :, :k].astype(F32) for i in range(group)]
        for f in range(N_FSDP):
            full = jnp.concatenate([p[:, f * per:(f + 1) * per] for p in parts], axis=1)
            m, bias = full[:n], full[n:n + 1]
            at = f * (ff // N_FSDP) + h * n
            w = weight_ref[:, at:at + n].astype(F32)
            widen_ref[:, at:at + n] = gain * m + shift * bias
            g_sum += w * m
            s_sum += w * bias
            bias_s[:, at:at + n] = full[n:n + 8]
    gain_out[...] = jnp.sum(g_sum.T, axis=0, keepdims=True)
    shift_out[...] = jnp.sum(s_sum.T, axis=0, keepdims=True)
    own = bias_out.shape[1]
    bias_out[...] = bias_s[:, pl.ds(pl.multiple_of(f_ref[0] * own, own), own)][0:1]


def finish_late_kernel(f_ref, core_ref, mine_ref, other_ref, weight_ref, gain_ref, shift_ref,
                       joint_ref, dense_ref, gain_out, shift_out, bias_out, bias_s):
    n = weight_ref.shape[0]
    hd = mine_ref.shape[2] // 4
    width = weight_ref.shape[1] // 3
    even = core_ref[0] == 0
    gain, shift = gain_ref[...], shift_ref[...]
    g_sum = jnp.zeros((n, 2 * hd), F32)
    s_sum = jnp.zeros((n, 2 * hd), F32)
    for q in range(mine_ref.shape[0]):
        mine, other = mine_ref[q].astype(F32), other_ref[q].astype(F32)
        pair = [jnp.where(even, mine, other), jnp.where(even, other, mine)]
        for k in range(3):
            full = jnp.concatenate([p[:, k * hd:(k + 1) * hd] for p in pair], axis=1)
            at = k * width + q * (2 * hd)
            m, bias = full[:n], full[n:n + 1]
            w = weight_ref[:, at:at + 2 * hd].astype(F32)
            joint_ref[:, at:at + 2 * hd] = gain * m + shift * bias
            g_sum += w * m
            s_sum += w * bias
            bias_s[:, at:at + 2 * hd] = full[n:n + 8]
        for b in range(2):
            dense_ref[b * hd:(b + 1) * hd, q * n:(q + 1) * n] = pair[b][:n].T[3 * hd:]
    gain_out[...] = jnp.sum(g_sum.T, axis=0, keepdims=True)
    shift_out[...] = jnp.sum(s_sum.T, axis=0, keepdims=True)
    own = bias_out.shape[1]
    bias_out[...] = bias_s[:, pl.ds(pl.multiple_of(f_ref[0] * own, 128), own)][0:1]


def finish(kernel, places, gathered, weight, gain, shift, side):
    n, columns = weight.shape
    vmem = pl.BlockSpec(memory_space=pltpu.VMEM)
    row = lambda m: jax.ShapeDtypeStruct((1, m), F32)
    wide = lambda v: v.astype(F32)[:, None]
    out = pl.pallas_call(
        kernel,
        in_specs=[pl.BlockSpec(memory_space=pltpu.SMEM)] * len(places) + [vmem] * (len(gathered) + 3),
        out_specs=[vmem] * 5,
        out_shape=[jax.ShapeDtypeStruct(weight.shape, F32), jax.ShapeDtypeStruct(side, F32), row(n), row(n),
                   row(columns // N_FSDP)],
        scratch_shapes=[pltpu.VMEM((8, columns), F32)],
        compiler_params=pltpu.CompilerParams(vmem_limit_bytes=VMEM),
        cost_estimate=pl.CostEstimate(flops=8 * weight.size, bytes_accessed=12 * weight.size, transcendentals=0),
    )(*places, *gathered, weight, wide(gain), wide(shift))
    return out[0], out[1], out[2][0], out[3][0], out[4][0]


def attention_kernel(order_ref, joint_ref, table_ref, grad_ref, out_ref,
                     joint_s, table_s, grad_s, k_s, v_s, qT_s, kT_s, vT_s, gT_s,
                     oT_s, dqT_s, dkT_s, dvT_s, cosT_s, sinT_s, out_s):
    rows, hd = joint_ref.shape[0], joint_ref.shape[1] // 4
    slots, half, tile = N_CTX, rows // (2 * N_CTX), 256
    last = 2 * slots - 1
    for j in range(slots):
        p = order_ref[j]
        for h in range(2):
            src = pl.ds(j * 2 * half + h * half, half)
            dst = pl.ds(pl.multiple_of((p if h == 0 else last - p) * half, half), half)
            joint_s[dst, :] = joint_ref[src, :]
            table_s[dst, :] = table_ref[src, :]
            grad_s[dst, :] = grad_ref[src, :]
    scale = hd ** -0.5

    def spin(t, c, s):
        return jnp.concatenate([t[0:8] * c - t[8:16] * s, t[8:16] * c + t[0:8] * s, t[16:]], axis=0)

    for i in range(rows // tile):
        at = pl.ds(i * tile, tile)
        jT = joint_s[at, :].T
        tT = table_s[at, :].T
        c, s = tT[0:8], tT[8:16]
        cosT_s[:, at] = c
        sinT_s[:, at] = s
        qT = spin(jT[0:hd], c, s).astype(BF16)
        kT = spin(jT[hd:2 * hd], c, s).astype(BF16)
        vT = jT[2 * hd:3 * hd].astype(BF16)
        qT_s[:, at] = (qT.astype(F32) * scale).astype(BF16)
        kT_s[:, at] = kT
        vT_s[:, at] = vT
        k_s[at, :] = kT.astype(F32).T.astype(BF16)
        v_s[at, :] = vT.astype(F32).T.astype(BF16)
        gT_s[:, at] = grad_s[at, :].T.astype(BF16)
    dkT_s[...] = jnp.zeros_like(dkT_s)
    dvT_s[...] = jnp.zeros_like(dvT_s)
    key_at = lax.broadcasted_iota(jnp.int32, (tile, tile), 0)
    query_at = lax.broadcasted_iota(jnp.int32, (tile, tile), 1)
    seen = key_at <= query_at
    dot = lambda a, b: jnp.dot(a, b, preferred_element_type=F32)
    dot_nt = lambda a, b: lax.dot_general(a, b, (((1,), (1,)), ((), ())), preferred_element_type=F32)
    for i in range(rows // tile):
        at = pl.ds(i * tile, tile)
        span = (i + 1) * tile
        upto = pl.ds(0, span)
        qT, gT = qT_s[:, at], gT_s[:, at]
        sT = dot(k_s[upto, :], qT)
        edge = jnp.where(seen, sT[i * tile:], NEGATIVE)
        sT = edge if i == 0 else jnp.concatenate([sT[:i * tile], edge], axis=0)
        largest = jnp.max(sT, axis=0, keepdims=True)
        e = jnp.exp(sT - largest)
        pT = e * (1.0 / jnp.sum(e, axis=0, keepdims=True))
        pT_low = pT.astype(BF16)
        dpT = dot(v_s[upto, :], gT)
        balance = jnp.sum(dpT * pT, axis=0, keepdims=True)
        dsT = (pT * (dpT - balance)).astype(BF16)
        oT_s[:, at] = dot(vT_s[:, upto], pT_low)
        dqT_s[:, at] = dot(kT_s[:, upto], dsT) * scale
        dkT_s[:, upto] += dot_nt(qT, dsT)
        dvT_s[:, upto] += dot_nt(gT, pT_low)
    for i in range(rows // tile):
        at = pl.ds(i * tile, tile)
        c, s = cosT_s[:, at], -sinT_s[:, at]
        full = jnp.concatenate(
            [spin(dqT_s[:, at], c, s), spin(dkT_s[:, at], c, s), dvT_s[:, at], oT_s[:, at]], axis=0)
        out_s[at, :] = full.T.astype(BF16)
    for j in range(slots):
        p = order_ref[j]
        for h in range(2):
            dst = pl.ds(j * 2 * half + h * half, half)
            src = pl.ds(pl.multiple_of((p if h == 0 else last - p) * half, half), half)
            out_ref[dst, :] = out_s[src, :]


def attention(order, joint, table, grad):
    rows, hd = joint.shape[0], joint.shape[1] // 4
    vmem = pl.BlockSpec(memory_space=pltpu.VMEM)
    return pl.pallas_call(
        attention_kernel,
        out_shape=jax.ShapeDtypeStruct((rows, 4 * hd), BF16),
        in_specs=[pl.BlockSpec(memory_space=pltpu.SMEM), vmem, vmem, vmem],
        out_specs=vmem,
        scratch_shapes=[
            pltpu.VMEM((rows, 4 * hd), F32),
            pltpu.VMEM((rows, 16), F32),
            pltpu.VMEM((rows, hd), F32),
            pltpu.VMEM((rows, hd), BF16),
            pltpu.VMEM((rows, hd), BF16),
            pltpu.VMEM((hd, rows), BF16),
            pltpu.VMEM((hd, rows), BF16),
            pltpu.VMEM((hd, rows), BF16),
            pltpu.VMEM((hd, rows), BF16),
            pltpu.VMEM((hd, rows), F32),
            pltpu.VMEM((hd, rows), F32),
            pltpu.VMEM((hd, rows), F32),
            pltpu.VMEM((hd, rows), F32),
            pltpu.VMEM((8, rows), F32),
            pltpu.VMEM((8, rows), F32),
            pltpu.VMEM((rows, 4 * hd), BF16),
        ],
        compiler_params=pltpu.CompilerParams(vmem_limit_bytes=VMEM),
        cost_estimate=pl.CostEstimate(flops=7 * rows * rows * hd, bytes_accessed=8 << 20, transcendentals=rows * rows // 2),
    )(order, joint, table, grad)


def shards(
    tokens, upstream, block_pairs, rotary_place,
    first_gain, first_shift, joint_weight, joint_bias, dense_weight, dense_bias,
    second_gain, second_shift, widen_weight, widen_bias, narrow_weight, narrow_bias,
):
    own_rows, width = tokens.shape[1], tokens.shape[2]
    hd = width // HEADS
    ff = widen_weight.shape[1]
    ffc = ff // N_CTX
    rows = own_rows * N_CTX
    c = lax.axis_index("ctx")
    f = lax.axis_index("fsdp")
    own_tokens, own_up = tokens[0], upstream[0]
    d_own = width // N_FSDP

    per = ffc // N_FSDP
    both = lax.all_gather(jnp.concatenate([own_tokens, own_up], axis=0), "ctx", axis=0)
    joint_part = lax.dynamic_index_in_dim(joint_weight.reshape(d_own, 3, HEADS, hd), c, 2, keepdims=False)
    vectors = jnp.concatenate(
        [v[:, None] for v in (first_gain, first_shift, second_gain, second_shift, dense_bias, narrow_bias)]
        + [joint_bias.reshape(d_own, 3), widen_bias.reshape(d_own, 4), jnp.zeros((d_own, 51), BF16)], axis=1)
    widen_part = [lax.dynamic_slice_in_dim(widen_weight, g * (ff // N_FSDP) + c * per, per, axis=1)
                  for g in range(N_FSDP)]
    narrow_part = lax.dynamic_slice_in_dim(narrow_weight, c * per, per, axis=0)
    narrow_part = jnp.concatenate([narrow_part[:, q * ffc:(q + 1) * ffc] for q in range(width // ffc)], axis=0)
    part = jnp.concatenate([joint_part.reshape(d_own, 3 * hd), vectors] + widen_part + [narrow_part], axis=1)
    slices = lax.all_to_all(jnp.broadcast_to(part[None], (N_FSDP,) + part.shape), "fsdp", 0, 0, tiled=True)
    dense_w = turn(lax.dynamic_slice_in_dim(dense_weight, (c % 2) * hd, hd, axis=0))
    place_all = lax.all_gather(rotary_place[0], "ctx", axis=0, tiled=True).astype(F32)
    narrow_w = jnp.concatenate(
        [slices[:, q * per:(q + 1) * per, 4 * hd + ffc:] for q in range(width // ffc)], axis=2).reshape(ffc, width)
    slices = slices.reshape(width, part.shape[1])
    back_w = jnp.concatenate([dense_w, narrow_w], axis=0)

    steps = jnp.arange(8, dtype=F32)
    angles = place_all[:, None] * (ROTARY_BASE ** (-2.0 * steps / 16))
    table = jnp.concatenate([jnp.cos(angles), jnp.sin(angles)], axis=1)
    order = block_pairs[0]

    wj = slices[:, :4 * hd].astype(F32)
    ww = slices[:, 4 * hd:4 * hd + ffc].astype(F32)
    vec = slices[:, 3 * hd:4 * hd].astype(F32)
    g1, s1, g2, s2 = vec[:, 0:1], vec[:, 1:2], vec[:, 2:3], vec[:, 3:4]
    dense_b, narrow_b = vec[:, 4], vec[:, 5]
    jb_full = vec[:, 6:9].reshape(3, HEADS, hd)
    wb_full = vec[:, 9:13].reshape(ff)
    jb_own = lax.dynamic_index_in_dim(jb_full, c, 1, keepdims=False).reshape(3 * hd)
    wb_own = lax.dynamic_index_in_dim(wb_full.reshape(N_FSDP, N_CTX, per), c, 1, keepdims=False).reshape(ffc)
    wj = jnp.where(jnp.arange(4 * hd)[None, :] < 3 * hd, wj, 0.0)
    wj_g = (g1 * wj).astype(BF16)
    ww_g = (g2 * ww).astype(BF16)
    shifted = jnp.concatenate([
        jnp.sum(s1 * wj, axis=0) + jnp.pad(jb_own, (0, hd)), jnp.sum(s2 * ww, axis=0) + wb_own])[None, :]
    dense_p = jnp.pad(dense_w, ((3 * hd, 0), (0, 0)))

    both, table, dense_p = tie(both, table, dense_p)
    xhat, joint, att_grad, act, wg, early = project(both, wj_g, ww_g, shifted, back_w)
    early = lax.all_to_all(early, "fsdp", 0, 0, tiled=True)

    mixed = attention(order, joint, table, att_grad)
    core = (c % 2)[None]
    shares = (mixed, wg, act, wj_g, ww_g, dense_p, narrow_w)
    other = spread(1 - core, *shares)
    other, early = tie(other, early)

    early = jnp.sum(early.astype(F32), axis=0)
    bias_grad = early[d_own, ffc:ffc + d_own]
    early_all = lax.all_gather(early.astype(BF16), "ctx", axis=0)
    late, other = tie(late_grads(xhat, both, mixed), lax.ppermute(other, "ctx", OTHER_CORE))
    pair = spread(core, *shares, other)
    late, pair = tie(lax.all_to_all(late, "fsdp", 0, 0, tiled=True), pair)
    low = jnp.sum(late.astype(F32), axis=0).astype(BF16)

    summed = lax.all_to_all(pair, "ctx", 0, 0, tiled=True, axis_index_groups=SAME_CORE)
    widen_grad, narrow_grad, g2_grad, s2_grad, wb_shard = finish(
        finish_early_kernel, (f[None],), (early_all,), widen_weight, second_gain, second_shift, (2 * ffc, width))
    low, summed, wb_shard = tie(
        jnp.concatenate([low[:, :3 * hd], turn(low[:, 3 * hd:])], axis=1), summed, wb_shard)
    late_all = gather_chips(low)
    summed = jnp.sum(summed.astype(F32), axis=0)
    u_own, out_own = summed[:, :width], summed[:, width:]

    own_x = own_tokens.astype(F32)
    block_out = (own_x + out_own + dense_b + narrow_b).astype(BF16)
    own_center = own_x - jnp.mean(own_x, axis=-1, keepdims=True)
    own_rstd = lax.rsqrt(jnp.mean(own_center * own_center, axis=-1, keepdims=True) + EPSILON)
    own_xhat = own_center * own_rstd
    tokens_grad = own_up.astype(F32) + own_rstd * (
        u_own - jnp.mean(u_own, axis=-1, keepdims=True)
        - own_xhat * jnp.mean(u_own * own_xhat, axis=-1, keepdims=True))

    joint_grad, dense_grad, g1_grad, s1_grad, jb_shard = finish(
        finish_late_kernel, (f[None], core), late_all, joint_weight, first_gain, first_shift, (2 * hd, width))
    return (
        block_out[None], tokens_grad[None], g1_grad, s1_grad, joint_grad, jb_shard,
        dense_grad, bias_grad, g2_grad, s2_grad, widen_grad, wb_shard, narrow_grad, bias_grad,
    )


def solution(mesh):
    rows = P("fsdp", "ctx", None)
    vec, mat = P("fsdp"), P("fsdp", None)
    in_specs = (rows, rows, mat, P("fsdp", "ctx"), vec, vec, mat, vec, mat, vec, vec, vec, mat, vec, mat, vec)
    out_specs = (rows, rows, vec, vec, mat, vec, mat, vec, vec, vec, mat, vec, mat, vec)
    return jax.shard_map(shards, mesh=mesh, in_specs=in_specs, out_specs=out_specs, check_vma=False)
```

time: 322 us -> 253 us (0.79)
  waiting for transfers between devices: 140 us -> 64.7 us
  local copies, waits for them, and re-layouts: 38.3 us -> 15.3 us
  starting transfers between devices: 26.2 us -> 48.1 us
  Pallas kernels: 41.4 us -> 59.8 us
  other arithmetic: 26.9 us -> 12.7 us
  blocking collectives: 30.2 us -> 35.9 us
    ppermute x2, waiting for transfers between devices: 43.8 us -> 0.01 us  [turn(): return lax.ppermute(v, ('ctx', 'fsdp'), TURN)]
    all_gather x0 -> x1, blocking collectives: none -> 35.9 us  [shards(): lax.all_gather(rotary_place[0], 'ctx', axis=0, tiled=True).astype(F32)]
    all_to_all x1 -> x4, waiting for transfers between devices: 65.9 us -> 35.7 us  [the longest x1 26 us: shards(): lax.all_to_all(pair, 'ctx', 0, 0, tiled=True, axis_index_groups=SAME_CORE)]
    all_to_all x1 -> x0, blocking collectives: 30.2 us -> none  [shards(): lax.all_to_all(grads(xhat, both, mixed, act, wg), 'fsdp', 0, 0, tiled=True)]
    all_to_all x1 -> x4, starting transfers between devices: 4.72 us -> 28.1 us  [the longest x1 9.13 us: shards(): early = lax.all_to_all(early, 'fsdp', 0, 0, tiled=True)]
    unnamed x58 -> x38, local copies, waits for them, and re-layouts: 14.5 us -> 1.78 us
    convert_element_type x9 -> x2, other arithmetic: 12.4 us -> 0.69 us  [the longest x1 0.68 us: shards(): early_all = lax.all_gather(early.astype(BF16), 'ctx', axis=0)]
    pallas_call x2 -> x5, Pallas kernels: 18.5 us -> 29.9 us  [the longest x2 13.8 us: spread(): pl.pallas_call(spread_kernel, grid_spec=pltpu.PrefetchScalarGridSpec(num_...]
  transfers between devices with their start and end apart: 7 -> 11, of which waited for: 4 -> 6; matrix products, arithmetic and copies ran while one was open for 8% -> 9% of each run, Pallas kernels for 3% -> 16%
where the time goes in v1:
time: 253 us; the launch traced here: 251 us
  waiting for transfers between devices  64.7 us (26%)
  Pallas kernels  59.8 us (24%)
  starting transfers between devices  48.1 us (19%)
  blocking collectives  35.9 us (14%)
  local copies, waits for them, and re-layouts  15.3 us (6%)
  between operations  14.5 us (6%)
  other arithmetic  12.7 us (5%)
    all_gather x1, blocking collectives, shards(): lax.all_gather(rotary_place[0], 'ctx', axis=0, tiled=True).astype(F32)  35.9 us
    all_to_all x1, waiting for transfers between devices, shards(): lax.all_to_all(pair, 'ctx', 0, 0, tiled=True, axis_index_groups=SAME_CORE)  26 us
    pallas_call x1, Pallas kernels, attention(): pl.pallas_call(attention_kernel, out_shape=jax.ShapeDtypeStruct((rows, 4...  15.2 us
    all_gather x1, waiting for transfers between devices, shards(): early_all = lax.all_gather(early.astype(BF16), 'ctx', axis=0)  14.8 us
    pallas_call x1, Pallas kernels, project(): pl.pallas_call(project_kernel, grid=(slots // per,), in_specs=[pl.BlockSp...  14.6 us
    pallas_call x2, Pallas kernels, spread(): pl.pallas_call(spread_kernel, grid_spec=pltpu.PrefetchScalarGridSpec(num_...  13.8 us
    all_gather x1, waiting for transfers between devices, shards(): lax.all_gather(jnp.concatenate([own_tokens, own_up], axis=0), 'ctx', axis=0)  13.6 us
    ppermute x2, starting transfers between devices, turn(): return lax.ppermute(v, ('ctx', 'fsdp'), TURN)  12.6 us
  transfers between devices with their start and end apart: 11, of which 6 were waited for; matrix products, arithmetic and copies ran while one was open for 9% of the time, Pallas kernels for 16%

profile of v1, /device:TPU:22, one launch (start us, length us, event | category | flops | bytes accessed | tf_op | source)
XLA Modules:
  0.0 251.0 jit_solution(13896231235065962073)
XLA Ops:
  7.3 1.9 pad_maximum_fusion.1
  9.3 0.4 copy.66
  9.7 0.1 copy.67
  9.8 0.1 copy.68
  10.0 0.1 copy.69
  10.1 0.1 copy.70
  10.2 0.1 copy.71
  10.4 0.1 copy.72
  10.5 0.1 copy.73
  10.7 0.2 reshape.115
  10.9 0.1 reshape.116
  11.0 0.8 constant_dynamic-slice_fusion
  11.8 1.0 constant_dynamic-slice_fusion.2
  12.9 0.2 concatenate.27
  13.1 1.2 broadcast_in_dim.87
  14.4 7.3 %all-to-all-start = ((bf16[8,128,768]{2,1,0:T(8,128)(2,1)}), bf16[8,128,768]{2,1,0:T(8,128)(2,1)S(1)}, u32[]{:S(2)}, u32[]{:S(2)}) async-start(bf16[8,128,768]{2,1,0:T(8,128)(2,1)} %broadcast_in_dim.87), calls=%async_computation | async-start | bytes 3145728 | tf_op jit(solution)/shard_map/all_to_all | solution.py:410
  21.7 4.6 %collective-permute-start = (bf16[64,1024]{1,0:T(8,128)(2,1)S(1)}, bf16[64,1024]{1,0:T(8,128)(2,1)S(1)}, u32[]{:S(2)}, u32[]{:S(2)}) collective-permute-start(bf16[64,1024]{1,0:T(8,128)(2,1)S(1)} %constant_dynamic-slice_fusion.11), channel_id=1, source_target_pairs={{0,0},{1,16},{2,32},{3,48},{4,64},{5,80},{6,96},{7,112},{8,8},{9,2... | collective-permute-start | bytes 393224 | tf_op jit(solution)/shard_map/ppermute | solution.py:28
  26.3 35.9 %all-gather.1 = s32[1,2048]{1,0:T(1,128)S(1)} all-gather(s32[1,128]{1,0:T(1,128)S(1)} %copy-done.16), channel_id=3, replica_groups=mesh['ctx'=16,'fsdp'=8] {'ctx'}, dimensions={1}, use_global_device_ids=true | all-gather | bytes 8704 | tf_op jit(solution)/shard_map/all_gather | solution.py:412
  62.3 0.3 multiply_cosine_fusion
  62.7 0.9 pad.8.dense_ref
  63.5 0.1 slice_convert_fusion
  63.7 0.2 slice.104
  63.9 0.2 slice.102
  64.1 0.2 reshape_reshape.3
  64.4 0.3 reshape.118
  64.8 1.6 slice_reduce_fusion.1
  66.4 1.7 multiply_reduce_fusion
  68.1 0.6 pad_maximum_fusion.6
  68.8 1.0 pad_maximum_fusion.back_ref
  69.8 13.6 %all-gather.6.cloned.1.call-done = bf16[4096,1024]{1,0:T(8,128)(2,1)} async-done(((bf16[256,1024]{1,0:T(8,128)(2,1)}), bf16[4096,1024]{1,0:T(8,128)(2,1)}) %all-gather.6.cloned.1.call-update) | async-done | bytes 8388624 | tf_op jit(solution)/shard_map/all_gather | solution.py:400
  83.4 14.6 %shard_map.263 = (bf16[2048,1024]{1,0:T(8,128)(2,1)}, f32[2048,256]{1,0:T(8,128)}, f32[2048,64]{1,0:T(8,128)}, bf16[2048,256]{1,0:T(8,128)(2,1)}, bf16[2048,256]...) custom-call(bf16[16,256,1024]{2,1,0:T(8,128)(2,1)} %bitcast.46, bf16[16,256,1024]{2,1,0:T(8,128)(2,1)} %bitcast.47, ...), custom_call_target="tpu_custom_call" | custom-call | flops 5637144576 | bytes 20971520 | tf_op jit(solution)/shard_map/pallas_call | solution.py:106
  98.0 9.1 %all-to-all-start.1 = ((bf16[8,144,512]{2,1,0:T(8,128)(2,1)}), bf16[8,144,512]{2,1,0:T(8,128)(2,1)S(1)}, u32[]{:S(2)}, u32[]{:S(2)}) async-start(bf16[8,144,512]{2,1,0:T(8,128)(2,1)} %get-tuple-element.50), calls=%async_computation.1 | async-start | bytes 2359296 | tf_op jit(solution)/shard_map/all_to_all | solution.py:441
  107.2 1.4 copy.74.table_ref
  108.6 15.2 %shard_map.264.mixed_ref = bf16[2048,256]{1,0:T(8,128)(2,1)} custom-call(s32[16]{0:T(128)} %bitcast.73, f32[2048,256]{1,0:T(8,128)} %get-tuple-element.44.joint_ref, f32[2048,16]{1,0:T(8,128)} %copy.74.table_ref, f32[2048,64]{1,0:T(8,128)} %get-tuple-element.46.grad_ref), custom_call_target="tpu_custom_call" | custom-call | flops 1879048192 | bytes 8388608 | tf_op jit(solution)/shard_map/pallas_call | solution.py:356
  123.8 6.5 %shard_map.266 = bf16[8,128,2048]{2,1,0:T(8,128)(2,1)} custom-call(s32[1]{0:T(128)S(6)} %sub.22.parity_ref, bf16[8,2,128,256]{3,2,1,0:T(8,128)(2,1)} %bitcast.44, bf16[8,2,128,256]{3,2,1,0:T(8,128)(2,1)} %bitcast.57, bf16[8,2,128,256]{3,2,1,0:T(8,128)(2,1)} %bitcast.55, bf16[1024,256]{1,0:T(8,128)(2,1)} %get-tuple-element.80.wj_ref, ...), custom_call_target="tpu_custom_call" | custom-call | flops 2147483648 | bytes 9437184 | tf_op jit(solution)/shard_map/pallas_call | solution.py:188
  130.3 0.2 convert_reduce_fusion.1
  130.5 0.7 convert_element_type.64
  131.2 6.8 %shard_map.265 = bf16[8,144,256]{2,1,0:T(8,128)(2,1)} custom-call(bf16[2048,1024]{1,0:T(8,128)(2,1)} %get-tuple-element.43.xhat_ref, bf16[16,256,1024]{2,1,0:T(8,128)(2,1)} %bitcast.48, bf16[2048,256]{1,0:T(8,128)(2,1)} %shard_map.264.mixed_ref), custom_call_target="tpu_custom_call" | custom-call | flops 1073741824 | bytes 10485760 | tf_op jit(solution)/shard_map/pallas_call | solution.py:149
  138.0 7.2 %all-to-all-start.2 = ((bf16[8,144,256]{2,1,0:T(8,128)(2,1)}), bf16[8,144,256]{2,1,0:T(8,128)(2,1)S(1)}, u32[]{:S(2)}, u32[]{:S(2)}) async-start(bf16[8,144,256]{2,1,0:T(8,128)(2,1)} %shard_map.265), calls=%async_computation.2 | async-start | bytes 1179648 | tf_op jit(solution)/shard_map/all_to_all | solution.py:454
  145.2 7.3 %shard_map.267 = bf16[8,128,2048]{2,1,0:T(8,128)(2,1)} custom-call(s32[1]{0:T(128)} %bitcast.16.parity_ref.core_ref, bf16[8,2,128,256]{3,2,1,0:T(8,128)(2,1)} %bitcast.45, bf16[8,2,128,256]{3,2,1,0:T(8,128)(2,1)} %bitcast.58, bf16[8,2,128,256]{3,2,1,0:T(8,128)(2,1)} %bitcast.56, bf16[1024,256]{1,0:T(8,128)(2,1)} %get-tuple-element.80.wj_ref, ...), custom_call_target="tpu_custom_call" | custom-call | flops 2147483648 | bytes 9437184 | tf_op jit(solution)/shard_map/pallas_call | solution.py:188
  152.5 1.5 all-to-all-done.2
  154.1 6.3 %all-to-all-start.3 = ((bf16[8,128,2048]{2,1,0:T(8,128)(2,1)}), bf16[8,128,2048]{2,1,0:T(8,128)(2,1)}, u32[]{:S(2)}, u32[]{:S(2)}) async-start(bf16[8,128,2048]{2,1,0:T(8,128)(2,1)} %shard_map.267), calls=%async_computation.3 | async-start | bytes 8388608 | tf_op jit(solution)/shard_map/all_to_all | solution.py:457
  160.4 0.1 convert_reduce_fusion.2
  160.5 0.2 fusion.11
  160.9 7.9 %collective-permute-start.2 = (bf16[144,64]{1,0:T(8,128)(2,1)S(1)}, bf16[144,64]{1,0:T(8,128)(2,1)S(1)}, u32[]{:S(2)}, u32[]{:S(2)}) collective-permute-start(bf16[144,64]{1,0:T(8,128)(2,1)S(1)} %slice.110), channel_id=1, source_target_pairs={{0,0},{1,16},{2,32},{3,48},{4,64},{5,80},{6,96},{7,112},{8,8},{9,2... | collective-permute-start | bytes 55304 | tf_op jit(solution)/shard_map/ppermute | solution.py:28
  168.9 0.7 copy.75.gain_ref
  169.6 0.7 copy.76.shift_ref
  170.4 0.7 copy.77.gain_ref
  171.1 0.7 copy.78.shift_ref
  171.8 14.8 %all-gather.8.cloned.1.call-done = bf16[2304,512]{1,0:T(8,128)(2,1)} async-done(((bf16[144,512]{1,0:T(8,128)(2,1)}), bf16[2304,512]{1,0:T(8,128)(2,1)}) %all-gather.8.cloned.1.call-update) | async-done | bytes 2359312 | tf_op jit(solution)/shard_map/all_gather | solution.py:451
  186.6 5.5 %shard_map.268 = (f32[128,4096]{1,0:T(8,128)}, f32[512,1024]{1,0:T(8,128)}, f32[1,128]{1,0:T(1,128)}, f32[1,128]{1,0:T(1,128)}, f32[1,512]{1,0:T(1,128)}) custom-call(s32[1]{0:T(128)} %bitcast.20.f_ref, bf16[16,144,512]{2,1,0:T(8,128)(2,1)} %bitcast.59, bf16[128,4096]{1,0:T(8,128)(2,1)} %weight_ref.2, f32[128,1]{1,0:T(8,128)} %copy.75.gain_ref, ...), custom_call_target="tpu_custom_call" | custom-call | flops 4194304 | bytes 6291456 | tf_op jit(solution)/shard_map/pallas_call | solution.py:265
  192.1 0.1 pad_maximum_fusion.4
  192.2 26.0 %all-to-all-done.3 = bf16[8,128,2048]{2,1,0:T(8,128)(2,1)} async-done(((bf16[8,128,2048]{2,1,0:T(8,128)(2,1)}), bf16[8,128,2048]{2,1,0:T(8,128)(2,1)}, u32[]{:S(2)}, u32[]{:S(2)}) %all-to-all-start.3) | async-done | bytes 4194336 | tf_op jit(solution)/shard_map/all_to_all | solution.py:457
  218.2 0.9 broadcast_in_dim.97
  219.1 5.5 %all-to-all-start.4 = ((bf16[8,144,256]{2,1,0:T(8,128)(2,1)}), bf16[8,144,256]{2,1,0:T(8,128)(2,1)S(1)}, u32[]{:S(2)}, u32[]{:S(2)}) async-start(bf16[8,144,256]{2,1,0:T(8,128)(2,1)} %broadcast_in_dim.97), calls=%async_computation.4 | async-start | bytes 1179648 | tf_op jit(solution)/shard_map/all_to_all | solution.py:32
  224.6 3.0 %convert_reduce_fusion = f32[128,2048]{1,0:T(8,128)S(1)} fusion(bf16[8,128,2048]{2,1,0:T(8,128)(2,1)} %all-to-all-done.3), kind=kLoop, calls=%fused_computation | loop fusion | flops 3932160 | bytes 5242880 | tf_op jit(solution)/shard_map/reduce_sum | solution.py:463
  227.6 8.1 %all-to-all-done.4.mine_ref = bf16[8,144,256]{2,1,0:T(8,128)(2,1)S(1)} async-done(((bf16[8,144,256]{2,1,0:T(8,128)(2,1)}), bf16[8,144,256]{2,1,0:T(8,128)(2,1)S(1)}, u32[]{:S(2)}, u32[]{:S(2)}) %all-to-all-start.4) | async-done | bytes 589856 | tf_op jit(solution)/shard_map/all_to_all | solution.py:32
  235.7 0.2 slice_reduce_fusion.6
  236.0 1.1 fusion.10
  237.0 0.7 collective-permute-done.3.other_ref
  237.7 0.8 copy-done.7
  238.5 3.8 %shard_map.269 = (f32[128,3072]{1,0:T(8,128)}, f32[128,1024]{1,0:T(8,128)}, f32[1,128]{1,0:T(1,128)}, f32[1,128]{1,0:T(1,128)}, f32[1,384]{1,0:T(1,128)}) custom-call(s32[1]{0:T(128)} %bitcast.20.f_ref, s32[1]{0:T(128)} %bitcast.16.parity_ref.core_ref, bf16[8,144,256]{2,1,0:T(8,128)(2,1)} %copy-done.5, bf16[8,144,256]{2,1,0:T(8,128)(2,1)} %copy-done.7, ...), custom_call_target="tpu_custom_call" | custom-call | flops 3145728 | bytes 4718592 | tf_op jit(solution)/shard_map/pallas_call | solution.py:265
  242.4 1.3 reduce.9
  243.6 0.5 copy.80
  (72 shorter events, 0.8 us)
Async XLA Ops:
  7.2 14.5 %copy-start = (bf16[128,1024]{1,0:T(8,128)(2,1)S(1)}, bf16[128,1024]{1,0:T(8,128)(2,1)}, u32[]{:S(2)}) copy-start(bf16[128,1024]{1,0:T(8,128)(2,1)} %param.24) | copy-start | bytes 786436
  7.2 2.1 copy-start.4
  7.2 2.6 %copy-start.14 = (bf16[128]{0:T(256)(128)(2,1)S(1)}, bf16[128]{0:T(256)(128)(2,1)}, u32[]{:S(2)}) copy-start(bf16[128]{0:T(256)(128)(2,1)} %param.20) | copy-start | bytes 772
  7.2 2.7 %copy-start.15 = (bf16[128]{0:T(256)(128)(2,1)S(1)}, bf16[128]{0:T(256)(128)(2,1)}, u32[]{:S(2)}) copy-start(bf16[128]{0:T(256)(128)(2,1)} %param.21) | copy-start | bytes 772
  7.2 2.9 %copy-start.12 = (bf16[128]{0:T(256)(128)(2,1)S(1)}, bf16[128]{0:T(256)(128)(2,1)}, u32[]{:S(2)}) copy-start(bf16[128]{0:T(256)(128)(2,1)} %param.26) | copy-start | bytes 772
  7.2 3.0 %copy-start.13 = (bf16[128]{0:T(256)(128)(2,1)S(1)}, bf16[128]{0:T(256)(128)(2,1)}, u32[]{:S(2)}) copy-start(bf16[128]{0:T(256)(128)(2,1)} %param.27) | copy-start | bytes 772
  7.3 3.1 %copy-start.10 = (bf16[128]{0:T(256)(128)(2,1)S(1)}, bf16[128]{0:T(256)(128)(2,1)}, u32[]{:S(2)}) copy-start(bf16[128]{0:T(256)(128)(2,1)} %param.25) | copy-start | bytes 772
  7.3 3.3 %copy-start.11 = (bf16[128]{0:T(256)(128)(2,1)S(1)}, bf16[128]{0:T(256)(128)(2,1)}, u32[]{:S(2)}) copy-start(bf16[128]{0:T(256)(128)(2,1)} %param.31) | copy-start | bytes 772
  7.3 3.4 %copy-start.8 = (bf16[384]{0:T(512)(128)(2,1)S(1)}, bf16[384]{0:T(512)(128)(2,1)}, u32[]{:S(2)}) copy-start(bf16[384]{0:T(512)(128)(2,1)} %param.23) | copy-start | bytes 2308
  7.3 3.6 %copy-start.9 = (bf16[512]{0:T(512)(128)(2,1)S(1)}, bf16[512]{0:T(512)(128)(2,1)}, u32[]{:S(2)}) copy-start(bf16[512]{0:T(512)(128)(2,1)} %param.29) | copy-start | bytes 3076
  7.3 76.1 %all-gather.6.cloned.1.call-start = ((), (), s32[]{:S(2)}) async-start(), calls=%async_computation.5 | async-start | bytes 8912896 | tf_op jit(solution)/shard_map/all_gather | solution.py:400
  14.4 12.0 %copy-start.16 = (s32[1,128]{1,0:T(1,128)S(1)}, s32[1,128]{1,0:T(1,128)}, u32[]{:S(2)}) copy-start(s32[1,128]{1,0:T(1,128)} %param.19) | copy-start | bytes 1540
  14.4 49.2 %all-to-all-start = ((bf16[8,128,768]{2,1,0:T(8,128)(2,1)}), bf16[8,128,768]{2,1,0:T(8,128)(2,1)S(1)}, u32[]{:S(2)}, u32[]{:S(2)}) async-start(bf16[8,128,768]{2,1,0:T(8,128)(2,1)} %broadcast_in_dim.87), calls=%async_computation | async-start | bytes 3145728 | tf_op jit(solution)/shard_map/all_to_all | solution.py:410
  21.7 40.9 %collective-permute-start = (bf16[64,1024]{1,0:T(8,128)(2,1)S(1)}, bf16[64,1024]{1,0:T(8,128)(2,1)S(1)}, u32[]{:S(2)}, u32[]{:S(2)}) collective-permute-start(bf16[64,1024]{1,0:T(8,128)(2,1)S(1)} %constant_dynamic-slice_fusion.11), channel_id=1, source_target_pairs={{0,0},{1,16},{2,32},{3,48},{4,64},{5,80},{6,96},{7,112},{8,8},{9,2... | collective-permute-start | bytes 393224 | tf_op jit(solution)/shard_map/ppermute | solution.py:28
  68.8 29.2 %copy-start.2 = (bf16[8,32,1024]{2,1,0:T(8,128)(2,1)}, bf16[8,32,1024]{2,1,0:T(8,128)(2,1)S(1)}, u32[]{:S(2)}) copy-start(bf16[8,32,1024]{2,1,0:T(8,128)(2,1)S(1)} %pad_maximum_fusion.2) | copy-start | bytes 1572868
  98.0 32.2 %all-to-all-start.1 = ((bf16[8,144,512]{2,1,0:T(8,128)(2,1)}), bf16[8,144,512]{2,1,0:T(8,128)(2,1)S(1)}, u32[]{:S(2)}, u32[]{:S(2)}) async-start(bf16[8,144,512]{2,1,0:T(8,128)(2,1)} %get-tuple-element.50), calls=%async_computation.1 | async-start | bytes 2359296 | tf_op jit(solution)/shard_map/all_to_all | solution.py:441
  107.2 79.4 %all-gather.8.cloned.1.call-start = ((), (), s32[]{:S(2)}) async-start(), calls=%async_computation.6 | async-start | bytes 2506752 | tf_op jit(solution)/shard_map/all_gather | solution.py:451
  130.3 7.7 %collective-permute-start.1 = (bf16[8,128,2048]{2,1,0:T(8,128)(2,1)}, bf16[8,128,2048]{2,1,0:T(8,128)(2,1)}, u32[]{:S(2)}, u32[]{:S(2)}) collective-permute-start(bf16[8,128,2048]{2,1,0:T(8,128)(2,1)} %shard_map.266), channel_id=1, source_target_pairs={{8,0},{0,8},{24,16},{16,24},{40,32},{32,40},{56,48},{48,56},{72,64... | collective-permute-start | bytes 12582920 | tf_op jit(solution)/shard_map/ppermute | solution.py:452
  138.0 16.1 %all-to-all-start.2 = ((bf16[8,144,256]{2,1,0:T(8,128)(2,1)}), bf16[8,144,256]{2,1,0:T(8,128)(2,1)S(1)}, u32[]{:S(2)}, u32[]{:S(2)}) async-start(bf16[8,144,256]{2,1,0:T(8,128)(2,1)} %shard_map.265), calls=%async_computation.2 | async-start | bytes 1179648 | tf_op jit(solution)/shard_map/all_to_all | solution.py:454
  152.5 7.8 %copy-start.3 = (bf16[1,128,1024]{2,1,0:T(8,128)(2,1)S(1)}, bf16[1,128,1024]{2,1,0:T(8,128)(2,1)}, u32[]{:S(2)}) copy-start(bf16[1,128,1024]{2,1,0:T(8,128)(2,1)} %param.16) | copy-start | bytes 786436
  154.1 64.1 %all-to-all-start.3 = ((bf16[8,128,2048]{2,1,0:T(8,128)(2,1)}), bf16[8,128,2048]{2,1,0:T(8,128)(2,1)}, u32[]{:S(2)}, u32[]{:S(2)}) async-start(bf16[8,128,2048]{2,1,0:T(8,128)(2,1)} %shard_map.267), calls=%async_computation.3 | async-start | bytes 8388608 | tf_op jit(solution)/shard_map/all_to_all | solution.py:457
  160.9 31.2 %collective-permute-start.2 = (bf16[144,64]{1,0:T(8,128)(2,1)S(1)}, bf16[144,64]{1,0:T(8,128)(2,1)S(1)}, u32[]{:S(2)}, u32[]{:S(2)}) collective-permute-start(bf16[144,64]{1,0:T(8,128)(2,1)S(1)} %slice.110), channel_id=1, source_target_pairs={{0,0},{1,16},{2,32},{3,48},{4,64},{5,80},{6,96},{7,112},{8,8},{9,2... | collective-permute-start | bytes 55304 | tf_op jit(solution)/shard_map/ppermute | solution.py:28
  219.1 16.7 %all-to-all-start.4 = ((bf16[8,144,256]{2,1,0:T(8,128)(2,1)}), bf16[8,144,256]{2,1,0:T(8,128)(2,1)S(1)}, u32[]{:S(2)}, u32[]{:S(2)}) async-start(bf16[8,144,256]{2,1,0:T(8,128)(2,1)} %broadcast_in_dim.97), calls=%async_computation.4 | async-start | bytes 1179648 | tf_op jit(solution)/shard_map/all_to_all | solution.py:32
  224.5 19.1 %copy-start.17 = (f32[128]{0:T(128)}, f32[128]{0:T(128)S(1)}, u32[]{:S(2)}) copy-start(f32[128]{0:T(128)S(1)} %slice_bitcast_fusion) | copy-start | bytes 1540
  224.5 11.4 %copy-start.6 = (bf16[1,128,1024]{2,1,0:T(8,128)(2,1)S(1)}, bf16[1,128,1024]{2,1,0:T(8,128)(2,1)}, u32[]{:S(2)}) copy-start(bf16[1,128,1024]{2,1,0:T(8,128)(2,1)} %param.17) | copy-start | bytes 786436
  235.7 2.0 copy-start.5
  235.7 2.0 collective-permute-start.3
  236.0 8.2 %copy-start.1 = (bf16[128,1024]{1,0:T(8,128)(2,1)S(1)}, bf16[128,1024]{1,0:T(8,128)(2,1)}, u32[]{:S(2)}) copy-start(bf16[128,1024]{1,0:T(8,128)(2,1)} %param.24) | copy-start | bytes 786436
  237.7 0.8 copy-start.7
Sparse Core Ops, SparseCore 0:
  10.4 72.9 all-gather.5
  131.3 55.2 all-gather.7

commit v2 on v1

--- a/solution.py
+++ b/solution.py
@@ -15,7 +15,9 @@
 F32 = jnp.float32
 BF16 = jnp.bfloat16
 
+ACROSS_Y = [(i ^ 2, i) for i in range(16)]
 OTHER_CORE = [(i ^ 1, i) for i in range(16)]
+AHEAD_Z = [[(i, (i + 4 * d) % 16) for i in range(16)] for d in range(4)]
 SAME_CORE = [list(range(0, 16, 2)), list(range(1, 16, 2))]
 TURN = [(c * 8 + f, (2 * f + (c & 1)) * 8 + (c >> 1)) for c in range(16) for f in range(8)]
 
@@ -28,10 +30,13 @@
     return lax.ppermute(v, ("ctx", "fsdp"), TURN)
 
 
+def move(v, way):
+    return lax.ppermute(v, "ctx", way)
+
+
 def gather_chips(own):
-    mine = lax.all_to_all(jnp.broadcast_to(own[None], (N_CTX // 2,) + own.shape), "ctx", 0, 0, tiled=True,
+    return lax.all_to_all(jnp.broadcast_to(own[None], (N_CTX // 2,) + own.shape), "ctx", 0, 0, tiled=True,
                           axis_index_groups=SAME_CORE)
-    return mine, lax.ppermute(mine, "ctx", OTHER_CORE)
 
 
 def dot_tn(a, b):
@@ -161,42 +166,61 @@
     )(xhat, both, mixed)
 
 
-def spread_kernel(parity_ref, mixed_ref, wg_ref, act_ref, wj_ref, ww_ref, dense_ref, narrow_ref, *refs):
-    out_ref = refs[-1]
-    width = wj_ref.shape[0]
-    chips, own = out_ref.shape[0], out_ref.shape[1]
+def spread_kernel(place_ref, mixed_ref, wg_ref, act_ref, wj_ref, ww_ref, dense_ref, narrow_ref, *refs):
+    chips, own = mixed_ref.shape[0], mixed_ref.shape[2]
     flat = lambda ref: ref[...].reshape(chips * own, ref.shape[3])
     mixed = flat(mixed_ref)
     u = dot_nt(mixed, wj_ref[...]) + dot_nt(flat(wg_ref), ww_ref[...])
     out = dot_nn(mixed, dense_ref[...]) + dot_nn(flat(act_ref), narrow_ref[...])
-    for q in range(chips):
-        rows = slice(q * own, (q + 1) * own)
-        for value, at in ((u[rows], slice(0, width)), (out[rows], slice(width, 2 * width))):
-            if len(refs) == 2:
-                value = value + refs[0][q, :, at].astype(F32)
-            out_ref[q, :, at] = value.astype(BF16)
-
-
-def spread(parity, mixed, wg, act, wj, ww, dense, narrow, got=None):
+    u = [u[q * own:(q + 1) * own] for q in range(chips)]
+    out = [out[q * own:(q + 1) * own] for q in range(chips)]
+    far = [q ^ place_ref[1] for q in range(chips)]
+    if len(refs) == 1:
+        for q in range(chips):
+            refs[0][0, far[q]] = u[q].astype(BF16)
+            refs[0][1, far[q]] = out[q].astype(BF16)
+        return
+    got_ref, near_ref, far_ref = refs[:3]
+    u = [(u[q] + got_ref[0, far[q]].astype(F32)).astype(BF16) for q in range(chips)]
+    out = [(out[q] + got_ref[1, far[q]].astype(F32)).astype(BF16) for q in range(chips)]
+    low = place_ref[1] == 0
+    near_ref[0] = jnp.where(low, u[0], u[1])
+    far_ref[0] = jnp.where(low, u[1], u[0])
+    for d, ref in enumerate(refs[3:]):
+        @pl.when(pl.program_id(0) == d)
+        def _():
+            ref[0] = jnp.where(low, out[0], out[1])
+            ref[1] = jnp.where(low, out[1], out[0])
+
+
+def spread(place, mixed, wg, act, wj, ww, dense, narrow, got=None):
     rows, width = mixed.shape[0], wj.shape[0]
     own, chips, per = rows // N_CTX, N_CTX // 2, 2
-    whole = lambda a: pl.BlockSpec(a.shape, lambda i, parity: (0, 0))
+    deep = chips // per
+    whole = lambda a: pl.BlockSpec(a.shape, lambda i, place: (0, 0))
     split = lambda a: a.reshape(chips, 2, own, a.shape[1])
-    tall = lambda a: pl.BlockSpec((per, 1, own, a.shape[1]), lambda i, parity: (i, parity[0], 0, 0))
-    block = pl.BlockSpec((per, own, 2 * width), lambda i, parity: (i, 0, 0))
-    more = [] if got is None else [got]
+    tall = lambda a: pl.BlockSpec((per, 1, own, a.shape[1]), lambda i, place: ((place[0] + i) % deep, place[2], 0, 0))
+    pair = pl.BlockSpec((2, per, own, width), lambda i, place: (0, i, 0, 0))
+    shape = lambda *lead: jax.ShapeDtypeStruct(lead + (own, width), BF16)
+    if got is None:
+        more, out_specs, out_shape = [], pair, shape(2, chips)
+    else:
+        more = [got]
+        out_specs = ([pl.BlockSpec((1, own, width), lambda i, place: (i, 0, 0))] * 2
+                     + [pl.BlockSpec((per, own, width), lambda i, place: (0, 0, 0))] * deep)
+        out_shape = [shape(deep)] * 2 + [shape(per)] * deep
     return pl.pallas_call(
         spread_kernel,
         grid_spec=pltpu.PrefetchScalarGridSpec(
             num_scalar_prefetch=1,
-            grid=(chips // per,),
+            grid=(deep,),
             in_specs=[tall(mixed), tall(wg), tall(act), whole(wj), whole(ww), whole(dense), whole(narrow)]
-            + [block] * len(more),
-            out_specs=block),
-        out_shape=jax.ShapeDtypeStruct((chips, own, 2 * width), BF16),
+            + [pair] * len(more),
+            out_specs=out_specs),
+        out_shape=out_shape,
         compiler_params=pltpu.CompilerParams(vmem_limit_bytes=VMEM),
         cost_estimate=pl.CostEstimate(flops=rows * width * 1024, bytes_accessed=9 << 20, transcendentals=0),
-    )(parity, split(mixed), split(wg), split(act), wj, ww, dense, narrow, *more)
+    )(place, split(mixed), split(wg), split(act), wj, ww, dense, narrow, *more)
 
 
 def finish_early_kernel(f_ref, all_ref, weight_ref, gain_ref, shift_ref,
@@ -443,25 +467,32 @@
     mixed = attention(order, joint, table, att_grad)
     core = (c % 2)[None]
     shares = (mixed, wg, act, wj_g, ww_g, dense_p, narrow_w)
-    other = spread(1 - core, *shares)
+    place = lambda parity: jnp.stack([c // 4, (c // 2) % 2, parity]).astype(jnp.int32)
+    other = spread(place(1 - c % 2), *shares)
     other, early = tie(other, early)
 
     early = jnp.sum(early.astype(F32), axis=0)
     bias_grad = early[d_own, ffc:ffc + d_own]
     early_all = lax.all_gather(early.astype(BF16), "ctx", axis=0)
-    late, other = tie(late_grads(xhat, both, mixed), lax.ppermute(other, "ctx", OTHER_CORE))
-    pair = spread(core, *shares, other)
-    late, pair = tie(lax.all_to_all(late, "fsdp", 0, 0, tiled=True), pair)
-    low = jnp.sum(late.astype(F32), axis=0).astype(BF16)
-
-    summed = lax.all_to_all(pair, "ctx", 0, 0, tiled=True, axis_index_groups=SAME_CORE)
+    late, other = tie(late_grads(xhat, both, mixed), move(other, OTHER_CORE))
+    near, far, *outs = spread(place(c % 2), *shares, other)
+
+    late, near, far, *outs = tie(lax.all_to_all(late, "fsdp", 0, 0, tiled=True), near, far, *outs)
+
+    wide = lambda v: v.astype(F32)
+    low = jnp.sum(wide(late), axis=0).astype(BF16)
+    low = jnp.concatenate([low[:, :3 * hd], turn(low[:, 3 * hd:])], axis=1)
+    late_mine, far, *outs[1:] = tie(
+        gather_chips(low), move(far, ACROSS_Y), *[move(outs[d], AHEAD_Z[d]) for d in range(1, 4)])
+    late_all = late_mine, move(late_mine, OTHER_CORE)
+    near = (wide(near) + wide(far)).astype(BF16)
+    out_own = sum(wide(v) for v in outs)
+    across = out_own[1].astype(BF16)
+    u_own = wide(near[0]) + sum(wide(move(near[d], AHEAD_Z[d])) for d in range(1, 4))
+    out_own = out_own[0] + wide(move(across, ACROSS_Y))
+
     widen_grad, narrow_grad, g2_grad, s2_grad, wb_shard = finish(
         finish_early_kernel, (f[None],), (early_all,), widen_weight, second_gain, second_shift, (2 * ffc, width))
-    low, summed, wb_shard = tie(
-        jnp.concatenate([low[:, :3 * hd], turn(low[:, 3 * hd:])], axis=1), summed, wb_shard)
-    late_all = gather_chips(low)
-    summed = jnp.sum(summed.astype(F32), axis=0)
-    u_own, out_own = summed[:, :width], summed[:, width:]
 
     own_x = own_tokens.astype(F32)
     block_out = (own_x + out_own + dense_b + narrow_b).astype(BF16)

time: 253 us -> 240 us (0.949)
  waiting for transfers between devices: 64.7 us -> 27.7 us
  starting transfers between devices: 48.1 us -> 68.8 us
    all_to_all x2 -> x1, waiting for transfers between devices: 27.5 us -> 0.01 us  [shards(): lax.all_to_all(late, 'fsdp', 0, 0, tiled=True)]
    all_to_all x1, starting transfers between devices: 5.48 us -> 23.7 us  [gather_chips(): lax.all_to_all(jnp.broadcast_to(own[None], (N_CTX // 2,) + own.shape), 'c...]
    all_gather x1, waiting for transfers between devices: 14.8 us -> 0.02 us  [shards(): early_all = lax.all_gather(early.astype(BF16), 'ctx', axis=0)]
    ppermute x2 -> x10, waiting for transfers between devices: 0.67 us -> 9.22 us  [move(): return lax.ppermute(v, 'ctx', way)]
    ppermute x2 -> x10, starting transfers between devices: 0.07 us -> 7.08 us  [move(): return lax.ppermute(v, 'ctx', way)]
    all_to_all x2 -> x1, starting transfers between devices: 13.5 us -> 7.21 us  [shards(): lax.all_to_all(late, 'fsdp', 0, 0, tiled=True)]
    all_to_all x1, waiting for transfers between devices: 8.14 us -> 4.8 us  [gather_chips(): lax.all_to_all(jnp.broadcast_to(own[None], (N_CTX // 2,) + own.shape), 'c...]
    reduce_sum x2 -> x1, other arithmetic: 3.08 us -> 0.08 us  [shards(): low = jnp.sum(wide(late), axis=0).astype(BF16)]
  transfers between devices with their start and end apart: 11 -> 18, of which waited for: 6 -> 5; matrix products, arithmetic and copies ran while one was open for 9% -> 10% of each run, Pallas kernels for 16% -> 18%
where the time goes in v2:
time: 240 us; the launch traced here: 239 us
  starting transfers between devices  68.8 us (29%)
  Pallas kernels  61.8 us (26%)
  blocking collectives  35.9 us (15%)
  waiting for transfers between devices  27.7 us (12%)
  local copies, waits for them, and re-layouts  15.4 us (6%)
  between operations  14.6 us (6%)
  other arithmetic  14.4 us (6%)
    all_gather x1, blocking collectives, shards(): lax.all_gather(rotary_place[0], 'ctx', axis=0, tiled=True).astype(F32)  35.9 us
    all_to_all x1, starting transfers between devices, gather_chips(): lax.all_to_all(jnp.broadcast_to(own[None], (N_CTX // 2,) + own.shape), 'c...  23.7 us
    pallas_call x2, Pallas kernels, spread(): pl.pallas_call(spread_kernel, grid_spec=pltpu.PrefetchScalarGridSpec(num_...  15.9 us
    pallas_call x1, Pallas kernels, attention(): pl.pallas_call(attention_kernel, out_shape=jax.ShapeDtypeStruct((rows, 4...  15.2 us
    pallas_call x1, Pallas kernels, project(): pl.pallas_call(project_kernel, grid=(slots // per,), in_specs=[pl.BlockSp...  14.6 us
    ppermute x2, starting transfers between devices, turn(): return lax.ppermute(v, ('ctx', 'fsdp'), TURN)  14.3 us
    all_gather x1, waiting for transfers between devices, shards(): lax.all_gather(jnp.concatenate([own_tokens, own_up], axis=0), 'ctx', axis=0)  13.6 us
    pallas_call x2, Pallas kernels, finish(): pl.pallas_call(kernel, in_specs=[pl.BlockSpec(memory_space=pltpu.SMEM)] *...  9.38 us
  transfers between devices with their start and end apart: 18, of which 5 were waited for; matrix products, arithmetic and copies ran while one was open for 10% of the time, Pallas kernels for 18%

profile of v2, /device:TPU:22, one launch (start us, length us, event | category | flops | bytes accessed | tf_op | source)
XLA Modules:
  0.0 238.7 jit_solution(1751019049835604287)
XLA Ops:
  7.3 1.9 pad_maximum_fusion.1
  9.3 0.4 copy.66
  9.8 0.1 copy.68
  10.1 0.1 copy.70
  10.2 0.1 copy.71
  10.4 0.1 copy.72
  10.7 0.2 reshape.118
  11.0 0.8 constant_dynamic-slice_fusion
  11.8 1.0 constant_dynamic-slice_fusion.2
  12.9 0.2 concatenate.27
  13.1 1.2 broadcast_in_dim.85
  14.4 7.3 %all-to-all-start = ((bf16[8,128,768]{2,1,0:T(8,128)(2,1)}), bf16[8,128,768]{2,1,0:T(8,128)(2,1)S(1)}, u32[]{:S(2)}, u32[]{:S(2)}) async-start(bf16[8,128,768]{2,1,0:T(8,128)(2,1)} %broadcast_in_dim.85), calls=%async_computation | async-start | bytes 3145728 | tf_op jit(solution)/shard_map/all_to_all | solution.py:434
  21.7 4.6 %collective-permute-start = (bf16[64,1024]{1,0:T(8,128)(2,1)S(1)}, bf16[64,1024]{1,0:T(8,128)(2,1)S(1)}, u32[]{:S(2)}, u32[]{:S(2)}) collective-permute-start(bf16[64,1024]{1,0:T(8,128)(2,1)S(1)} %constant_dynamic-slice_fusion.11), channel_id=1, source_target_pairs={{0,0},{1,16},{2,32},{3,48},{4,64},{5,80},{6,96},{7,112},{8,8},{9,2... | collective-permute-start | bytes 393224 | tf_op jit(solution)/shard_map/ppermute | solution.py:30
  26.3 35.9 %all-gather.1 = s32[1,2048]{1,0:T(1,128)S(1)} all-gather(s32[1,128]{1,0:T(1,128)S(1)} %copy-done.18), channel_id=3, replica_groups=mesh['ctx'=16,'fsdp'=8] {'ctx'}, dimensions={1}, use_global_device_ids=true | all-gather | bytes 8704 | tf_op jit(solution)/shard_map/all_gather | solution.py:436
  62.3 0.3 multiply_cosine_fusion
  62.7 0.9 pad.8.dense_ref
  63.7 0.2 slice.121
  63.9 0.2 slice.119
  64.1 0.2 reshape_reshape.3
  64.4 0.3 reshape.121
  64.8 1.6 slice_reduce_fusion.1
  66.4 1.7 multiply_reduce_fusion
  68.1 0.6 pad_maximum_fusion.6
  68.8 1.0 pad_maximum_fusion.back_ref
  69.8 13.6 %all-gather.6.cloned.1.call-done = bf16[4096,1024]{1,0:T(8,128)(2,1)} async-done(((bf16[256,1024]{1,0:T(8,128)(2,1)}), bf16[4096,1024]{1,0:T(8,128)(2,1)}) %all-gather.6.cloned.1.call-update) | async-done | bytes 8388624 | tf_op jit(solution)/shard_map/all_gather | solution.py:424
  83.4 14.6 %shard_map.263 = (bf16[2048,1024]{1,0:T(8,128)(2,1)}, f32[2048,256]{1,0:T(8,128)}, f32[2048,64]{1,0:T(8,128)}, bf16[2048,256]{1,0:T(8,128)(2,1)}, bf16[2048,256]...) custom-call(bf16[16,256,1024]{2,1,0:T(8,128)(2,1)} %bitcast.76, bf16[16,256,1024]{2,1,0:T(8,128)(2,1)} %bitcast.77, ...), custom_call_target="tpu_custom_call" | custom-call | flops 5637144576 | bytes 20971520 | tf_op jit(solution)/shard_map/pallas_call | solution.py:111
  98.0 9.1 %all-to-all-start.1 = ((bf16[8,144,512]{2,1,0:T(8,128)(2,1)}), bf16[8,144,512]{2,1,0:T(8,128)(2,1)S(1)}, u32[]{:S(2)}, u32[]{:S(2)}) async-start(bf16[8,144,512]{2,1,0:T(8,128)(2,1)} %get-tuple-element.63), calls=%async_computation.1 | async-start | bytes 2359296 | tf_op jit(solution)/shard_map/all_to_all | solution.py:465
  107.2 0.6 pad_add_fusion.1.place_ref
  107.8 1.4 copy.74.table_ref
  109.2 15.2 %shard_map.264.mixed_ref = bf16[2048,256]{1,0:T(8,128)(2,1)} custom-call(s32[16]{0:T(128)} %bitcast.103, f32[2048,256]{1,0:T(8,128)} %get-tuple-element.57.joint_ref, f32[2048,16]{1,0:T(8,128)} %copy.74.table_ref, f32[2048,64]{1,0:T(8,128)} %get-tuple-element.59.grad_ref), custom_call_target="tpu_custom_call" | custom-call | flops 1879048192 | bytes 8388608 | tf_op jit(solution)/shard_map/pallas_call | solution.py:380
  124.4 7.2 %shard_map.266 = bf16[2,8,128,1024]{3,2,1,0:T(8,128)(2,1)} custom-call(s32[3]{0:T(128)} %pad_add_fusion.1.place_ref, bf16[8,2,128,256]{3,2,1,0:T(8,128)(2,1)} %bitcast.74, bf16[8,2,128,256]{3,2,1,0:T(8,128)(2,1)} %bitcast.87, bf16[8,2,128,256]{3,2,1,0:T(8,128)(2,1)} %bitcast.85, bf16[1024,256]{1,0:T(8,128)(2,1)} %get-tuple-element.106.wj_ref, ...), custom_call_target="tpu_custom_call" | custom-call | flops 2147483648 | bytes 9437184 | tf_op jit(solution)/shard_map/pallas_call | solution.py:212
  131.6 0.2 convert_reduce_fusion
  131.8 0.7 convert_element_type.120
  132.5 6.7 %shard_map.265 = bf16[8,144,256]{2,1,0:T(8,128)(2,1)} custom-call(bf16[2048,1024]{1,0:T(8,128)(2,1)} %get-tuple-element.56.xhat_ref, bf16[16,256,1024]{2,1,0:T(8,128)(2,1)} %bitcast.78, bf16[2048,256]{1,0:T(8,128)(2,1)} %shard_map.264.mixed_ref), custom_call_target="tpu_custom_call" | custom-call | flops 1073741824 | bytes 10485760 | tf_op jit(solution)/shard_map/pallas_call | solution.py:154
  139.3 7.2 %all-to-all-start.2 = ((bf16[8,144,256]{2,1,0:T(8,128)(2,1)}), bf16[8,144,256]{2,1,0:T(8,128)(2,1)S(1)}, u32[]{:S(2)}, u32[]{:S(2)}) async-start(bf16[8,144,256]{2,1,0:T(8,128)(2,1)} %shard_map.265), calls=%async_computation.2 | async-start | bytes 1179648 | tf_op jit(solution)/shard_map/all_to_all | solution.py:480
  146.5 0.6 pad_add_fusion.3.place_ref
  147.1 8.7 %shard_map.267 = (bf16[4,128,1024]{2,1,0:T(8,128)(2,1)}, bf16[4,128,1024]{2,1,0:T(8,128)(2,1)}, bf16[2,128,1024]{2,1,0:T(8,128)(2,1)}, bf16[2,128,1024]{2,1,0:T(...) custom-call(s32[3]{0:T(128)} %pad_add_fusion.3.place_ref, bf16[8,2,128,256]{3,2,1,0:T(8,128)(2,1)} %bitcast.75, ...), custom_call_target="tpu_custom_call" | custom-call | flops 2147483648 | bytes 9437184 | tf_op jit(solution)/shard_map/pallas_call | solution.py:212
  156.2 9.7 %collective-permute-start.2 = (bf16[144,64]{1,0:T(8,128)(2,1)S(1)}, bf16[144,64]{1,0:T(8,128)(2,1)S(1)}, u32[]{:S(2)}, u32[]{:S(2)}) collective-permute-start(bf16[144,64]{1,0:T(8,128)(2,1)S(1)} %slice.127), channel_id=1, source_target_pairs={{0,0},{1,16},{2,32},{3,48},{4,64},{5,80},{6,96},{7,112},{8,8},{9,2... | collective-permute-start | bytes 55304 | tf_op jit(solution)/shard_map/ppermute | solution.py:30
  165.9 0.7 copy.75.gain_ref
  166.7 0.7 copy.76.shift_ref
  167.4 0.7 copy.77.gain_ref
  168.2 0.7 copy.78.shift_ref
  168.9 0.5 collective-permute-start.4
  169.4 2.8 %collective-permute-start.6 = (bf16[2,128,1024]{2,1,0:T(8,128)(2,1)}, bf16[2,128,1024]{2,1,0:T(8,128)(2,1)}, u32[]{:S(2)}, u32[]{:S(2)}) collective-permute-start(bf16[2,128,1024]{2,1,0:T(8,128)(2,1)} %get-tuple-element.78), channel_id=1, source_target_pairs={{0,96},{8,104},{16,112},{24,120},{32,0},{40,8},{48,16},{56,24},{64... | collective-permute-start | bytes 1572872 | tf_op jit(solution)/shard_map/ppermute | solution.py:34
  172.2 0.9 broadcast_in_dim.89
  173.1 23.7 %all-to-all-start.3 = ((bf16[8,144,256]{2,1,0:T(8,128)(2,1)}), bf16[8,144,256]{2,1,0:T(8,128)(2,1)S(1)}, u32[]{:S(2)}, u32[]{:S(2)}) async-start(bf16[8,144,256]{2,1,0:T(8,128)(2,1)} %broadcast_in_dim.89), calls=%async_computation.3 | async-start | bytes 1179648 | tf_op jit(solution)/shard_map/all_to_all | solution.py:38
  196.8 0.2 fusion.11
  197.1 5.5 %shard_map.269 = (f32[128,4096]{1,0:T(8,128)}, f32[512,1024]{1,0:T(8,128)}, f32[1,128]{1,0:T(1,128)}, f32[1,128]{1,0:T(1,128)}, f32[1,512]{1,0:T(1,128)}) custom-call(s32[1]{0:T(128)} %bitcast.31.f_ref, bf16[16,144,512]{2,1,0:T(8,128)(2,1)} %bitcast.89, bf16[128,4096]{1,0:T(8,128)(2,1)} %weight_ref.3, f32[128,1]{1,0:T(8,128)} %copy.77.gain_ref, ...), custom_call_target="tpu_custom_call" | custom-call | flops 4194304 | bytes 6291456 | tf_op jit(solution)/shard_map/pallas_call | solution.py:289
  202.7 4.8 %all-to-all-done.3.mine_ref = bf16[8,144,256]{2,1,0:T(8,128)(2,1)S(1)} async-done(((bf16[8,144,256]{2,1,0:T(8,128)(2,1)}), bf16[8,144,256]{2,1,0:T(8,128)(2,1)S(1)}, u32[]{:S(2)}, u32[]{:S(2)}) %all-to-all-start.3) | async-done | bytes 589856 | tf_op jit(solution)/shard_map/all_to_all | solution.py:38
  207.5 1.8 add_convert_fusion
  209.4 0.9 collective-permute-start.10
  210.3 1.2 collective-permute-start.9
  211.5 0.2 collective-permute-start.8
  211.7 1.5 convert_add_fusion
  213.3 1.3 collective-permute-start.7
  214.7 4.0 %collective-permute-done.10 = bf16[128,1024]{1,0:T(8,128)(2,1)S(1)} collective-permute-done((bf16[128,1024]{1,0:T(8,128)(2,1)S(1)}, bf16[128,1024]{1,0:T(8,128)(2,1)S(1)}, u32[]{:S(2)}, u32[]{:S(2)}) %collective-permute-start.10) | collective-permute-done | bytes 262176 | tf_op jit(solution)/shard_map/ppermute | solution.py:34
  218.7 2.4 collective-permute-done.9
  221.1 2.8 %collective-permute-done.8 = bf16[128,1024]{1,0:T(8,128)(2,1)S(1)} collective-permute-done((bf16[128,1024]{1,0:T(8,128)(2,1)S(1)}, bf16[128,1024]{1,0:T(8,128)(2,1)S(1)}, u32[]{:S(2)}, u32[]{:S(2)}) %collective-permute-start.8) | collective-permute-done | bytes 262176 | tf_op jit(solution)/shard_map/ppermute | solution.py:34
  223.9 0.3 fusion.19
  224.2 1.2 fusion.10
  225.4 0.8 copy-done.8
  226.2 3.8 %shard_map.268 = (f32[128,3072]{1,0:T(8,128)}, f32[128,1024]{1,0:T(8,128)}, f32[1,128]{1,0:T(1,128)}, f32[1,128]{1,0:T(1,128)}, f32[1,384]{1,0:T(1,128)}) custom-call(s32[1]{0:T(128)} %bitcast.31.f_ref, s32[1]{0:T(128)} %bitcast.22.core_ref, bf16[8,144,256]{2,1,0:T(8,128)(2,1)} %copy-done.5, bf16[8,144,256]{2,1,0:T(8,128)(2,1)} %copy-done.8, ...), custom_call_target="tpu_custom_call" | custom-call | flops 3145728 | bytes 4718592 | tf_op jit(solution)/shard_map/pallas_call | solution.py:289
  230.1 1.3 reduce.9
  231.3 0.5 copy.80
  (95 shorter events, 1.9 us)
Async XLA Ops:
  7.2 14.5 %copy-start = (bf16[128,1024]{1,0:T(8,128)(2,1)S(1)}, bf16[128,1024]{1,0:T(8,128)(2,1)}, u32[]{:S(2)}) copy-start(bf16[128,1024]{1,0:T(8,128)(2,1)} %param.24) | copy-start | bytes 786436
  7.2 2.1 copy-start.4
  7.2 2.6 %copy-start.14 = (bf16[128]{0:T(256)(128)(2,1)S(1)}, bf16[128]{0:T(256)(128)(2,1)}, u32[]{:S(2)}) copy-start(bf16[128]{0:T(256)(128)(2,1)} %param.20) | copy-start | bytes 772
  7.2 2.7 %copy-start.15 = (bf16[128]{0:T(256)(128)(2,1)S(1)}, bf16[128]{0:T(256)(128)(2,1)}, u32[]{:S(2)}) copy-start(bf16[128]{0:T(256)(128)(2,1)} %param.21) | copy-start | bytes 772
  7.2 2.9 %copy-start.16 = (bf16[128]{0:T(256)(128)(2,1)S(1)}, bf16[128]{0:T(256)(128)(2,1)}, u32[]{:S(2)}) copy-start(bf16[128]{0:T(256)(128)(2,1)} %param.26) | copy-start | bytes 772
  7.2 3.0 %copy-start.17 = (bf16[128]{0:T(256)(128)(2,1)S(1)}, bf16[128]{0:T(256)(128)(2,1)}, u32[]{:S(2)}) copy-start(bf16[128]{0:T(256)(128)(2,1)} %param.27) | copy-start | bytes 772
  7.3 3.1 %copy-start.12 = (bf16[128]{0:T(256)(128)(2,1)S(1)}, bf16[128]{0:T(256)(128)(2,1)}, u32[]{:S(2)}) copy-start(bf16[128]{0:T(256)(128)(2,1)} %param.25) | copy-start | bytes 772
  7.3 3.3 %copy-start.13 = (bf16[128]{0:T(256)(128)(2,1)S(1)}, bf16[128]{0:T(256)(128)(2,1)}, u32[]{:S(2)}) copy-start(bf16[128]{0:T(256)(128)(2,1)} %param.31) | copy-start | bytes 772
  7.3 3.4 %copy-start.10 = (bf16[384]{0:T(512)(128)(2,1)S(1)}, bf16[384]{0:T(512)(128)(2,1)}, u32[]{:S(2)}) copy-start(bf16[384]{0:T(512)(128)(2,1)} %param.23) | copy-start | bytes 2308
  7.3 3.6 %copy-start.11 = (bf16[512]{0:T(512)(128)(2,1)S(1)}, bf16[512]{0:T(512)(128)(2,1)}, u32[]{:S(2)}) copy-start(bf16[512]{0:T(512)(128)(2,1)} %param.29) | copy-start | bytes 3076
  7.3 76.1 %all-gather.6.cloned.1.call-start = ((), (), s32[]{:S(2)}) async-start(), calls=%async_computation.4 | async-start | bytes 8912896 | tf_op jit(solution)/shard_map/all_gather | solution.py:424
  14.4 12.0 %copy-start.18 = (s32[1,128]{1,0:T(1,128)S(1)}, s32[1,128]{1,0:T(1,128)}, u32[]{:S(2)}) copy-start(s32[1,128]{1,0:T(1,128)} %param.19) | copy-start | bytes 1540
  14.4 49.2 %all-to-all-start = ((bf16[8,128,768]{2,1,0:T(8,128)(2,1)}), bf16[8,128,768]{2,1,0:T(8,128)(2,1)S(1)}, u32[]{:S(2)}, u32[]{:S(2)}) async-start(bf16[8,128,768]{2,1,0:T(8,128)(2,1)} %broadcast_in_dim.85), calls=%async_computation | async-start | bytes 3145728 | tf_op jit(solution)/shard_map/all_to_all | solution.py:434
  21.7 40.9 %collective-permute-start = (bf16[64,1024]{1,0:T(8,128)(2,1)S(1)}, bf16[64,1024]{1,0:T(8,128)(2,1)S(1)}, u32[]{:S(2)}, u32[]{:S(2)}) collective-permute-start(bf16[64,1024]{1,0:T(8,128)(2,1)S(1)} %constant_dynamic-slice_fusion.11), channel_id=1, source_target_pairs={{0,0},{1,16},{2,32},{3,48},{4,64},{5,80},{6,96},{7,112},{8,8},{9,2... | collective-permute-start | bytes 393224 | tf_op jit(solution)/shard_map/ppermute | solution.py:30
  68.8 29.3 %copy-start.2 = (bf16[8,32,1024]{2,1,0:T(8,128)(2,1)}, bf16[8,32,1024]{2,1,0:T(8,128)(2,1)S(1)}, u32[]{:S(2)}) copy-start(bf16[8,32,1024]{2,1,0:T(8,128)(2,1)S(1)} %pad_maximum_fusion.2) | copy-start | bytes 1572868
  98.0 33.5 %all-to-all-start.1 = ((bf16[8,144,512]{2,1,0:T(8,128)(2,1)}), bf16[8,144,512]{2,1,0:T(8,128)(2,1)S(1)}, u32[]{:S(2)}, u32[]{:S(2)}) async-start(bf16[8,144,512]{2,1,0:T(8,128)(2,1)} %get-tuple-element.63), calls=%async_computation.1 | async-start | bytes 2359296 | tf_op jit(solution)/shard_map/all_to_all | solution.py:465
  107.2 89.9 %all-gather.8.cloned.1.call-start = ((), (), s32[]{:S(2)}) async-start(), calls=%async_computation.5 | async-start | bytes 2506752 | tf_op jit(solution)/shard_map/all_gather | solution.py:476
  131.6 7.7 %collective-permute-start.1 = (bf16[2,8,128,1024]{3,2,1,0:T(8,128)(2,1)}, bf16[2,8,128,1024]{3,2,1,0:T(8,128)(2,1)}, u32[]{:S(2)}, u32[]{:S(2)}) collective-permute-start(bf16[2,8,128,1024]{3,2,1,0:T(8,128)(2,1)} %shard_map.266), channel_id=1, source_target_pairs={{8,0},{0,8},{24,16},{16,24},{40,32},{32,40},{56,48},{48,56},{72,64... | collective-permute-start | bytes 12582920 | tf_op jit(solution)/shard_map/ppermute | solution.py:34
  139.3 16.5 %all-to-all-start.2 = ((bf16[8,144,256]{2,1,0:T(8,128)(2,1)}), bf16[8,144,256]{2,1,0:T(8,128)(2,1)S(1)}, u32[]{:S(2)}, u32[]{:S(2)}) async-start(bf16[8,144,256]{2,1,0:T(8,128)(2,1)} %shard_map.265), calls=%async_computation.2 | async-start | bytes 1179648 | tf_op jit(solution)/shard_map/all_to_all | solution.py:480
  147.1 8.8 %copy-start.3 = (bf16[1,128,1024]{2,1,0:T(8,128)(2,1)S(1)}, bf16[1,128,1024]{2,1,0:T(8,128)(2,1)}, u32[]{:S(2)}) copy-start(bf16[1,128,1024]{2,1,0:T(8,128)(2,1)} %param.16) | copy-start | bytes 786436
  155.8 51.7 %collective-permute-start.3 = (bf16[4,128,1024]{2,1,0:T(8,128)(2,1)}, bf16[4,128,1024]{2,1,0:T(8,128)(2,1)}, u32[]{:S(2)}, u32[]{:S(2)}) collective-permute-start(bf16[4,128,1024]{2,1,0:T(8,128)(2,1)} %get-tuple-element.75), channel_id=1, source_target_pairs={{16,0},{24,8},{0,16},{8,24},{48,32},{56,40},{32,48},{40,56},{80,64... | collective-permute-start | bytes 3145736 | tf_op jit(solution)/shard_map/ppermute | solution.py:34
  156.2 15.9 %collective-permute-start.2 = (bf16[144,64]{1,0:T(8,128)(2,1)S(1)}, bf16[144,64]{1,0:T(8,128)(2,1)S(1)}, u32[]{:S(2)}, u32[]{:S(2)}) collective-permute-start(bf16[144,64]{1,0:T(8,128)(2,1)S(1)} %slice.127), channel_id=1, source_target_pairs={{0,0},{1,16},{2,32},{3,48},{4,64},{5,80},{6,96},{7,112},{8,8},{9,2... | collective-permute-start | bytes 55304 | tf_op jit(solution)/shard_map/ppermute | solution.py:30
  168.9 33.8 %collective-permute-start.4 = (bf16[2,128,1024]{2,1,0:T(8,128)(2,1)}, bf16[2,128,1024]{2,1,0:T(8,128)(2,1)S(1)}, u32[]{:S(2)}, u32[]{:S(2)}) collective-permute-start(bf16[2,128,1024]{2,1,0:T(8,128)(2,1)} %get-tuple-element.76), channel_id=1, source_target_pairs={{0,32},{8,40},{16,48},{24,56},{32,64},{40,72},{48,80},{56,88},{64,... | collective-permute-start | bytes 1572872 | tf_op jit(solution)/shard_map/ppermute | solution.py:34
  169.4 33.3 %collective-permute-start.5 = (bf16[2,128,1024]{2,1,0:T(8,128)(2,1)}, bf16[2,128,1024]{2,1,0:T(8,128)(2,1)}, u32[]{:S(2)}, u32[]{:S(2)}) collective-permute-start(bf16[2,128,1024]{2,1,0:T(8,128)(2,1)} %get-tuple-element.77), channel_id=1, source_target_pairs={{0,64},{8,72},{16,80},{24,88},{32,96},{40,104},{48,112},{56,120},{... | collective-permute-start | bytes 1572872 | tf_op jit(solution)/shard_map/ppermute | solution.py:34
  169.4 33.3 %collective-permute-start.6 = (bf16[2,128,1024]{2,1,0:T(8,128)(2,1)}, bf16[2,128,1024]{2,1,0:T(8,128)(2,1)}, u32[]{:S(2)}, u32[]{:S(2)}) collective-permute-start(bf16[2,128,1024]{2,1,0:T(8,128)(2,1)} %get-tuple-element.78), channel_id=1, source_target_pairs={{0,96},{8,104},{16,112},{24,120},{32,0},{40,8},{48,16},{56,24},{64... | collective-permute-start | bytes 1572872 | tf_op jit(solution)/shard_map/ppermute | solution.py:34
  173.1 34.4 %all-to-all-start.3 = ((bf16[8,144,256]{2,1,0:T(8,128)(2,1)}), bf16[8,144,256]{2,1,0:T(8,128)(2,1)S(1)}, u32[]{:S(2)}, u32[]{:S(2)}) async-start(bf16[8,144,256]{2,1,0:T(8,128)(2,1)} %broadcast_in_dim.89), calls=%async_computation.3 | async-start | bytes 1179648 | tf_op jit(solution)/shard_map/all_to_all | solution.py:38
  196.8 10.7 %copy-start.6 = (bf16[4,128,1024]{2,1,0:T(8,128)(2,1)S(1)}, bf16[4,128,1024]{2,1,0:T(8,128)(2,1)}, u32[]{:S(2)}) copy-start(bf16[4,128,1024]{2,1,0:T(8,128)(2,1)} %get-tuple-element.82) | copy-start | bytes 3145732
  197.1 34.3 %copy-start.19 = (f32[128]{0:T(128)}, f32[128]{0:T(128)S(1)}, u32[]{:S(2)}) copy-start(f32[128]{0:T(128)S(1)} %slice_bitcast_fusion.5) | copy-start | bytes 1540
  202.7 9.1 %copy-start.9 = (bf16[2,128,1024]{2,1,0:T(8,128)(2,1)S(1)}, bf16[2,128,1024]{2,1,0:T(8,128)(2,1)}, u32[]{:S(2)}) copy-start(bf16[2,128,1024]{2,1,0:T(8,128)(2,1)} %get-tuple-element.73) | copy-start | bytes 1572868
  207.5 7.2 %copy-start.5 = (bf16[8,144,256]{2,1,0:T(8,128)(2,1)}, bf16[8,144,256]{2,1,0:T(8,128)(2,1)S(1)}, u32[]{:S(2)}) copy-start(bf16[8,144,256]{2,1,0:T(8,128)(2,1)S(1)} %all-to-all-done.3.mine_ref) | copy-start | bytes 1769476
  209.4 9.3 %collective-permute-start.10 = (bf16[128,1024]{1,0:T(8,128)(2,1)S(1)}, bf16[128,1024]{1,0:T(8,128)(2,1)S(1)}, u32[]{:S(2)}, u32[]{:S(2)}) collective-permute-start(bf16[128,1024]{1,0:T(8,128)(2,1)S(1)} %get-tuple-element.113), channel_id=1, source_target_pairs={{0,96},{8,104},{16,112},{24,120},{32,0},{40,8},{48,16},{56,24},{64... | collective-permute-start | bytes 786440 | tf_op jit(solution)/shard_map/ppermute | solution.py:34
  210.3 10.7 %collective-permute-start.9 = (bf16[128,1024]{1,0:T(8,128)(2,1)S(1)}, bf16[128,1024]{1,0:T(8,128)(2,1)S(1)}, u32[]{:S(2)}, u32[]{:S(2)}) collective-permute-start(bf16[128,1024]{1,0:T(8,128)(2,1)S(1)} %get-tuple-element.114), channel_id=1, source_target_pairs={{0,64},{8,72},{16,80},{24,88},{32,96},{40,104},{48,112},{56,120},{... | collective-permute-start | bytes 786440 | tf_op jit(solution)/shard_map/ppermute | solution.py:34
  211.5 12.7 %copy-start.7 = (bf16[1,128,1024]{2,1,0:T(8,128)(2,1)S(1)}, bf16[1,128,1024]{2,1,0:T(8,128)(2,1)}, u32[]{:S(2)}) copy-start(bf16[1,128,1024]{2,1,0:T(8,128)(2,1)} %param.17) | copy-start | bytes 786436
  211.5 12.4 %collective-permute-start.8 = (bf16[128,1024]{1,0:T(8,128)(2,1)S(1)}, bf16[128,1024]{1,0:T(8,128)(2,1)S(1)}, u32[]{:S(2)}, u32[]{:S(2)}) collective-permute-start(bf16[128,1024]{1,0:T(8,128)(2,1)S(1)} %get-tuple-element.112), channel_id=1, source_target_pairs={{0,32},{8,40},{16,48},{24,56},{32,64},{40,72},{48,80},{56,88},{64,... | collective-permute-start | bytes 786440 | tf_op jit(solution)/shard_map/ppermute | solution.py:34
  213.3 10.9 %collective-permute-start.7 = (bf16[128,1024]{1,0:T(8,128)(2,1)S(1)}, bf16[128,1024]{1,0:T(8,128)(2,1)S(1)}, u32[]{:S(2)}, u32[]{:S(2)}) collective-permute-start(bf16[128,1024]{1,0:T(8,128)(2,1)S(1)} %fusion.16), channel_id=1, source_target_pairs={{16,0},{24,8},{0,16},{8,24},{48,32},{56,40},{32,48},{40,56},{80,64... | collective-permute-start | bytes 786440 | tf_op jit(solution)/shard_map/ppermute | solution.py:34
  214.7 10.8 %collective-permute-start.11 = (bf16[8,144,256]{2,1,0:T(8,128)(2,1)S(1)}, bf16[8,144,256]{2,1,0:T(8,128)(2,1)S(1)}, u32[]{:S(2)}, u32[]{:S(2)}) collective-permute-start(bf16[8,144,256]{2,1,0:T(8,128)(2,1)S(1)} %all-to-all-done.3.mine_ref), channel_id=1, source_target_pairs={{8,0},{0,8},{24,16},{16,24},{40,32},{32,40},{56,48},{48,56},{72,64... | collective-permute-start | bytes 1769480 | tf_op jit(solution)/shard_map/ppermute | solution.py:34
  224.2 7.7 %copy-start.1 = (bf16[128,1024]{1,0:T(8,128)(2,1)S(1)}, bf16[128,1024]{1,0:T(8,128)(2,1)}, u32[]{:S(2)}) copy-start(bf16[128,1024]{1,0:T(8,128)(2,1)} %param.24) | copy-start | bytes 786436
  225.4 0.8 copy-start.8
Sparse Core Ops, SparseCore 0:
  10.4 72.9 all-gather.5
  132.6 43.3 all-gather.7

commit v3 on v2

--- a/solution.py
+++ b/solution.py
@@ -311,7 +311,7 @@
             src = pl.ds(j * 2 * half + h * half, half)
             dst = pl.ds(pl.multiple_of((p if h == 0 else last - p) * half, half), half)
             joint_s[dst, :] = joint_ref[src, :]
-            table_s[dst, :] = table_ref[src, :]
+            table_s[dst, :] = table_ref[src, 0:16]
             grad_s[dst, :] = grad_ref[src, :]
     scale = hd ** -0.5
 
@@ -439,9 +439,9 @@
     slices = slices.reshape(width, part.shape[1])
     back_w = jnp.concatenate([dense_w, narrow_w], axis=0)
 
-    steps = jnp.arange(8, dtype=F32)
-    angles = place_all[:, None] * (ROTARY_BASE ** (-2.0 * steps / 16))
-    table = jnp.concatenate([jnp.cos(angles), jnp.sin(angles)], axis=1)
+    lane = jnp.arange(128)[None, :]
+    angles = place_all[:, None] * (ROTARY_BASE ** (-2.0 * (lane % 8).astype(F32) / 16))
+    table = jnp.where(lane < 8, jnp.cos(angles), jnp.sin(angles))
     order = block_pairs[0]
 
     wj = slices[:, :4 * hd].astype(F32)
@@ -488,12 +488,16 @@
     near = (wide(near) + wide(far)).astype(BF16)
     out_own = sum(wide(v) for v in outs)
     across = out_own[1].astype(BF16)
-    u_own = wide(near[0]) + sum(wide(move(near[d], AHEAD_Z[d])) for d in range(1, 4))
-    out_own = out_own[0] + wide(move(across, ACROSS_Y))
-
     widen_grad, narrow_grad, g2_grad, s2_grad, wb_shard = finish(
         finish_early_kernel, (f[None],), (early_all,), widen_weight, second_gain, second_shift, (2 * ffc, width))
 
+    joint_grad, dense_grad, g1_grad, s1_grad, jb_shard = finish(
+        finish_late_kernel, (f[None], core), late_all, joint_weight, first_gain, first_shift, (2 * hd, width))
+
+    moved = [move(near[d], AHEAD_Z[d]) for d in range(1, 4)]
+    across, wb_shard, jb_shard, *moved = tie(move(across, ACROSS_Y), wb_shard, jb_shard, *moved)
+    u_own = wide(near[0]) + sum(wide(v) for v in moved)
+    out_own = out_own[0] + wide(across)
     own_x = own_tokens.astype(F32)
     block_out = (own_x + out_own + dense_b + narrow_b).astype(BF16)
     own_center = own_x - jnp.mean(own_x, axis=-1, keepdims=True)
@@ -503,8 +507,6 @@
         u_own - jnp.mean(u_own, axis=-1, keepdims=True)
         - own_xhat * jnp.mean(u_own * own_xhat, axis=-1, keepdims=True))
 
-    joint_grad, dense_grad, g1_grad, s1_grad, jb_shard = finish(
-        finish_late_kernel, (f[None], core), late_all, joint_weight, first_gain, first_shift, (2 * hd, width))
     return (
         block_out[None], tokens_grad[None], g1_grad, s1_grad, joint_grad, jb_shard,
         dense_grad, bias_grad, g2_grad, s2_grad, widen_grad, wb_shard, narrow_grad, bias_grad,

time: 240 us -> 241 us (level)
  waiting for transfers between devices: 27.7 us -> 19.6 us
  other arithmetic: 14.4 us -> 21.7 us
  starting transfers between devices: 68.8 us -> 72.1 us
    ppermute x10, waiting for transfers between devices: 9.22 us -> 0.03 us  [move(): return lax.ppermute(v, 'ctx', way)]
    all_to_all x1, waiting for transfers between devices: 4.8 us -> 10.4 us  [gather_chips(): lax.all_to_all(jnp.broadcast_to(own[None], (N_CTX // 2,) + own.shape), 'c...]
    select_n x0 -> x1, other arithmetic: none -> 4.99 us  [shards(): table = jnp.where(lane < 8, jnp.cos(angles), jnp.sin(angles))]
    all_gather x1, waiting for transfers between devices: 13.6 us -> 9.16 us  [shards(): lax.all_gather(jnp.concatenate([own_tokens, own_up], axis=0), 'ctx', axis=0)]
    all_to_all x1, starting transfers between devices: 23.7 us -> 26.6 us  [gather_chips(): lax.all_to_all(jnp.broadcast_to(own[None], (N_CTX // 2,) + own.shape), 'c...]
  transfers between devices with their start and end apart: 18 -> 18, of which waited for: 5 -> 2; matrix products, arithmetic and copies ran while one was open for 10% -> 12% of each run, Pallas kernels for 18% -> 20%
where the time goes in v3:
time: 241 us; the launch traced here: 240 us
  starting transfers between devices  72.1 us (30%)
  Pallas kernels  61.9 us (26%)
  blocking collectives  35.9 us (15%)
  other arithmetic  21.7 us (9%)
  waiting for transfers between devices  19.6 us (8%)
  between operations  14.6 us (6%)
  local copies, waits for them, and re-layouts  14 us (6%)
    all_gather x1, blocking collectives, shards(): lax.all_gather(rotary_place[0], 'ctx', axis=0, tiled=True).astype(F32)  35.9 us
    all_to_all x1, starting transfers between devices, gather_chips(): lax.all_to_all(jnp.broadcast_to(own[None], (N_CTX // 2,) + own.shape), 'c...  26.6 us
    pallas_call x2, Pallas kernels, spread(): pl.pallas_call(spread_kernel, grid_spec=pltpu.PrefetchScalarGridSpec(num_...  15.9 us
    pallas_call x1, Pallas kernels, attention(): pl.pallas_call(attention_kernel, out_shape=jax.ShapeDtypeStruct((rows, 4...  15.2 us
    pallas_call x1, Pallas kernels, project(): pl.pallas_call(project_kernel, grid=(slots // per,), in_specs=[pl.BlockSp...  14.6 us
    ppermute x2, starting transfers between devices, turn(): return lax.ppermute(v, ('ctx', 'fsdp'), TURN)  14.3 us
    all_to_all x1, waiting for transfers between devices, gather_chips(): lax.all_to_all(jnp.broadcast_to(own[None], (N_CTX // 2,) + own.shape), 'c...  10.4 us
    pallas_call x2, Pallas kernels, finish(): pl.pallas_call(kernel, in_specs=[pl.BlockSpec(memory_space=pltpu.SMEM)] *...  9.39 us
  transfers between devices with their start and end apart: 18, of which 2 were waited for; matrix products, arithmetic and copies ran while one was open for 12% of the time, Pallas kernels for 20%

profile of v3, /device:TPU:22, one launch (start us, length us, event | category | flops | bytes accessed | tf_op | source)
XLA Modules:
  0.0 239.8 jit_solution(12669550882818710206)
XLA Ops:
  7.3 1.9 pad_maximum_fusion.1
  9.3 0.4 copy.53
  9.8 0.1 copy.55
  10.0 0.1 copy.56
  10.1 0.1 copy.57
  10.2 0.1 copy.58
  10.4 0.1 copy.59
  10.5 0.1 copy.60
  10.7 0.2 reshape.140
  10.9 0.1 reshape.141
  11.0 0.8 constant_dynamic-slice_fusion
  11.8 1.0 constant_dynamic-slice_fusion.2
  12.9 0.2 concatenate.23
  13.1 1.2 broadcast_in_dim.94
  14.4 7.3 %all-to-all-start = ((bf16[8,128,768]{2,1,0:T(8,128)(2,1)}), bf16[8,128,768]{2,1,0:T(8,128)(2,1)S(1)}, u32[]{:S(2)}, u32[]{:S(2)}) async-start(bf16[8,128,768]{2,1,0:T(8,128)(2,1)} %broadcast_in_dim.94), calls=%async_computation | async-start | bytes 3145728 | tf_op jit(solution)/shard_map/all_to_all | solution.py:434
  21.7 4.6 %collective-permute-start = (bf16[64,1024]{1,0:T(8,128)(2,1)S(1)}, bf16[64,1024]{1,0:T(8,128)(2,1)S(1)}, u32[]{:S(2)}, u32[]{:S(2)}) collective-permute-start(bf16[64,1024]{1,0:T(8,128)(2,1)S(1)} %constant_dynamic-slice_fusion.11), channel_id=1, source_target_pairs={{0,0},{1,16},{2,32},{3,48},{4,64},{5,80},{6,96},{7,112},{8,8},{9,2... | collective-permute-start | bytes 393224 | tf_op jit(solution)/shard_map/ppermute | solution.py:30
  26.3 35.9 %all-gather.1 = s32[1,2048]{1,0:T(1,128)S(1)} all-gather(s32[1,128]{1,0:T(1,128)S(1)} %copy-done.18), channel_id=3, replica_groups=mesh['ctx'=16,'fsdp'=8] {'ctx'}, dimensions={1}, use_global_device_ids=true | all-gather | bytes 8704 | tf_op jit(solution)/shard_map/all_gather | solution.py:436
  62.3 5.0 %fusion.2.table_ref = f32[2048,128]{1,0:T(8,128)} fusion(f32[128]{0:T(128)S(1)} %fusion.22, f32[2048]{0:T(1024)S(1)} %bitcast.94, pred[128]{0:T(512)(128)(4,1)S(1)} %iota_compare_fusion.1), kind=kLoop, calls=%fused_computation.8 | loop fusion | flops 524288 | bytes 1057408 | tf_op jit(solution)/shard_map/jit(_where)/select_n | solution.py:444
  67.3 0.9 pad.8.dense_ref
  68.2 0.1 slice_convert_fusion.1
  68.3 0.2 slice.121
  68.5 0.2 slice.119
  68.7 0.2 reshape_reshape.3
  69.0 0.3 reshape.143
  69.5 1.6 slice_reduce_fusion.1
  71.1 1.7 multiply_reduce_fusion
  72.8 0.6 pad_maximum_fusion.5
  73.5 0.9 pad_maximum_fusion.back_ref
  74.4 9.2 %all-gather.6.cloned.1.call-done = bf16[4096,1024]{1,0:T(8,128)(2,1)} async-done(((bf16[256,1024]{1,0:T(8,128)(2,1)}), bf16[4096,1024]{1,0:T(8,128)(2,1)}) %all-gather.6.cloned.1.call-update) | async-done | bytes 8388624 | tf_op jit(solution)/shard_map/all_gather | solution.py:424
  83.5 14.6 %shard_map.263 = (bf16[2048,1024]{1,0:T(8,128)(2,1)}, f32[2048,256]{1,0:T(8,128)}, f32[2048,64]{1,0:T(8,128)}, bf16[2048,256]{1,0:T(8,128)(2,1)}, bf16[2048,256]...) custom-call(bf16[16,256,1024]{2,1,0:T(8,128)(2,1)} %bitcast.76, bf16[16,256,1024]{2,1,0:T(8,128)(2,1)} %bitcast.77, ...), custom_call_target="tpu_custom_call" | custom-call | flops 5637144576 | bytes 20971520 | tf_op jit(solution)/shard_map/pallas_call | solution.py:111
  98.2 9.0 %all-to-all-start.1 = ((bf16[8,144,512]{2,1,0:T(8,128)(2,1)}), bf16[8,144,512]{2,1,0:T(8,128)(2,1)S(1)}, u32[]{:S(2)}, u32[]{:S(2)}) async-start(bf16[8,144,512]{2,1,0:T(8,128)(2,1)} %get-tuple-element.69), calls=%async_computation.1 | async-start | bytes 2359296 | tf_op jit(solution)/shard_map/all_to_all | solution.py:465
  107.2 0.6 pad_add_fusion.1.place_ref
  107.8 15.2 %shard_map.264.mixed_ref = bf16[2048,256]{1,0:T(8,128)(2,1)} custom-call(s32[16]{0:T(128)} %bitcast.103, f32[2048,256]{1,0:T(8,128)} %get-tuple-element.63.joint_ref, f32[2048,128]{1,0:T(8,128)} %fusion.2.table_ref, f32[2048,64]{1,0:T(8,128)} %get-tuple-element.65.grad_ref), custom_call_target="tpu_custom_call" | custom-call | flops 1879048192 | bytes 8388608 | tf_op jit(solution)/shard_map/pallas_call | solution.py:380
  123.0 7.2 %shard_map.266 = bf16[2,8,128,1024]{3,2,1,0:T(8,128)(2,1)} custom-call(s32[3]{0:T(128)} %pad_add_fusion.1.place_ref, bf16[8,2,128,256]{3,2,1,0:T(8,128)(2,1)} %bitcast.74, bf16[8,2,128,256]{3,2,1,0:T(8,128)(2,1)} %bitcast.87, bf16[8,2,128,256]{3,2,1,0:T(8,128)(2,1)} %bitcast.85, bf16[1024,256]{1,0:T(8,128)(2,1)} %get-tuple-element.118.wj_ref, ...), custom_call_target="tpu_custom_call" | custom-call | flops 2147483648 | bytes 9437184 | tf_op jit(solution)/shard_map/pallas_call | solution.py:212
  130.2 0.2 convert_reduce_fusion
  130.4 0.7 convert_element_type.118
  131.1 6.7 %shard_map.265 = bf16[8,144,256]{2,1,0:T(8,128)(2,1)} custom-call(bf16[2048,1024]{1,0:T(8,128)(2,1)} %get-tuple-element.62.xhat_ref, bf16[16,256,1024]{2,1,0:T(8,128)(2,1)} %bitcast.78, bf16[2048,256]{1,0:T(8,128)(2,1)} %shard_map.264.mixed_ref), custom_call_target="tpu_custom_call" | custom-call | flops 1073741824 | bytes 10485760 | tf_op jit(solution)/shard_map/pallas_call | solution.py:154
  137.8 7.2 %all-to-all-start.2 = ((bf16[8,144,256]{2,1,0:T(8,128)(2,1)}), bf16[8,144,256]{2,1,0:T(8,128)(2,1)S(1)}, u32[]{:S(2)}, u32[]{:S(2)}) async-start(bf16[8,144,256]{2,1,0:T(8,128)(2,1)} %shard_map.265), calls=%async_computation.2 | async-start | bytes 1179648 | tf_op jit(solution)/shard_map/all_to_all | solution.py:480
  145.0 0.6 pad_add_fusion.3.place_ref
  145.6 8.7 %shard_map.267 = (bf16[4,128,1024]{2,1,0:T(8,128)(2,1)}, bf16[4,128,1024]{2,1,0:T(8,128)(2,1)}, bf16[2,128,1024]{2,1,0:T(8,128)(2,1)}, bf16[2,128,1024]{2,1,0:T(...) custom-call(s32[3]{0:T(128)} %pad_add_fusion.3.place_ref, bf16[8,2,128,256]{3,2,1,0:T(8,128)(2,1)} %bitcast.75, ...), custom_call_target="tpu_custom_call" | custom-call | flops 2147483648 | bytes 9437184 | tf_op jit(solution)/shard_map/pallas_call | solution.py:212
  154.8 9.7 %collective-permute-start.2 = (bf16[144,64]{1,0:T(8,128)(2,1)S(1)}, bf16[144,64]{1,0:T(8,128)(2,1)S(1)}, u32[]{:S(2)}, u32[]{:S(2)}) collective-permute-start(bf16[144,64]{1,0:T(8,128)(2,1)S(1)} %slice.127), channel_id=1, source_target_pairs={{0,0},{1,16},{2,32},{3,48},{4,64},{5,80},{6,96},{7,112},{8,8},{9,2... | collective-permute-start | bytes 55304 | tf_op jit(solution)/shard_map/ppermute | solution.py:30
  164.5 0.5 collective-permute-start.4
  165.0 2.8 %collective-permute-start.6 = (bf16[2,128,1024]{2,1,0:T(8,128)(2,1)}, bf16[2,128,1024]{2,1,0:T(8,128)(2,1)S(1)}, u32[]{:S(2)}, u32[]{:S(2)}) collective-permute-start(bf16[2,128,1024]{2,1,0:T(8,128)(2,1)} %get-tuple-element.84), channel_id=1, source_target_pairs={{0,96},{8,104},{16,112},{24,120},{32,0},{40,8},{48,16},{56,24},{64... | collective-permute-start | bytes 1572872 | tf_op jit(solution)/shard_map/ppermute | solution.py:34
  167.9 0.9 broadcast_in_dim.98
  168.8 26.6 %all-to-all-start.3 = ((bf16[8,144,256]{2,1,0:T(8,128)(2,1)}), bf16[8,144,256]{2,1,0:T(8,128)(2,1)S(1)}, u32[]{:S(2)}, u32[]{:S(2)}) async-start(bf16[8,144,256]{2,1,0:T(8,128)(2,1)} %broadcast_in_dim.98), calls=%async_computation.3 | async-start | bytes 1179648 | tf_op jit(solution)/shard_map/all_to_all | solution.py:38
  195.4 0.2 fusion.12
  195.7 10.4 %all-to-all-done.3.mine_ref = bf16[8,144,256]{2,1,0:T(8,128)(2,1)S(1)} async-done(((bf16[8,144,256]{2,1,0:T(8,128)(2,1)}), bf16[8,144,256]{2,1,0:T(8,128)(2,1)S(1)}, u32[]{:S(2)}, u32[]{:S(2)}) %all-to-all-start.3) | async-done | bytes 589856 | tf_op jit(solution)/shard_map/all_to_all | solution.py:38
  206.1 1.7 convert_add_fusion
  207.9 0.9 collective-permute-start.7
  208.8 2.0 add_convert_fusion
  210.8 0.9 slice_bitcast_fusion.2
  211.7 0.6 collective-permute-start.9
  212.3 2.1 collective-permute-start.10
  214.3 0.6 collective-permute-start.11
  215.0 0.7 copy.61.gain_ref
  215.7 0.7 copy.62.shift_ref
  216.4 0.7 copy.63.gain_ref
  217.2 0.7 copy.64.shift_ref
  217.9 5.5 %shard_map.268 = (f32[128,4096]{1,0:T(8,128)}, f32[512,1024]{1,0:T(8,128)}, f32[1,128]{1,0:T(1,128)}, f32[1,128]{1,0:T(1,128)}, f32[1,512]{1,0:T(1,128)}) custom-call(s32[1]{0:T(128)} %bitcast.25.f_ref, bf16[16,144,512]{2,1,0:T(8,128)(2,1)} %bitcast.89, bf16[128,4096]{1,0:T(8,128)(2,1)} %weight_ref.2, f32[128,1]{1,0:T(8,128)} %copy.61.gain_ref, ...), custom_call_target="tpu_custom_call" | custom-call | flops 4194304 | bytes 6291456 | tf_op jit(solution)/shard_map/pallas_call | solution.py:289
  223.4 3.9 %shard_map.269 = (f32[128,3072]{1,0:T(8,128)}, f32[128,1024]{1,0:T(8,128)}, f32[1,128]{1,0:T(1,128)}, f32[1,128]{1,0:T(1,128)}, f32[1,384]{1,0:T(1,128)}) custom-call(s32[1]{0:T(128)} %bitcast.25.f_ref, s32[1]{0:T(128)} %bitcast.22.core_ref, bf16[8,144,256]{2,1,0:T(8,128)(2,1)} %copy-done.5, bf16[8,144,256]{2,1,0:T(8,128)(2,1)} %collective-permute-done.8.other_ref, ...), custom_call_target="tpu_custom_call" | custom-call | flops 3145728 | bytes 4718592 | tf_op jit(solution)/shard_map/pallas_call | solution.py:289
  227.3 1.3 reduce.7
  228.6 1.5 fusion.23
  230.1 2.4 fusion.11
  232.5 0.5 copy.66
  (94 shorter events, 1.3 us)
Async XLA Ops:
  7.2 14.5 %copy-start = (bf16[128,1024]{1,0:T(8,128)(2,1)S(1)}, bf16[128,1024]{1,0:T(8,128)(2,1)}, u32[]{:S(2)}) copy-start(bf16[128,1024]{1,0:T(8,128)(2,1)} %param.24) | copy-start | bytes 786436
  7.2 2.1 copy-start.4
  7.2 2.6 %copy-start.16 = (bf16[128]{0:T(256)(128)(2,1)S(1)}, bf16[128]{0:T(256)(128)(2,1)}, u32[]{:S(2)}) copy-start(bf16[128]{0:T(256)(128)(2,1)} %param.20) | copy-start | bytes 772
  7.2 2.7 %copy-start.17 = (bf16[128]{0:T(256)(128)(2,1)S(1)}, bf16[128]{0:T(256)(128)(2,1)}, u32[]{:S(2)}) copy-start(bf16[128]{0:T(256)(128)(2,1)} %param.21) | copy-start | bytes 772
  7.2 2.9 %copy-start.14 = (bf16[128]{0:T(256)(128)(2,1)S(1)}, bf16[128]{0:T(256)(128)(2,1)}, u32[]{:S(2)}) copy-start(bf16[128]{0:T(256)(128)(2,1)} %param.26) | copy-start | bytes 772
  7.2 3.0 %copy-start.15 = (bf16[128]{0:T(256)(128)(2,1)S(1)}, bf16[128]{0:T(256)(128)(2,1)}, u32[]{:S(2)}) copy-start(bf16[128]{0:T(256)(128)(2,1)} %param.27) | copy-start | bytes 772
  7.3 3.1 %copy-start.12 = (bf16[128]{0:T(256)(128)(2,1)S(1)}, bf16[128]{0:T(256)(128)(2,1)}, u32[]{:S(2)}) copy-start(bf16[128]{0:T(256)(128)(2,1)} %param.25) | copy-start | bytes 772
  7.3 3.3 %copy-start.13 = (bf16[128]{0:T(256)(128)(2,1)S(1)}, bf16[128]{0:T(256)(128)(2,1)}, u32[]{:S(2)}) copy-start(bf16[128]{0:T(256)(128)(2,1)} %param.31) | copy-start | bytes 772
  7.3 3.4 %copy-start.10 = (bf16[384]{0:T(512)(128)(2,1)S(1)}, bf16[384]{0:T(512)(128)(2,1)}, u32[]{:S(2)}) copy-start(bf16[384]{0:T(512)(128)(2,1)} %param.23) | copy-start | bytes 2308
  7.3 3.6 %copy-start.11 = (bf16[512]{0:T(512)(128)(2,1)S(1)}, bf16[512]{0:T(512)(128)(2,1)}, u32[]{:S(2)}) copy-start(bf16[512]{0:T(512)(128)(2,1)} %param.29) | copy-start | bytes 3076
  7.3 76.3 %all-gather.6.cloned.1.call-start = ((), (), s32[]{:S(2)}) async-start(), calls=%async_computation.4 | async-start | bytes 8912896 | tf_op jit(solution)/shard_map/all_gather | solution.py:424
  14.4 12.0 %copy-start.18 = (s32[1,128]{1,0:T(1,128)S(1)}, s32[1,128]{1,0:T(1,128)}, u32[]{:S(2)}) copy-start(s32[1,128]{1,0:T(1,128)} %param.19) | copy-start | bytes 1540
  14.4 53.8 %all-to-all-start = ((bf16[8,128,768]{2,1,0:T(8,128)(2,1)}), bf16[8,128,768]{2,1,0:T(8,128)(2,1)S(1)}, u32[]{:S(2)}, u32[]{:S(2)}) async-start(bf16[8,128,768]{2,1,0:T(8,128)(2,1)} %broadcast_in_dim.94), calls=%async_computation | async-start | bytes 3145728 | tf_op jit(solution)/shard_map/all_to_all | solution.py:434
  21.7 45.6 %collective-permute-start = (bf16[64,1024]{1,0:T(8,128)(2,1)S(1)}, bf16[64,1024]{1,0:T(8,128)(2,1)S(1)}, u32[]{:S(2)}, u32[]{:S(2)}) collective-permute-start(bf16[64,1024]{1,0:T(8,128)(2,1)S(1)} %constant_dynamic-slice_fusion.11), channel_id=1, source_target_pairs={{0,0},{1,16},{2,32},{3,48},{4,64},{5,80},{6,96},{7,112},{8,8},{9,2... | collective-permute-start | bytes 393224 | tf_op jit(solution)/shard_map/ppermute | solution.py:30
  73.4 24.7 %copy-start.2 = (bf16[8,32,1024]{2,1,0:T(8,128)(2,1)}, bf16[8,32,1024]{2,1,0:T(8,128)(2,1)S(1)}, u32[]{:S(2)}) copy-start(bf16[8,32,1024]{2,1,0:T(8,128)(2,1)S(1)} %pad_maximum_fusion.2) | copy-start | bytes 1572868
  98.2 32.0 %all-to-all-start.1 = ((bf16[8,144,512]{2,1,0:T(8,128)(2,1)}), bf16[8,144,512]{2,1,0:T(8,128)(2,1)S(1)}, u32[]{:S(2)}, u32[]{:S(2)}) async-start(bf16[8,144,512]{2,1,0:T(8,128)(2,1)} %get-tuple-element.69), calls=%async_computation.1 | async-start | bytes 2359296 | tf_op jit(solution)/shard_map/all_to_all | solution.py:465
  107.2 110.8 %all-gather.8.cloned.1.call-start = ((), (), s32[]{:S(2)}) async-start(), calls=%async_computation.5 | async-start | bytes 2506752 | tf_op jit(solution)/shard_map/all_gather | solution.py:476
  130.2 7.7 %collective-permute-start.1 = (bf16[2,8,128,1024]{3,2,1,0:T(8,128)(2,1)}, bf16[2,8,128,1024]{3,2,1,0:T(8,128)(2,1)}, u32[]{:S(2)}, u32[]{:S(2)}) collective-permute-start(bf16[2,8,128,1024]{3,2,1,0:T(8,128)(2,1)} %shard_map.266), channel_id=1, source_target_pairs={{8,0},{0,8},{24,16},{16,24},{40,32},{32,40},{56,48},{48,56},{72,64... | collective-permute-start | bytes 12582920 | tf_op jit(solution)/shard_map/ppermute | solution.py:34
  137.8 16.6 %all-to-all-start.2 = ((bf16[8,144,256]{2,1,0:T(8,128)(2,1)}), bf16[8,144,256]{2,1,0:T(8,128)(2,1)S(1)}, u32[]{:S(2)}, u32[]{:S(2)}) async-start(bf16[8,144,256]{2,1,0:T(8,128)(2,1)} %shard_map.265), calls=%async_computation.2 | async-start | bytes 1179648 | tf_op jit(solution)/shard_map/all_to_all | solution.py:480
  145.6 8.9 %copy-start.3 = (bf16[1,128,1024]{2,1,0:T(8,128)(2,1)S(1)}, bf16[1,128,1024]{2,1,0:T(8,128)(2,1)}, u32[]{:S(2)}) copy-start(bf16[1,128,1024]{2,1,0:T(8,128)(2,1)} %param.16) | copy-start | bytes 786436
  154.4 51.7 %copy-start.7 = (bf16[2,128,1024]{2,1,0:T(8,128)(2,1)S(1)}, bf16[2,128,1024]{2,1,0:T(8,128)(2,1)}, u32[]{:S(2)}) copy-start(bf16[2,128,1024]{2,1,0:T(8,128)(2,1)} %get-tuple-element.79) | copy-start | bytes 1572868
  154.4 51.7 %collective-permute-start.3 = (bf16[4,128,1024]{2,1,0:T(8,128)(2,1)}, bf16[4,128,1024]{2,1,0:T(8,128)(2,1)}, u32[]{:S(2)}, u32[]{:S(2)}) collective-permute-start(bf16[4,128,1024]{2,1,0:T(8,128)(2,1)} %get-tuple-element.81), channel_id=1, source_target_pairs={{16,0},{24,8},{0,16},{8,24},{48,32},{56,40},{32,48},{40,56},{80,64... | collective-permute-start | bytes 3145736 | tf_op jit(solution)/shard_map/ppermute | solution.py:34
  154.8 13.0 %collective-permute-start.2 = (bf16[144,64]{1,0:T(8,128)(2,1)S(1)}, bf16[144,64]{1,0:T(8,128)(2,1)S(1)}, u32[]{:S(2)}, u32[]{:S(2)}) collective-permute-start(bf16[144,64]{1,0:T(8,128)(2,1)S(1)} %slice.127), channel_id=1, source_target_pairs={{0,0},{1,16},{2,32},{3,48},{4,64},{5,80},{6,96},{7,112},{8,8},{9,2... | collective-permute-start | bytes 55304 | tf_op jit(solution)/shard_map/ppermute | solution.py:30
  164.5 31.1 %collective-permute-start.4 = (bf16[2,128,1024]{2,1,0:T(8,128)(2,1)}, bf16[2,128,1024]{2,1,0:T(8,128)(2,1)S(1)}, u32[]{:S(2)}, u32[]{:S(2)}) collective-permute-start(bf16[2,128,1024]{2,1,0:T(8,128)(2,1)} %get-tuple-element.82), channel_id=1, source_target_pairs={{0,32},{8,40},{16,48},{24,56},{32,64},{40,72},{48,80},{56,88},{64,... | collective-permute-start | bytes 1572872 | tf_op jit(solution)/shard_map/ppermute | solution.py:34
  165.0 30.6 %collective-permute-start.5 = (bf16[2,128,1024]{2,1,0:T(8,128)(2,1)}, bf16[2,128,1024]{2,1,0:T(8,128)(2,1)S(1)}, u32[]{:S(2)}, u32[]{:S(2)}) collective-permute-start(bf16[2,128,1024]{2,1,0:T(8,128)(2,1)} %get-tuple-element.83), channel_id=1, source_target_pairs={{0,64},{8,72},{16,80},{24,88},{32,96},{40,104},{48,112},{56,120},{... | collective-permute-start | bytes 1572872 | tf_op jit(solution)/shard_map/ppermute | solution.py:34
  165.0 30.6 %collective-permute-start.6 = (bf16[2,128,1024]{2,1,0:T(8,128)(2,1)}, bf16[2,128,1024]{2,1,0:T(8,128)(2,1)S(1)}, u32[]{:S(2)}, u32[]{:S(2)}) collective-permute-start(bf16[2,128,1024]{2,1,0:T(8,128)(2,1)} %get-tuple-element.84), channel_id=1, source_target_pairs={{0,96},{8,104},{16,112},{24,120},{32,0},{40,8},{48,16},{56,24},{64... | collective-permute-start | bytes 1572872 | tf_op jit(solution)/shard_map/ppermute | solution.py:34
  168.8 37.3 %all-to-all-start.3 = ((bf16[8,144,256]{2,1,0:T(8,128)(2,1)}), bf16[8,144,256]{2,1,0:T(8,128)(2,1)S(1)}, u32[]{:S(2)}, u32[]{:S(2)}) async-start(bf16[8,144,256]{2,1,0:T(8,128)(2,1)} %broadcast_in_dim.98), calls=%async_computation.3 | async-start | bytes 1179648 | tf_op jit(solution)/shard_map/all_to_all | solution.py:38
  195.6 10.4 %copy-start.8 = (bf16[2,128,1024]{2,1,0:T(8,128)(2,1)}, bf16[2,128,1024]{2,1,0:T(8,128)(2,1)S(1)}, u32[]{:S(2)}) copy-start(bf16[2,128,1024]{2,1,0:T(8,128)(2,1)S(1)} %collective-permute-done.5) | copy-start | bytes 1572868
  195.7 10.4 %copy-start.9 = (bf16[2,128,1024]{2,1,0:T(8,128)(2,1)}, bf16[2,128,1024]{2,1,0:T(8,128)(2,1)S(1)}, u32[]{:S(2)}) copy-start(bf16[2,128,1024]{2,1,0:T(8,128)(2,1)S(1)} %collective-permute-done.6) | copy-start | bytes 1572868
  206.1 4.7 %copy-start.5 = (bf16[8,144,256]{2,1,0:T(8,128)(2,1)}, bf16[8,144,256]{2,1,0:T(8,128)(2,1)S(1)}, u32[]{:S(2)}) copy-start(bf16[8,144,256]{2,1,0:T(8,128)(2,1)S(1)} %all-to-all-done.3.mine_ref) | copy-start | bytes 1769476
  207.9 20.7 %collective-permute-start.7 = (bf16[128,1024]{1,0:T(8,128)(2,1)S(1)}, bf16[128,1024]{1,0:T(8,128)(2,1)}, u32[]{:S(2)}, u32[]{:S(2)}) collective-permute-start(bf16[128,1024]{1,0:T(8,128)(2,1)S(1)} %fusion.17), channel_id=1, source_target_pairs={{16,0},{24,8},{0,16},{8,24},{48,32},{56,40},{32,48},{40,56},{80,64... | collective-permute-start | bytes 786440 | tf_op jit(solution)/shard_map/ppermute | solution.py:34
  208.8 14.6 %collective-permute-start.8 = (bf16[8,144,256]{2,1,0:T(8,128)(2,1)S(1)}, bf16[8,144,256]{2,1,0:T(8,128)(2,1)}, u32[]{:S(2)}, u32[]{:S(2)}) collective-permute-start(bf16[8,144,256]{2,1,0:T(8,128)(2,1)S(1)} %all-to-all-done.3.mine_ref), channel_id=1, source_target_pairs={{8,0},{0,8},{24,16},{16,24},{40,32},{32,40},{56,48},{48,56},{72,64... | collective-permute-start | bytes 1769480 | tf_op jit(solution)/shard_map/ppermute | solution.py:34
  211.7 16.9 %collective-permute-start.9 = (bf16[128,1024]{1,0:T(8,128)(2,1)}, bf16[128,1024]{1,0:T(8,128)(2,1)}, u32[]{:S(2)}, u32[]{:S(2)}) collective-permute-start(bf16[128,1024]{1,0:T(8,128)(2,1)} %get-tuple-element.126), channel_id=1, source_target_pairs={{0,32},{8,40},{16,48},{24,56},{32,64},{40,72},{48,80},{56,88},{64,... | collective-permute-start | bytes 786440 | tf_op jit(solution)/shard_map/ppermute | solution.py:34
  212.3 16.3 %collective-permute-start.10 = (bf16[128,1024]{1,0:T(8,128)(2,1)}, bf16[128,1024]{1,0:T(8,128)(2,1)}, u32[]{:S(2)}, u32[]{:S(2)}) collective-permute-start(bf16[128,1024]{1,0:T(8,128)(2,1)} %get-tuple-element.125), channel_id=1, source_target_pairs={{0,64},{8,72},{16,80},{24,88},{32,96},{40,104},{48,112},{56,120},{... | collective-permute-start | bytes 786440 | tf_op jit(solution)/shard_map/ppermute | solution.py:34
  214.3 14.3 %collective-permute-start.11 = (bf16[128,1024]{1,0:T(8,128)(2,1)}, bf16[128,1024]{1,0:T(8,128)(2,1)}, u32[]{:S(2)}, u32[]{:S(2)}) collective-permute-start(bf16[128,1024]{1,0:T(8,128)(2,1)} %get-tuple-element.124), channel_id=1, source_target_pairs={{0,96},{8,104},{16,112},{24,120},{32,0},{40,8},{48,16},{56,24},{64... | collective-permute-start | bytes 786440 | tf_op jit(solution)/shard_map/ppermute | solution.py:34
  217.9 14.6 %copy-start.19 = (f32[128]{0:T(128)}, f32[128]{0:T(128)S(1)}, u32[]{:S(2)}) copy-start(f32[128]{0:T(128)S(1)} %slice_bitcast_fusion.5) | copy-start | bytes 1540
  223.4 6.7 %copy-start.6 = (bf16[1,128,1024]{2,1,0:T(8,128)(2,1)S(1)}, bf16[1,128,1024]{2,1,0:T(8,128)(2,1)}, u32[]{:S(2)}) copy-start(bf16[1,128,1024]{2,1,0:T(8,128)(2,1)} %param.17) | copy-start | bytes 786436
  228.6 4.4 %copy-start.1 = (bf16[128,1024]{1,0:T(8,128)(2,1)S(1)}, bf16[128,1024]{1,0:T(8,128)(2,1)}, u32[]{:S(2)}) copy-start(bf16[128,1024]{1,0:T(8,128)(2,1)} %param.24) | copy-start | bytes 786436
Sparse Core Ops, SparseCore 0:
  10.4 73.0 all-gather.5
  131.2 45.6 all-gather.7

commit v4 on v3

--- a/solution.py
+++ b/solution.py
@@ -482,20 +482,19 @@
     wide = lambda v: v.astype(F32)
     low = jnp.sum(wide(late), axis=0).astype(BF16)
     low = jnp.concatenate([low[:, :3 * hd], turn(low[:, 3 * hd:])], axis=1)
-    late_mine, far, *outs[1:] = tie(
-        gather_chips(low), move(far, ACROSS_Y), *[move(outs[d], AHEAD_Z[d]) for d in range(1, 4)])
+    widen_grad, narrow_grad, g2_grad, s2_grad, wb_shard = finish(
+        finish_early_kernel, (f[None],), (early_all,), widen_weight, second_gain, second_shift, (2 * ffc, width))
+    late_mine, wb_shard, far, *outs[1:] = tie(
+        gather_chips(low), wb_shard, move(far, ACROSS_Y), *[move(outs[d], AHEAD_Z[d]) for d in range(1, 4)])
     late_all = late_mine, move(late_mine, OTHER_CORE)
     near = (wide(near) + wide(far)).astype(BF16)
     out_own = sum(wide(v) for v in outs)
     across = out_own[1].astype(BF16)
-    widen_grad, narrow_grad, g2_grad, s2_grad, wb_shard = finish(
-        finish_early_kernel, (f[None],), (early_all,), widen_weight, second_gain, second_shift, (2 * ffc, width))
-
     joint_grad, dense_grad, g1_grad, s1_grad, jb_shard = finish(
         finish_late_kernel, (f[None], core), late_all, joint_weight, first_gain, first_shift, (2 * hd, width))
 
     moved = [move(near[d], AHEAD_Z[d]) for d in range(1, 4)]
-    across, wb_shard, jb_shard, *moved = tie(move(across, ACROSS_Y), wb_shard, jb_shard, *moved)
+    across, jb_shard, *moved = tie(move(across, ACROSS_Y), jb_shard, *moved)
     u_own = wide(near[0]) + sum(wide(v) for v in moved)
     out_own = out_own[0] + wide(across)
     own_x = own_tokens.astype(F32)

time: 241 us -> 242 us (level)
    ppermute x10, waiting for transfers between devices: 0.03 us -> 6.65 us  [move(): return lax.ppermute(v, 'ctx', way)]
    all_to_all x1, waiting for transfers between devices: 10.4 us -> 4.89 us  [gather_chips(): lax.all_to_all(jnp.broadcast_to(own[None], (N_CTX // 2,) + own.shape), 'c...]
  transfers between devices with their start and end apart: 18 -> 18, of which waited for: 2 -> 4; matrix products, arithmetic and copies ran while one was open for 12% -> 11% of each run, Pallas kernels for 20% -> 20%
where the time goes in v4:
time: 242 us; the launch traced here: 241 us
  starting transfers between devices  70.6 us (29%)
  Pallas kernels  61.8 us (26%)
  blocking collectives  35.9 us (15%)
  other arithmetic  22.4 us (9%)
  waiting for transfers between devices  20.8 us (9%)
  local copies, waits for them, and re-layouts  14.7 us (6%)
  between operations  14.5 us (6%)
    all_gather x1, blocking collectives, shards(): lax.all_gather(rotary_place[0], 'ctx', axis=0, tiled=True).astype(F32)  35.9 us
    all_to_all x1, starting transfers between devices, gather_chips(): lax.all_to_all(jnp.broadcast_to(own[None], (N_CTX // 2,) + own.shape), 'c...  25.2 us
    pallas_call x2, Pallas kernels, spread(): pl.pallas_call(spread_kernel, grid_spec=pltpu.PrefetchScalarGridSpec(num_...  15.9 us
    pallas_call x1, Pallas kernels, attention(): pl.pallas_call(attention_kernel, out_shape=jax.ShapeDtypeStruct((rows, 4...  15.2 us
    pallas_call x1, Pallas kernels, project(): pl.pallas_call(project_kernel, grid=(slots // per,), in_specs=[pl.BlockSp...  14.6 us
    ppermute x2, starting transfers between devices, turn(): return lax.ppermute(v, ('ctx', 'fsdp'), TURN)  14.3 us
    pallas_call x2, Pallas kernels, finish(): pl.pallas_call(kernel, in_specs=[pl.BlockSpec(memory_space=pltpu.SMEM)] *...  9.35 us
    all_gather x1, waiting for transfers between devices, shards(): lax.all_gather(jnp.concatenate([own_tokens, own_up], axis=0), 'ctx', axis=0)  9.16 us
  transfers between devices with their start and end apart: 18, of which 4 were waited for; matrix products, arithmetic and copies ran while one was open for 11% of the time, Pallas kernels for 20%

profile of v4, /device:TPU:22, one launch (start us, length us, event | category | flops | bytes accessed | tf_op | source)
XLA Modules:
  0.0 240.8 jit_solution(15575674961645445800)
XLA Ops:
  7.3 1.9 pad_maximum_fusion.1
  9.3 0.4 copy.53
  9.8 0.1 copy.55
  10.1 0.1 copy.57
  10.2 0.1 copy.58
  10.4 0.1 copy.59
  10.5 0.1 copy.60
  10.7 0.2 reshape.140
  11.0 0.8 constant_dynamic-slice_fusion
  11.8 1.0 constant_dynamic-slice_fusion.2
  12.9 0.2 concatenate.23
  13.1 1.2 broadcast_in_dim.94
  14.4 7.3 %all-to-all-start = ((bf16[8,128,768]{2,1,0:T(8,128)(2,1)}), bf16[8,128,768]{2,1,0:T(8,128)(2,1)S(1)}, u32[]{:S(2)}, u32[]{:S(2)}) async-start(bf16[8,128,768]{2,1,0:T(8,128)(2,1)} %broadcast_in_dim.94), calls=%async_computation | async-start | bytes 3145728 | tf_op jit(solution)/shard_map/all_to_all | solution.py:434
  21.7 4.6 %collective-permute-start = (bf16[64,1024]{1,0:T(8,128)(2,1)S(1)}, bf16[64,1024]{1,0:T(8,128)(2,1)S(1)}, u32[]{:S(2)}, u32[]{:S(2)}) collective-permute-start(bf16[64,1024]{1,0:T(8,128)(2,1)S(1)} %constant_dynamic-slice_fusion.11), channel_id=1, source_target_pairs={{0,0},{1,16},{2,32},{3,48},{4,64},{5,80},{6,96},{7,112},{8,8},{9,2... | collective-permute-start | bytes 393224 | tf_op jit(solution)/shard_map/ppermute | solution.py:30
  26.3 35.9 %all-gather.1 = s32[1,2048]{1,0:T(1,128)S(1)} all-gather(s32[1,128]{1,0:T(1,128)S(1)} %copy-done.17), channel_id=3, replica_groups=mesh['ctx'=16,'fsdp'=8] {'ctx'}, dimensions={1}, use_global_device_ids=true | all-gather | bytes 8704 | tf_op jit(solution)/shard_map/all_gather | solution.py:436
  62.3 5.0 %fusion.2.table_ref = f32[2048,128]{1,0:T(8,128)} fusion(f32[128]{0:T(128)S(1)} %fusion.22, f32[2048]{0:T(1024)S(1)} %bitcast.94, pred[128]{0:T(512)(128)(4,1)S(1)} %iota_compare_fusion.1), kind=kLoop, calls=%fused_computation.8 | loop fusion | flops 524288 | bytes 1057408 | tf_op jit(solution)/shard_map/jit(_where)/select_n | solution.py:444
  67.3 0.9 pad.8.dense_ref
  68.4 0.2 slice.121
  68.6 0.2 slice.119
  68.8 0.2 reshape_reshape.3
  69.1 0.3 reshape.143
  69.5 1.6 slice_reduce_fusion.1
  71.1 1.7 multiply_reduce_fusion
  72.8 0.6 pad_maximum_fusion.5
  73.5 0.9 pad_maximum_fusion.back_ref
  74.4 9.2 %all-gather.6.cloned.1.call-done = bf16[4096,1024]{1,0:T(8,128)(2,1)} async-done(((bf16[256,1024]{1,0:T(8,128)(2,1)}), bf16[4096,1024]{1,0:T(8,128)(2,1)}) %all-gather.6.cloned.1.call-update) | async-done | bytes 8388624 | tf_op jit(solution)/shard_map/all_gather | solution.py:424
  83.5 14.6 %shard_map.263 = (bf16[2048,1024]{1,0:T(8,128)(2,1)}, f32[2048,256]{1,0:T(8,128)}, f32[2048,64]{1,0:T(8,128)}, bf16[2048,256]{1,0:T(8,128)(2,1)}, bf16[2048,256]...) custom-call(bf16[16,256,1024]{2,1,0:T(8,128)(2,1)} %bitcast.76, bf16[16,256,1024]{2,1,0:T(8,128)(2,1)} %bitcast.77, ...), custom_call_target="tpu_custom_call" | custom-call | flops 5637144576 | bytes 20971520 | tf_op jit(solution)/shard_map/pallas_call | solution.py:111
  98.2 9.0 %all-to-all-start.1 = ((bf16[8,144,512]{2,1,0:T(8,128)(2,1)}), bf16[8,144,512]{2,1,0:T(8,128)(2,1)S(1)}, u32[]{:S(2)}, u32[]{:S(2)}) async-start(bf16[8,144,512]{2,1,0:T(8,128)(2,1)} %get-tuple-element.69), calls=%async_computation.1 | async-start | bytes 2359296 | tf_op jit(solution)/shard_map/all_to_all | solution.py:465
  107.2 0.6 pad_add_fusion.1.place_ref
  107.8 15.2 %shard_map.264.mixed_ref = bf16[2048,256]{1,0:T(8,128)(2,1)} custom-call(s32[16]{0:T(128)} %bitcast.103, f32[2048,256]{1,0:T(8,128)} %get-tuple-element.63.joint_ref, f32[2048,128]{1,0:T(8,128)} %fusion.2.table_ref, f32[2048,64]{1,0:T(8,128)} %get-tuple-element.65.grad_ref), custom_call_target="tpu_custom_call" | custom-call | flops 1879048192 | bytes 8388608 | tf_op jit(solution)/shard_map/pallas_call | solution.py:380
  123.0 7.2 %shard_map.266 = bf16[2,8,128,1024]{3,2,1,0:T(8,128)(2,1)} custom-call(s32[3]{0:T(128)} %pad_add_fusion.1.place_ref, bf16[8,2,128,256]{3,2,1,0:T(8,128)(2,1)} %bitcast.74, bf16[8,2,128,256]{3,2,1,0:T(8,128)(2,1)} %bitcast.87, bf16[8,2,128,256]{3,2,1,0:T(8,128)(2,1)} %bitcast.85, bf16[1024,256]{1,0:T(8,128)(2,1)} %get-tuple-element.118.wj_ref, ...), custom_call_target="tpu_custom_call" | custom-call | flops 2147483648 | bytes 9437184 | tf_op jit(solution)/shard_map/pallas_call | solution.py:212
  130.2 0.2 convert_reduce_fusion
  130.4 0.7 convert_element_type.114
  131.1 6.7 %shard_map.265 = bf16[8,144,256]{2,1,0:T(8,128)(2,1)} custom-call(bf16[2048,1024]{1,0:T(8,128)(2,1)} %get-tuple-element.62.xhat_ref, bf16[16,256,1024]{2,1,0:T(8,128)(2,1)} %bitcast.78, bf16[2048,256]{1,0:T(8,128)(2,1)} %shard_map.264.mixed_ref), custom_call_target="tpu_custom_call" | custom-call | flops 1073741824 | bytes 10485760 | tf_op jit(solution)/shard_map/pallas_call | solution.py:154
  137.8 7.2 %all-to-all-start.2 = ((bf16[8,144,256]{2,1,0:T(8,128)(2,1)}), bf16[8,144,256]{2,1,0:T(8,128)(2,1)S(1)}, u32[]{:S(2)}, u32[]{:S(2)}) async-start(bf16[8,144,256]{2,1,0:T(8,128)(2,1)} %shard_map.265), calls=%async_computation.2 | async-start | bytes 1179648 | tf_op jit(solution)/shard_map/all_to_all | solution.py:480
  145.0 0.6 pad_add_fusion.3.place_ref
  145.6 8.7 %shard_map.267 = (bf16[4,128,1024]{2,1,0:T(8,128)(2,1)}, bf16[4,128,1024]{2,1,0:T(8,128)(2,1)}, bf16[2,128,1024]{2,1,0:T(8,128)(2,1)}, bf16[2,128,1024]{2,1,0:T(...) custom-call(s32[3]{0:T(128)} %pad_add_fusion.3.place_ref, bf16[8,2,128,256]{3,2,1,0:T(8,128)(2,1)} %bitcast.75, ...), custom_call_target="tpu_custom_call" | custom-call | flops 2147483648 | bytes 9437184 | tf_op jit(solution)/shard_map/pallas_call | solution.py:212
  154.8 9.7 %collective-permute-start.2 = (bf16[144,64]{1,0:T(8,128)(2,1)S(1)}, bf16[144,64]{1,0:T(8,128)(2,1)S(1)}, u32[]{:S(2)}, u32[]{:S(2)}) collective-permute-start(bf16[144,64]{1,0:T(8,128)(2,1)S(1)} %slice.127), channel_id=1, source_target_pairs={{0,0},{1,16},{2,32},{3,48},{4,64},{5,80},{6,96},{7,112},{8,8},{9,2... | collective-permute-start | bytes 55304 | tf_op jit(solution)/shard_map/ppermute | solution.py:30
  164.5 0.7 copy.61.gain_ref
  165.2 0.7 copy.62.shift_ref
  166.0 0.5 collective-permute-start.4
  166.5 2.7 %collective-permute-start.6 = (bf16[2,128,1024]{2,1,0:T(8,128)(2,1)}, bf16[2,128,1024]{2,1,0:T(8,128)(2,1)}, u32[]{:S(2)}, u32[]{:S(2)}) collective-permute-start(bf16[2,128,1024]{2,1,0:T(8,128)(2,1)} %get-tuple-element.86), channel_id=1, source_target_pairs={{0,96},{8,104},{16,112},{24,120},{32,0},{40,8},{48,16},{56,24},{64... | collective-permute-start | bytes 1572872 | tf_op jit(solution)/shard_map/ppermute | solution.py:34
  169.3 0.9 broadcast_in_dim.98
  170.2 25.2 %all-to-all-start.3 = ((bf16[8,144,256]{2,1,0:T(8,128)(2,1)}), bf16[8,144,256]{2,1,0:T(8,128)(2,1)S(1)}, u32[]{:S(2)}, u32[]{:S(2)}) async-start(bf16[8,144,256]{2,1,0:T(8,128)(2,1)} %broadcast_in_dim.98), calls=%async_computation.3 | async-start | bytes 1179648 | tf_op jit(solution)/shard_map/all_to_all | solution.py:38
  195.4 0.2 fusion.12
  195.7 5.5 %shard_map.268 = (f32[128,4096]{1,0:T(8,128)}, f32[512,1024]{1,0:T(8,128)}, f32[1,128]{1,0:T(1,128)}, f32[1,128]{1,0:T(1,128)}, f32[1,512]{1,0:T(1,128)}) custom-call(s32[1]{0:T(128)} %bitcast.23.f_ref, bf16[16,144,512]{2,1,0:T(8,128)(2,1)} %bitcast.89, bf16[128,4096]{1,0:T(8,128)(2,1)} %weight_ref.2, f32[128,1]{1,0:T(8,128)} %copy.61.gain_ref, ...), custom_call_target="tpu_custom_call" | custom-call | flops 4194304 | bytes 6291456 | tf_op jit(solution)/shard_map/pallas_call | solution.py:289
  201.2 4.9 %all-to-all-done.3.mine_ref = bf16[8,144,256]{2,1,0:T(8,128)(2,1)S(1)} async-done(((bf16[8,144,256]{2,1,0:T(8,128)(2,1)}), bf16[8,144,256]{2,1,0:T(8,128)(2,1)S(1)}, u32[]{:S(2)}, u32[]{:S(2)}) %all-to-all-start.3) | async-done | bytes 589856 | tf_op jit(solution)/shard_map/all_to_all | solution.py:38
  206.1 2.4 %convert_add_fusion = f32[2,128,1024]{2,1,0:T(8,128)S(1)} fusion(bf16[2,128,1024]{2,1,0:T(8,128)(2,1)} %collective-permute-done.6, bf16[2,128,1024]{2,1,0:T(8,128)(2,1)} %copy-done.8, bf16[2,128,1024]{2,1,0:T(8,128)(2,1)} %copy-done.7, bf16[2,128,1024]{2,1,0:T(8,128)(2,1)} %get-tuple-element.79), kind=kLoop, calls=%fused_computation.9 | loop fusion | flops 1835008 | bytes 3145728 | tf_op jit(solution)/shard_map/add | solution.py:491
  208.6 0.7 fusion.17
  209.3 0.9 collective-permute-start.7
  210.2 2.0 add_convert_fusion
  212.2 0.9 slice_bitcast_fusion.2
  213.1 0.6 collective-permute-start.9
  213.6 2.1 collective-permute-start.10
  215.7 0.6 collective-permute-start.11
  216.3 0.7 copy.63.gain_ref
  217.0 0.7 copy.64.shift_ref
  217.8 3.8 %shard_map.269 = (f32[128,3072]{1,0:T(8,128)}, f32[128,1024]{1,0:T(8,128)}, f32[1,128]{1,0:T(1,128)}, f32[1,128]{1,0:T(1,128)}, f32[1,384]{1,0:T(1,128)}) custom-call(s32[1]{0:T(128)} %bitcast.23.f_ref, s32[1]{0:T(128)} %bitcast.22.core_ref, bf16[8,144,256]{2,1,0:T(8,128)(2,1)} %copy-done.5, bf16[8,144,256]{2,1,0:T(8,128)(2,1)} %collective-permute-done.8.other_ref, ...), custom_call_target="tpu_custom_call" | custom-call | flops 3145728 | bytes 4718592 | tf_op jit(solution)/shard_map/pallas_call | solution.py:289
  221.6 1.3 reduce.7
  222.9 6.0 %collective-permute-done.9 = bf16[128,1024]{1,0:T(8,128)(2,1)} collective-permute-done((bf16[128,1024]{1,0:T(8,128)(2,1)}, bf16[128,1024]{1,0:T(8,128)(2,1)}, u32[]{:S(2)}, u32[]{:S(2)}) %collective-permute-start.9) | collective-permute-done | bytes 262176 | tf_op jit(solution)/shard_map/ppermute | solution.py:34
  228.9 0.6 collective-permute-done.11
  229.5 1.4 fusion.23
  231.0 2.5 %fusion.11 = (f32[1,128,1024]{2,1,0:T(8,128)}, bf16[1,128,1024]{2,1,0:T(8,128)(2,1)}) fusion(f32[128]{0:T(128)S(1)} %get-tuple-element.141, f32[128]{0:T(128)S(1)} %get-tuple-element.142, f32[128]{0:T(128)S(1)} %add_rsqrt_fusion, f32[128]{0:T(128)S(1)} %broadcast_multiply_fusion.2, bf16[1,128,1024]{2,1,0:T(8,128)(2,1)} %param.17, ...), kind=kLoop, calls=%fused_computation.25 | loop fusion | flops 2883584 | bytes 3155968 | tf_op jit(solution)/shard_map/broadcast_in_dim | solution.py:510
  233.4 0.5 copy.66
  (92 shorter events, 1.6 us)
Async XLA Ops:
  7.2 14.5 %copy-start = (bf16[128,1024]{1,0:T(8,128)(2,1)S(1)}, bf16[128,1024]{1,0:T(8,128)(2,1)}, u32[]{:S(2)}) copy-start(bf16[128,1024]{1,0:T(8,128)(2,1)} %param.24) | copy-start | bytes 786436
  7.2 2.1 copy-start.4
  7.2 2.6 %copy-start.15 = (bf16[128]{0:T(256)(128)(2,1)S(1)}, bf16[128]{0:T(256)(128)(2,1)}, u32[]{:S(2)}) copy-start(bf16[128]{0:T(256)(128)(2,1)} %param.20) | copy-start | bytes 772
  7.2 2.7 %copy-start.16 = (bf16[128]{0:T(256)(128)(2,1)S(1)}, bf16[128]{0:T(256)(128)(2,1)}, u32[]{:S(2)}) copy-start(bf16[128]{0:T(256)(128)(2,1)} %param.21) | copy-start | bytes 772
  7.2 2.9 %copy-start.13 = (bf16[128]{0:T(256)(128)(2,1)S(1)}, bf16[128]{0:T(256)(128)(2,1)}, u32[]{:S(2)}) copy-start(bf16[128]{0:T(256)(128)(2,1)} %param.26) | copy-start | bytes 772
  7.2 3.0 %copy-start.14 = (bf16[128]{0:T(256)(128)(2,1)S(1)}, bf16[128]{0:T(256)(128)(2,1)}, u32[]{:S(2)}) copy-start(bf16[128]{0:T(256)(128)(2,1)} %param.27) | copy-start | bytes 772
  7.3 3.1 %copy-start.11 = (bf16[128]{0:T(256)(128)(2,1)S(1)}, bf16[128]{0:T(256)(128)(2,1)}, u32[]{:S(2)}) copy-start(bf16[128]{0:T(256)(128)(2,1)} %param.25) | copy-start | bytes 772
  7.3 3.3 %copy-start.12 = (bf16[128]{0:T(256)(128)(2,1)S(1)}, bf16[128]{0:T(256)(128)(2,1)}, u32[]{:S(2)}) copy-start(bf16[128]{0:T(256)(128)(2,1)} %param.31) | copy-start | bytes 772
  7.3 3.4 %copy-start.9 = (bf16[384]{0:T(512)(128)(2,1)S(1)}, bf16[384]{0:T(512)(128)(2,1)}, u32[]{:S(2)}) copy-start(bf16[384]{0:T(512)(128)(2,1)} %param.23) | copy-start | bytes 2308
  7.3 3.6 %copy-start.10 = (bf16[512]{0:T(512)(128)(2,1)S(1)}, bf16[512]{0:T(512)(128)(2,1)}, u32[]{:S(2)}) copy-start(bf16[512]{0:T(512)(128)(2,1)} %param.29) | copy-start | bytes 3076
  7.3 76.3 %all-gather.6.cloned.1.call-start = ((), (), s32[]{:S(2)}) async-start(), calls=%async_computation.4 | async-start | bytes 8912896 | tf_op jit(solution)/shard_map/all_gather | solution.py:424
  14.4 12.0 %copy-start.17 = (s32[1,128]{1,0:T(1,128)S(1)}, s32[1,128]{1,0:T(1,128)}, u32[]{:S(2)}) copy-start(s32[1,128]{1,0:T(1,128)} %param.19) | copy-start | bytes 1540
  14.4 53.8 %all-to-all-start = ((bf16[8,128,768]{2,1,0:T(8,128)(2,1)}), bf16[8,128,768]{2,1,0:T(8,128)(2,1)S(1)}, u32[]{:S(2)}, u32[]{:S(2)}) async-start(bf16[8,128,768]{2,1,0:T(8,128)(2,1)} %broadcast_in_dim.94), calls=%async_computation | async-start | bytes 3145728 | tf_op jit(solution)/shard_map/all_to_all | solution.py:434
  21.7 45.6 %collective-permute-start = (bf16[64,1024]{1,0:T(8,128)(2,1)S(1)}, bf16[64,1024]{1,0:T(8,128)(2,1)S(1)}, u32[]{:S(2)}, u32[]{:S(2)}) collective-permute-start(bf16[64,1024]{1,0:T(8,128)(2,1)S(1)} %constant_dynamic-slice_fusion.11), channel_id=1, source_target_pairs={{0,0},{1,16},{2,32},{3,48},{4,64},{5,80},{6,96},{7,112},{8,8},{9,2... | collective-permute-start | bytes 393224 | tf_op jit(solution)/shard_map/ppermute | solution.py:30
  73.5 24.7 %copy-start.2 = (bf16[8,32,1024]{2,1,0:T(8,128)(2,1)}, bf16[8,32,1024]{2,1,0:T(8,128)(2,1)S(1)}, u32[]{:S(2)}) copy-start(bf16[8,32,1024]{2,1,0:T(8,128)(2,1)S(1)} %pad_maximum_fusion.2) | copy-start | bytes 1572868
  98.2 32.0 %all-to-all-start.1 = ((bf16[8,144,512]{2,1,0:T(8,128)(2,1)}), bf16[8,144,512]{2,1,0:T(8,128)(2,1)S(1)}, u32[]{:S(2)}, u32[]{:S(2)}) async-start(bf16[8,144,512]{2,1,0:T(8,128)(2,1)} %get-tuple-element.69), calls=%async_computation.1 | async-start | bytes 2359296 | tf_op jit(solution)/shard_map/all_to_all | solution.py:465
  107.2 88.5 %all-gather.8.cloned.1.call-start = ((), (), s32[]{:S(2)}) async-start(), calls=%async_computation.5 | async-start | bytes 2506752 | tf_op jit(solution)/shard_map/all_gather | solution.py:476
  130.2 7.7 %collective-permute-start.1 = (bf16[2,8,128,1024]{3,2,1,0:T(8,128)(2,1)}, bf16[2,8,128,1024]{3,2,1,0:T(8,128)(2,1)}, u32[]{:S(2)}, u32[]{:S(2)}) collective-permute-start(bf16[2,8,128,1024]{3,2,1,0:T(8,128)(2,1)} %shard_map.266), channel_id=1, source_target_pairs={{8,0},{0,8},{24,16},{16,24},{40,32},{32,40},{56,48},{48,56},{72,64... | collective-permute-start | bytes 12582920 | tf_op jit(solution)/shard_map/ppermute | solution.py:34
  137.8 16.5 %all-to-all-start.2 = ((bf16[8,144,256]{2,1,0:T(8,128)(2,1)}), bf16[8,144,256]{2,1,0:T(8,128)(2,1)S(1)}, u32[]{:S(2)}, u32[]{:S(2)}) async-start(bf16[8,144,256]{2,1,0:T(8,128)(2,1)} %shard_map.265), calls=%async_computation.2 | async-start | bytes 1179648 | tf_op jit(solution)/shard_map/all_to_all | solution.py:480
  145.6 8.9 %copy-start.3 = (bf16[1,128,1024]{2,1,0:T(8,128)(2,1)S(1)}, bf16[1,128,1024]{2,1,0:T(8,128)(2,1)}, u32[]{:S(2)}) copy-start(bf16[1,128,1024]{2,1,0:T(8,128)(2,1)} %param.16) | copy-start | bytes 786436
  154.4 51.7 %collective-permute-start.3 = (bf16[4,128,1024]{2,1,0:T(8,128)(2,1)}, bf16[4,128,1024]{2,1,0:T(8,128)(2,1)S(1)}, u32[]{:S(2)}, u32[]{:S(2)}) collective-permute-start(bf16[4,128,1024]{2,1,0:T(8,128)(2,1)} %get-tuple-element.83), channel_id=1, source_target_pairs={{16,0},{24,8},{0,16},{8,24},{48,32},{56,40},{32,48},{40,56},{80,64... | collective-permute-start | bytes 3145736 | tf_op jit(solution)/shard_map/ppermute | solution.py:34
  154.8 14.4 %collective-permute-start.2 = (bf16[144,64]{1,0:T(8,128)(2,1)S(1)}, bf16[144,64]{1,0:T(8,128)(2,1)S(1)}, u32[]{:S(2)}, u32[]{:S(2)}) collective-permute-start(bf16[144,64]{1,0:T(8,128)(2,1)S(1)} %slice.127), channel_id=1, source_target_pairs={{0,0},{1,16},{2,32},{3,48},{4,64},{5,80},{6,96},{7,112},{8,8},{9,2... | collective-permute-start | bytes 55304 | tf_op jit(solution)/shard_map/ppermute | solution.py:30
  166.0 35.2 %collective-permute-start.4 = (bf16[2,128,1024]{2,1,0:T(8,128)(2,1)}, bf16[2,128,1024]{2,1,0:T(8,128)(2,1)S(1)}, u32[]{:S(2)}, u32[]{:S(2)}) collective-permute-start(bf16[2,128,1024]{2,1,0:T(8,128)(2,1)} %get-tuple-element.84), channel_id=1, source_target_pairs={{0,32},{8,40},{16,48},{24,56},{32,64},{40,72},{48,80},{56,88},{64,... | collective-permute-start | bytes 1572872 | tf_op jit(solution)/shard_map/ppermute | solution.py:34
  166.5 34.8 %collective-permute-start.5 = (bf16[2,128,1024]{2,1,0:T(8,128)(2,1)}, bf16[2,128,1024]{2,1,0:T(8,128)(2,1)S(1)}, u32[]{:S(2)}, u32[]{:S(2)}) collective-permute-start(bf16[2,128,1024]{2,1,0:T(8,128)(2,1)} %get-tuple-element.85), channel_id=1, source_target_pairs={{0,64},{8,72},{16,80},{24,88},{32,96},{40,104},{48,112},{56,120},{... | collective-permute-start | bytes 1572872 | tf_op jit(solution)/shard_map/ppermute | solution.py:34
  166.5 34.8 %collective-permute-start.6 = (bf16[2,128,1024]{2,1,0:T(8,128)(2,1)}, bf16[2,128,1024]{2,1,0:T(8,128)(2,1)}, u32[]{:S(2)}, u32[]{:S(2)}) collective-permute-start(bf16[2,128,1024]{2,1,0:T(8,128)(2,1)} %get-tuple-element.86), channel_id=1, source_target_pairs={{0,96},{8,104},{16,112},{24,120},{32,0},{40,8},{48,16},{56,24},{64... | collective-permute-start | bytes 1572872 | tf_op jit(solution)/shard_map/ppermute | solution.py:34
  170.2 35.9 %all-to-all-start.3 = ((bf16[8,144,256]{2,1,0:T(8,128)(2,1)}), bf16[8,144,256]{2,1,0:T(8,128)(2,1)S(1)}, u32[]{:S(2)}, u32[]{:S(2)}) async-start(bf16[8,144,256]{2,1,0:T(8,128)(2,1)} %broadcast_in_dim.98), calls=%async_computation.3 | async-start | bytes 1179648 | tf_op jit(solution)/shard_map/all_to_all | solution.py:38
  201.2 4.9 %copy-start.7 = (bf16[2,128,1024]{2,1,0:T(8,128)(2,1)}, bf16[2,128,1024]{2,1,0:T(8,128)(2,1)S(1)}, u32[]{:S(2)}) copy-start(bf16[2,128,1024]{2,1,0:T(8,128)(2,1)S(1)} %collective-permute-done.4) | copy-start | bytes 1572868
  201.2 4.9 %copy-start.8 = (bf16[2,128,1024]{2,1,0:T(8,128)(2,1)}, bf16[2,128,1024]{2,1,0:T(8,128)(2,1)S(1)}, u32[]{:S(2)}) copy-start(bf16[2,128,1024]{2,1,0:T(8,128)(2,1)S(1)} %collective-permute-done.5) | copy-start | bytes 1572868
  206.1 6.0 %copy-start.5 = (bf16[8,144,256]{2,1,0:T(8,128)(2,1)}, bf16[8,144,256]{2,1,0:T(8,128)(2,1)S(1)}, u32[]{:S(2)}) copy-start(bf16[8,144,256]{2,1,0:T(8,128)(2,1)S(1)} %all-to-all-done.3.mine_ref) | copy-start | bytes 1769476
  206.1 4.1 %copy-start.6 = (bf16[4,128,1024]{2,1,0:T(8,128)(2,1)}, bf16[4,128,1024]{2,1,0:T(8,128)(2,1)S(1)}, u32[]{:S(2)}) copy-start(bf16[4,128,1024]{2,1,0:T(8,128)(2,1)S(1)} %collective-permute-done.3) | copy-start | bytes 3145732
  209.3 13.6 %collective-permute-start.7 = (bf16[128,1024]{1,0:T(8,128)(2,1)}, bf16[128,1024]{1,0:T(8,128)(2,1)}, u32[]{:S(2)}, u32[]{:S(2)}) collective-permute-start(bf16[128,1024]{1,0:T(8,128)(2,1)} %fusion.17), channel_id=1, source_target_pairs={{16,0},{24,8},{0,16},{8,24},{48,32},{56,40},{32,48},{40,56},{80,64... | collective-permute-start | bytes 786440 | tf_op jit(solution)/shard_map/ppermute | solution.py:34
  210.2 7.6 %collective-permute-start.8 = (bf16[8,144,256]{2,1,0:T(8,128)(2,1)S(1)}, bf16[8,144,256]{2,1,0:T(8,128)(2,1)}, u32[]{:S(2)}, u32[]{:S(2)}) collective-permute-start(bf16[8,144,256]{2,1,0:T(8,128)(2,1)S(1)} %all-to-all-done.3.mine_ref), channel_id=1, source_target_pairs={{8,0},{0,8},{24,16},{16,24},{40,32},{32,40},{56,48},{48,56},{72,64... | collective-permute-start | bytes 1769480 | tf_op jit(solution)/shard_map/ppermute | solution.py:34
  213.1 15.9 %collective-permute-start.9 = (bf16[128,1024]{1,0:T(8,128)(2,1)}, bf16[128,1024]{1,0:T(8,128)(2,1)}, u32[]{:S(2)}, u32[]{:S(2)}) collective-permute-start(bf16[128,1024]{1,0:T(8,128)(2,1)} %get-tuple-element.126), channel_id=1, source_target_pairs={{0,32},{8,40},{16,48},{24,56},{32,64},{40,72},{48,80},{56,88},{64,... | collective-permute-start | bytes 786440 | tf_op jit(solution)/shard_map/ppermute | solution.py:34
  213.6 15.3 %collective-permute-start.10 = (bf16[128,1024]{1,0:T(8,128)(2,1)}, bf16[128,1024]{1,0:T(8,128)(2,1)}, u32[]{:S(2)}, u32[]{:S(2)}) collective-permute-start(bf16[128,1024]{1,0:T(8,128)(2,1)} %get-tuple-element.125), channel_id=1, source_target_pairs={{0,64},{8,72},{16,80},{24,88},{32,96},{40,104},{48,112},{56,120},{... | collective-permute-start | bytes 786440 | tf_op jit(solution)/shard_map/ppermute | solution.py:34
  215.7 13.9 %collective-permute-start.11 = (bf16[128,1024]{1,0:T(8,128)(2,1)}, bf16[128,1024]{1,0:T(8,128)(2,1)}, u32[]{:S(2)}, u32[]{:S(2)}) collective-permute-start(bf16[128,1024]{1,0:T(8,128)(2,1)} %get-tuple-element.124), channel_id=1, source_target_pairs={{0,96},{8,104},{16,112},{24,120},{32,0},{40,8},{48,16},{56,24},{64... | collective-permute-start | bytes 786440 | tf_op jit(solution)/shard_map/ppermute | solution.py:34
  217.8 15.7 %copy-start.18 = (f32[128]{0:T(128)}, f32[128]{0:T(128)S(1)}, u32[]{:S(2)}) copy-start(f32[128]{0:T(128)S(1)} %slice_bitcast_fusion.5) | copy-start | bytes 1540
  221.6 12.3 %copy-start.1 = (bf16[128,1024]{1,0:T(8,128)(2,1)S(1)}, bf16[128,1024]{1,0:T(8,128)(2,1)}, u32[]{:S(2)}) copy-start(bf16[128,1024]{1,0:T(8,128)(2,1)} %param.24) | copy-start | bytes 786436
Sparse Core Ops, SparseCore 0:
  10.4 73.0 all-gather.5
  131.2 44.0 all-gather.7

commit v5 on v2

--- a/solution.py
+++ b/solution.py
@@ -51,8 +51,8 @@
     return jnp.dot(a, b, preferred_element_type=F32)
 
 
-def project_kernel(x_ref, up_ref, wj_ref, ww_ref, add_ref, back_ref,
-                   xhat_ref, joint_ref, grad_ref, act_ref, wg_ref, early_ref, widen_s, narrow_s, wg_sum_s, up_sum_s):
+def project_kernel(x_ref, up_ref, wj_ref, ww_ref, add_ref, back_ref, table_ref,
+                   xhat_ref, joint_ref, act_ref, wg_ref, early_ref, widen_s, narrow_s, wg_sum_s, up_sum_s):
     block, width = x_ref.shape[0] * x_ref.shape[1], x_ref.shape[2]
     i = pl.program_id(0)
 
@@ -66,7 +66,7 @@
     xhat = (center * lax.rsqrt(jnp.mean(center * center, axis=-1, keepdims=True) + EPSILON)).astype(BF16)
     xhat_ref[...] = xhat
     wide = wj_ref.shape[1]
-    joint_ref[...] = dot_nn(xhat, wj_ref[...]) + add_ref[0:1, :wide]
+    joint_ref[:, :wide] = dot_nn(xhat, wj_ref[...]) + add_ref[0:1, :wide]
     widened = dot_nn(xhat, ww_ref[...]) + add_ref[0:1, wide:]
     phi = 0.5 * (1.0 + lax.erf(widened * (0.5 ** 0.5)))
     act = (widened * phi).astype(BF16)
@@ -75,7 +75,8 @@
     up = up_ref[...].reshape(block, width)
     k = ww_ref.shape[1]
     hd = back_ref.shape[0] - k
-    grad_ref[...] = dot_nt(up, back_ref[0:hd, :])
+    joint_ref[:, 3 * hd:4 * hd] = dot_nt(up, back_ref[0:hd, :])
+    joint_ref[:, wide:wide + table_ref.shape[1]] = table_ref[...]
     wg = (dot_nt(up, back_ref[hd:, :]) * slope).astype(BF16)
     wg_ref[...] = wg
     widen_s[...] += dot_nn(wg.T, xhat)
@@ -98,13 +99,12 @@
             early_ref[f, n:, k + n:] = jnp.zeros((16, k - n), BF16)
 
 
-def project(both, wj, ww, add, back):
+def project(both, wj, ww, add, back, table):
     slots, _, width = both.shape
     own, per = 128, 4
     rows, block = slots * own, per * own
     n = width // N_FSDP
     wide, ffc = wj.shape[1], ww.shape[1]
-    hd = back.shape[0] - ffc
     whole = lambda a: pl.BlockSpec(a.shape, lambda i: (0, 0))
     tall = lambda n: pl.BlockSpec((block, n), lambda i: (i, 0))
     payload = (N_FSDP, n + 16, 2 * ffc)
@@ -114,56 +114,18 @@
         in_specs=[
             pl.BlockSpec((per, own, width), lambda i: (i, 0, 0)),
             pl.BlockSpec((per, own, width), lambda i: (i, 1, 0)),
-            whole(wj), whole(ww), whole(add), whole(back)],
-        out_specs=[tall(width), tall(wide), tall(hd), tall(ffc), tall(ffc),
+            whole(wj), whole(ww), whole(add), whole(back), tall(table.shape[1])],
+        out_specs=[tall(width), tall(wide + 128), tall(ffc), tall(ffc),
                    pl.BlockSpec(payload, lambda i: (0, 0, 0))],
         out_shape=[
-            jax.ShapeDtypeStruct((rows, width), BF16), jax.ShapeDtypeStruct((rows, wide), F32),
-            jax.ShapeDtypeStruct((rows, hd), F32), jax.ShapeDtypeStruct((rows, ffc), BF16),
+            jax.ShapeDtypeStruct((rows, width), BF16), jax.ShapeDtypeStruct((rows, wide + 128), F32),
+            jax.ShapeDtypeStruct((rows, ffc), BF16),
             jax.ShapeDtypeStruct((rows, ffc), BF16), jax.ShapeDtypeStruct(payload, BF16)],
         scratch_shapes=[pltpu.VMEM((ffc, width), F32), pltpu.VMEM((ffc, width), F32),
                         pltpu.VMEM((16, ffc), F32), pltpu.VMEM((16, width), F32)],
         compiler_params=pltpu.CompilerParams(vmem_limit_bytes=VMEM),
         cost_estimate=pl.CostEstimate(flops=2 * rows * width * 1344, bytes_accessed=20 << 20, transcendentals=rows * 512),
-    )(both, both, wj, ww, add, back)
-
-
-def late_kernel(xhat_ref, up_ref, mixed_ref, out_ref, mixedT_s, sum_s):
-    rows, block = xhat_ref.shape
-    m = mixed_ref.shape[1]
-    n = out_ref.shape[1] - 16
-    hd = m // 4
-
-    @pl.when(pl.program_id(0) == 0)
-    def _():
-        mixedT_s[...] = mixed_ref[...].T
-        sum_s[...] = dot_nn(jnp.ones((16, rows), BF16), mixed_ref[...]).astype(BF16)
-
-    joint = dot_nn(mixedT_s[0:3 * hd, :], xhat_ref[...])
-    dense = dot_nn(mixedT_s[3 * hd:, :], up_ref[...].reshape(rows, block))
-    full = jnp.concatenate([joint, dense], axis=0).T.astype(BF16)
-    for b in range(block // n):
-        out_ref[b, 0:n, :] = full[b * n:(b + 1) * n]
-        out_ref[b, n:, :] = sum_s[...]
-
-
-def late_grads(xhat, both, mixed):
-    rows, width = xhat.shape
-    n, m = width // N_FSDP, mixed.shape[1]
-    block = 2 * n
-    return pl.pallas_call(
-        late_kernel,
-        grid=(width // block,),
-        in_specs=[
-            pl.BlockSpec((rows, block), lambda i: (0, i)),
-            pl.BlockSpec((both.shape[0], 128, block), lambda i: (0, 1, i)),
-            pl.BlockSpec(mixed.shape, lambda i: (0, 0))],
-        out_specs=pl.BlockSpec((2, n + 16, m), lambda i: (i, 0, 0)),
-        out_shape=jax.ShapeDtypeStruct((N_FSDP, n + 16, m), BF16),
-        scratch_shapes=[pltpu.VMEM((m, rows), BF16), pltpu.VMEM((16, m), BF16)],
-        compiler_params=pltpu.CompilerParams(vmem_limit_bytes=VMEM),
-        cost_estimate=pl.CostEstimate(flops=2 * rows * width * m, bytes_accessed=10 << 20, transcendentals=0),
-    )(xhat, both, mixed)
+    )(both, both, wj, ww, add, back, table)
 
 
 def spread_kernel(place_ref, mixed_ref, wg_ref, act_ref, wj_ref, ww_ref, dense_ref, narrow_ref, *refs):
@@ -299,20 +261,23 @@
     return out[0], out[1], out[2][0], out[3][0], out[4][0]
 
 
-def attention_kernel(order_ref, joint_ref, table_ref, grad_ref, out_ref,
-                     joint_s, table_s, grad_s, k_s, v_s, qT_s, kT_s, vT_s, gT_s,
-                     oT_s, dqT_s, dkT_s, dvT_s, cosT_s, sinT_s, out_s):
-    rows, hd = joint_ref.shape[0], joint_ref.shape[1] // 4
+def attention_kernel(order_ref, joint_ref, xhat_ref, both_ref, out_ref, late_ref,
+                     xhat_s, up_s, sems, joint_s, k_s, v_s, qT_s, kT_s, vT_s, gT_s,
+                     oT_s, dqT_s, dkT_s, dvT_s, cosT_s, sinT_s, out_s, mixedT_s):
+    rows, hd = joint_ref.shape[0], out_ref.shape[1] // 4
     slots, half, tile = N_CTX, rows // (2 * N_CTX), 256
+    own = rows // slots
     last = 2 * slots - 1
+    xhat_copy = pltpu.make_async_copy(xhat_ref, xhat_s, sems.at[0])
+    up_copy = pltpu.make_async_copy(both_ref.at[:, pl.ds(own, own), :], up_s, sems.at[1])
+    xhat_copy.start()
+    up_copy.start()
     for j in range(slots):
         p = order_ref[j]
         for h in range(2):
             src = pl.ds(j * 2 * half + h * half, half)
             dst = pl.ds(pl.multiple_of((p if h == 0 else last - p) * half, half), half)
             joint_s[dst, :] = joint_ref[src, :]
-            table_s[dst, :] = table_ref[src, :]
-            grad_s[dst, :] = grad_ref[src, :]
     scale = hd ** -0.5
 
     def spin(t, c, s):
@@ -321,8 +286,7 @@
     for i in range(rows // tile):
         at = pl.ds(i * tile, tile)
         jT = joint_s[at, :].T
-        tT = table_s[at, :].T
-        c, s = tT[0:8], tT[8:16]
+        c, s = jT[4 * hd:4 * hd + 8], jT[4 * hd + 8:4 * hd + 16]
         cosT_s[:, at] = c
         sinT_s[:, at] = s
         qT = spin(jT[0:hd], c, s).astype(BF16)
@@ -333,7 +297,7 @@
         vT_s[:, at] = vT
         k_s[at, :] = kT.astype(F32).T.astype(BF16)
         v_s[at, :] = vT.astype(F32).T.astype(BF16)
-        gT_s[:, at] = grad_s[at, :].T.astype(BF16)
+        gT_s[:, at] = jT[3 * hd:4 * hd].astype(BF16)
     dkT_s[...] = jnp.zeros_like(dkT_s)
     dvT_s[...] = jnp.zeros_like(dvT_s)
     key_at = lax.broadcasted_iota(jnp.int32, (tile, tile), 0)
@@ -372,20 +336,38 @@
             dst = pl.ds(j * 2 * half + h * half, half)
             src = pl.ds(pl.multiple_of((p if h == 0 else last - p) * half, half), half)
             out_ref[dst, :] = out_s[src, :]
-
-
-def attention(order, joint, table, grad):
-    rows, hd = joint.shape[0], joint.shape[1] // 4
+    mixedT_s[...] = out_ref[...].T
+    n = late_ref.shape[1] - 16
+    sums = dot(jnp.ones((16, rows), BF16), out_ref[...]).astype(BF16)
+    xhat_copy.wait()
+    up_copy.wait()
+    for i in range(late_ref.shape[0] * n // tile):
+        at = slice(i * tile, (i + 1) * tile)
+        joint = dot(mixedT_s[0:3 * hd, :], xhat_s[:, at])
+        dense = dot(mixedT_s[3 * hd:, :], up_s[:, :, at].reshape(rows, tile))
+        full = jnp.concatenate([joint, dense], axis=0).T.astype(BF16)
+        for b in range(tile // n):
+            late_ref[i * (tile // n) + b, 0:n, :] = full[b * n:(b + 1) * n]
+            late_ref[i * (tile // n) + b, n:, :] = sums
+
+
+def attention(order, joint, xhat, both):
+    rows, width = xhat.shape
+    hd = width // HEADS
+    own = rows // N_CTX
     vmem = pl.BlockSpec(memory_space=pltpu.VMEM)
+    anywhere = pl.BlockSpec(memory_space=pl.ANY)
     return pl.pallas_call(
         attention_kernel,
-        out_shape=jax.ShapeDtypeStruct((rows, 4 * hd), BF16),
-        in_specs=[pl.BlockSpec(memory_space=pltpu.SMEM), vmem, vmem, vmem],
-        out_specs=vmem,
+        out_shape=[jax.ShapeDtypeStruct((rows, 4 * hd), BF16),
+                   jax.ShapeDtypeStruct((N_FSDP, width // N_FSDP + 16, 4 * hd), BF16)],
+        in_specs=[pl.BlockSpec(memory_space=pltpu.SMEM), vmem, anywhere, anywhere],
+        out_specs=[vmem, vmem],
         scratch_shapes=[
-            pltpu.VMEM((rows, 4 * hd), F32),
-            pltpu.VMEM((rows, 16), F32),
-            pltpu.VMEM((rows, hd), F32),
+            pltpu.VMEM((rows, width), BF16),
+            pltpu.VMEM((N_CTX, own, width), BF16),
+            pltpu.SemaphoreType.DMA((2,)),
+            pltpu.VMEM(joint.shape, F32),
             pltpu.VMEM((rows, hd), BF16),
             pltpu.VMEM((rows, hd), BF16),
             pltpu.VMEM((hd, rows), BF16),
@@ -399,10 +381,11 @@
             pltpu.VMEM((8, rows), F32),
             pltpu.VMEM((8, rows), F32),
             pltpu.VMEM((rows, 4 * hd), BF16),
+            pltpu.VMEM((4 * hd, rows), BF16),
         ],
         compiler_params=pltpu.CompilerParams(vmem_limit_bytes=VMEM),
-        cost_estimate=pl.CostEstimate(flops=7 * rows * rows * hd, bytes_accessed=8 << 20, transcendentals=rows * rows // 2),
-    )(order, joint, table, grad)
+        cost_estimate=pl.CostEstimate(flops=8 * rows * rows * hd, bytes_accessed=14 << 20, transcendentals=rows * rows // 2),
+    )(order, joint, xhat, both)
 
 
 def shards(
@@ -439,9 +422,9 @@
     slices = slices.reshape(width, part.shape[1])
     back_w = jnp.concatenate([dense_w, narrow_w], axis=0)
 
-    steps = jnp.arange(8, dtype=F32)
-    angles = place_all[:, None] * (ROTARY_BASE ** (-2.0 * steps / 16))
-    table = jnp.concatenate([jnp.cos(angles), jnp.sin(angles)], axis=1)
+    lane = jnp.arange(128)[None, :]
+    angles = place_all[:, None] * (ROTARY_BASE ** (-2.0 * (lane % 8).astype(F32) / 16))
+    table = jnp.where(lane < 8, jnp.cos(angles), jnp.sin(angles))
     order = block_pairs[0]
 
     wj = slices[:, :4 * hd].astype(F32)
@@ -461,21 +444,20 @@
     dense_p = jnp.pad(dense_w, ((3 * hd, 0), (0, 0)))
 
     both, table, dense_p = tie(both, table, dense_p)
-    xhat, joint, att_grad, act, wg, early = project(both, wj_g, ww_g, shifted, back_w)
+    xhat, joint, act, wg, early = project(both, wj_g, ww_g, shifted, back_w, table)
     early = lax.all_to_all(early, "fsdp", 0, 0, tiled=True)
 
-    mixed = attention(order, joint, table, att_grad)
+    mixed, late = attention(order, joint, xhat, both)
     core = (c % 2)[None]
     shares = (mixed, wg, act, wj_g, ww_g, dense_p, narrow_w)
     place = lambda parity: jnp.stack([c // 4, (c // 2) % 2, parity]).astype(jnp.int32)
     other = spread(place(1 - c % 2), *shares)
-    other, early = tie(other, early)
+    other, early, late = tie(other, early, late)
 
     early = jnp.sum(early.astype(F32), axis=0)
     bias_grad = early[d_own, ffc:ffc + d_own]
     early_all = lax.all_gather(early.astype(BF16), "ctx", axis=0)
-    late, other = tie(late_grads(xhat, both, mixed), move(other, OTHER_CORE))
-    near, far, *outs = spread(place(c % 2), *shares, other)
+    near, far, *outs = spread(place(c % 2), *shares, move(other, OTHER_CORE))
 
     late, near, far, *outs = tie(lax.all_to_all(late, "fsdp", 0, 0, tiled=True), near, far, *outs)
 

time: 240 us -> 239 us (level)
  waiting for transfers between devices: 27.7 us -> 22.3 us
  other arithmetic: 14.4 us -> 19.1 us
    select_n x0 -> x1, other arithmetic: none -> 4.99 us  [shards(): table = jnp.where(lane < 8, jnp.cos(angles), jnp.sin(angles))]
    all_gather x1, waiting for transfers between devices: 13.6 us -> 9.13 us  [shards(): lax.all_gather(jnp.concatenate([own_tokens, own_up], axis=0), 'ctx', axis=0)]
    pallas_call x2 -> x1, Pallas kernels: 22 us -> 20.3 us  [attention(): pl.pallas_call(attention_kernel, out_shape=[jax.ShapeDtypeStruct((rows, 4...]
  transfers between devices with their start and end apart: 18 -> 18, of which waited for: 5 -> 5; matrix products, arithmetic and copies ran while one was open for 10% -> 11% of each run, Pallas kernels for 18% -> 18%
where the time goes in v5:
time: 239 us; the launch traced here: 237 us
  starting transfers between devices  70.6 us (30%)
  Pallas kernels  60.3 us (25%)
  blocking collectives  35.9 us (15%)
  waiting for transfers between devices  22.3 us (9%)
  other arithmetic  19.1 us (8%)
  between operations  14.5 us (6%)
  local copies, waits for them, and re-layouts  14 us (6%)
    all_gather x1, blocking collectives, shards(): lax.all_gather(rotary_place[0], 'ctx', axis=0, tiled=True).astype(F32)  35.9 us
    all_to_all x1, starting transfers between devices, gather_chips(): lax.all_to_all(jnp.broadcast_to(own[None], (N_CTX // 2,) + own.shape), 'c...  25.6 us
    pallas_call x1, Pallas kernels, attention(): pl.pallas_call(attention_kernel, out_shape=[jax.ShapeDtypeStruct((rows, 4...  20.3 us
    pallas_call x2, Pallas kernels, spread(): pl.pallas_call(spread_kernel, grid_spec=pltpu.PrefetchScalarGridSpec(num_...  16 us
    pallas_call x1, Pallas kernels, project(): pl.pallas_call(project_kernel, grid=(slots // per,), in_specs=[pl.BlockSp...  14.7 us
    ppermute x2, starting transfers between devices, turn(): return lax.ppermute(v, ('ctx', 'fsdp'), TURN)  14.3 us
    pallas_call x2, Pallas kernels, finish(): pl.pallas_call(kernel, in_specs=[pl.BlockSpec(memory_space=pltpu.SMEM)] *...  9.38 us
    all_gather x1, waiting for transfers between devices, shards(): lax.all_gather(jnp.concatenate([own_tokens, own_up], axis=0), 'ctx', axis=0)  9.13 us
  transfers between devices with their start and end apart: 18, of which 5 were waited for; matrix products, arithmetic and copies ran while one was open for 11% of the time, Pallas kernels for 18%

profile of v5, /device:TPU:22, one launch (start us, length us, event | category | flops | bytes accessed | tf_op | source)
XLA Modules:
  0.0 236.7 jit_solution(3464816987554030935)
XLA Ops:
  7.3 1.9 pad_maximum_fusion.1
  9.3 0.4 copy.53
  9.8 0.1 copy.55
  10.0 0.1 copy.56
  10.1 0.1 copy.57
  10.2 0.1 copy.58
  10.4 0.1 copy.59
  10.5 0.1 copy.60
  10.7 0.2 reshape.140
  11.0 0.8 constant_dynamic-slice_fusion
  11.8 1.0 constant_dynamic-slice_fusion.2
  12.9 0.2 concatenate.23
  13.1 1.2 broadcast_in_dim.94
  14.4 7.3 %all-to-all-start = ((bf16[8,128,768]{2,1,0:T(8,128)(2,1)}), bf16[8,128,768]{2,1,0:T(8,128)(2,1)S(1)}, u32[]{:S(2)}, u32[]{:S(2)}) async-start(bf16[8,128,768]{2,1,0:T(8,128)(2,1)} %broadcast_in_dim.94), calls=%async_computation | async-start | bytes 3145728 | tf_op jit(solution)/shard_map/all_to_all | solution.py:417
  21.7 4.6 %collective-permute-start = (bf16[64,1024]{1,0:T(8,128)(2,1)S(1)}, bf16[64,1024]{1,0:T(8,128)(2,1)S(1)}, u32[]{:S(2)}, u32[]{:S(2)}) collective-permute-start(bf16[64,1024]{1,0:T(8,128)(2,1)S(1)} %constant_dynamic-slice_fusion.11), channel_id=1, source_target_pairs={{0,0},{1,16},{2,32},{3,48},{4,64},{5,80},{6,96},{7,112},{8,8},{9,2... | collective-permute-start | bytes 393224 | tf_op jit(solution)/shard_map/ppermute | solution.py:30
  26.3 35.9 %all-gather.1 = s32[1,2048]{1,0:T(1,128)S(1)} all-gather(s32[1,128]{1,0:T(1,128)S(1)} %copy-done.18), channel_id=3, replica_groups=mesh['ctx'=16,'fsdp'=8] {'ctx'}, dimensions={1}, use_global_device_ids=true | all-gather | bytes 8704 | tf_op jit(solution)/shard_map/all_gather | solution.py:419
  62.3 5.0 %fusion.2.table_ref = f32[2048,128]{1,0:T(8,128)} fusion(f32[128]{0:T(128)S(1)} %fusion.22, f32[2048]{0:T(1024)S(1)} %bitcast.94, pred[128]{0:T(512)(128)(4,1)S(1)} %iota_compare_fusion.1), kind=kLoop, calls=%fused_computation.8 | loop fusion | flops 524288 | bytes 1057408 | tf_op jit(solution)/shard_map/jit(_where)/select_n | solution.py:427
  67.3 0.9 pad.8.dense_ref
  68.3 0.2 slice.121
  68.5 0.2 slice.119
  68.7 0.2 reshape_reshape.3
  69.0 0.3 reshape.143
  69.5 1.6 slice_reduce_fusion.1
  71.1 1.7 multiply_reduce_fusion
  72.8 0.6 pad_maximum_fusion.5
  73.5 1.0 pad_maximum_fusion.back_ref
  74.4 9.1 %all-gather.6.cloned.1.call-done = bf16[4096,1024]{1,0:T(8,128)(2,1)} async-done(((bf16[256,1024]{1,0:T(8,128)(2,1)}), bf16[4096,1024]{1,0:T(8,128)(2,1)}) %all-gather.6.cloned.1.call-update) | async-done | bytes 8388624 | tf_op jit(solution)/shard_map/all_gather | solution.py:407
  83.5 14.7 %shard_map.263 = (bf16[2048,1024]{1,0:T(8,128)(2,1)}, f32[2048,384]{1,0:T(8,128)}, bf16[2048,256]{1,0:T(8,128)(2,1)}, bf16[2048,256]{1,0:T(8,128)(2,1)}, bf16[8,144,512]{2,1,0:T(8,128)(2,1)}) custom-call(bf16[16,256,1024]{2,1,0:T(8,128)(2,1)} %bitcast.74, bf16[16,256,1024]{2,1,0:T(8,128)(2,1)} %bitcast.75, bf16[1024,256]{1,0:T(8,128)(2,1)} %get-tuple-element.106.wj_ref, ...), custom_call_target="tpu_custom_call" | custom-call | flops 5637144576 | bytes 20971520 | tf_op jit(solution)/shard_map/pallas_call | solution.py:111
  98.2 9.0 %all-to-all-start.1 = ((bf16[8,144,512]{2,1,0:T(8,128)(2,1)}), bf16[8,144,512]{2,1,0:T(8,128)(2,1)S(1)}, u32[]{:S(2)}, u32[]{:S(2)}) async-start(bf16[8,144,512]{2,1,0:T(8,128)(2,1)} %get-tuple-element.63), calls=%async_computation.1 | async-start | bytes 2359296 | tf_op jit(solution)/shard_map/all_to_all | solution.py:448
  107.2 0.6 pad_add_fusion.1.place_ref
  107.8 20.3 %shard_map.264 = (bf16[2048,256]{1,0:T(8,128)(2,1)}, bf16[8,144,256]{2,1,0:T(8,128)(2,1)}) custom-call(s32[16]{0:T(128)} %bitcast.96, f32[2048,384]{1,0:T(8,128)} %get-tuple-element.57.joint_ref, bf16[2048,1024]{1,0:T(8,128)(2,1)} %get-tuple-element.58.xhat_ref, bf16[16,256,1024]{2,1,0:T(8,128)(2,1)} %bitcast.76), custom_call_target="tpu_custom_call" | custom-call | flops 2147483648 | bytes 14680064 | tf_op jit(solution)/shard_map/pallas_call | solution.py:360
  128.1 7.3 %shard_map.265 = bf16[2,8,128,1024]{3,2,1,0:T(8,128)(2,1)} custom-call(s32[3]{0:T(128)} %pad_add_fusion.1.place_ref, bf16[8,2,128,256]{3,2,1,0:T(8,128)(2,1)} %bitcast.87, bf16[8,2,128,256]{3,2,1,0:T(8,128)(2,1)} %bitcast.85, bf16[8,2,128,256]{3,2,1,0:T(8,128)(2,1)} %bitcast.83, bf16[1024,256]{1,0:T(8,128)(2,1)} %get-tuple-element.106.wj_ref, ...), custom_call_target="tpu_custom_call" | custom-call | flops 2147483648 | bytes 9437184 | tf_op jit(solution)/shard_map/pallas_call | solution.py:174
  135.4 0.2 convert_reduce_fusion
  135.5 0.7 convert_element_type.129
  136.3 7.2 %all-to-all-start.2 = ((bf16[8,144,256]{2,1,0:T(8,128)(2,1)}), bf16[8,144,256]{2,1,0:T(8,128)(2,1)S(1)}, u32[]{:S(2)}, u32[]{:S(2)}) async-start(bf16[8,144,256]{2,1,0:T(8,128)(2,1)} %get-tuple-element.65), calls=%async_computation.2 | async-start | bytes 1179648 | tf_op jit(solution)/shard_map/all_to_all | solution.py:462
  143.5 0.6 pad_add_fusion.3.place_ref
  144.1 8.7 %shard_map.266 = (bf16[4,128,1024]{2,1,0:T(8,128)(2,1)}, bf16[4,128,1024]{2,1,0:T(8,128)(2,1)}, bf16[2,128,1024]{2,1,0:T(8,128)(2,1)}, bf16[2,128,1024]{2,1,0:T(...) custom-call(s32[3]{0:T(128)} %pad_add_fusion.3.place_ref, bf16[8,2,128,256]{3,2,1,0:T(8,128)(2,1)} %bitcast.88, ...), custom_call_target="tpu_custom_call" | custom-call | flops 2147483648 | bytes 9437184 | tf_op jit(solution)/shard_map/pallas_call | solution.py:174
  153.2 9.7 %collective-permute-start.2 = (bf16[144,64]{1,0:T(8,128)(2,1)S(1)}, bf16[144,64]{1,0:T(8,128)(2,1)S(1)}, u32[]{:S(2)}, u32[]{:S(2)}) collective-permute-start(bf16[144,64]{1,0:T(8,128)(2,1)S(1)} %slice.127), channel_id=1, source_target_pairs={{0,0},{1,16},{2,32},{3,48},{4,64},{5,80},{6,96},{7,112},{8,8},{9,2... | collective-permute-start | bytes 55304 | tf_op jit(solution)/shard_map/ppermute | solution.py:30
  163.0 0.7 copy.61.gain_ref
  163.7 0.7 copy.62.shift_ref
  164.4 0.7 copy.63.gain_ref
  165.2 0.7 copy.64.shift_ref
  165.9 0.3 collective-permute-start.4
  166.2 3.0 %collective-permute-start.6 = (bf16[2,128,1024]{2,1,0:T(8,128)(2,1)}, bf16[2,128,1024]{2,1,0:T(8,128)(2,1)}, u32[]{:S(2)}, u32[]{:S(2)}) collective-permute-start(bf16[2,128,1024]{2,1,0:T(8,128)(2,1)} %get-tuple-element.78), channel_id=1, source_target_pairs={{0,96},{8,104},{16,112},{24,120},{32,0},{40,8},{48,16},{56,24},{64... | collective-permute-start | bytes 1572872 | tf_op jit(solution)/shard_map/ppermute | solution.py:34
  169.2 0.9 broadcast_in_dim.98
  170.1 25.6 %all-to-all-start.3 = ((bf16[8,144,256]{2,1,0:T(8,128)(2,1)}), bf16[8,144,256]{2,1,0:T(8,128)(2,1)S(1)}, u32[]{:S(2)}, u32[]{:S(2)}) async-start(bf16[8,144,256]{2,1,0:T(8,128)(2,1)} %broadcast_in_dim.98), calls=%async_computation.3 | async-start | bytes 1179648 | tf_op jit(solution)/shard_map/all_to_all | solution.py:38
  195.7 0.2 fusion.12
  196.0 5.5 %shard_map.268 = (f32[128,4096]{1,0:T(8,128)}, f32[512,1024]{1,0:T(8,128)}, f32[1,128]{1,0:T(1,128)}, f32[1,128]{1,0:T(1,128)}, f32[1,512]{1,0:T(1,128)}) custom-call(s32[1]{0:T(128)} %bitcast.31.f_ref, bf16[16,144,512]{2,1,0:T(8,128)(2,1)} %bitcast.89, bf16[128,4096]{1,0:T(8,128)(2,1)} %weight_ref.3, f32[128,1]{1,0:T(8,128)} %copy.63.gain_ref, ...), custom_call_target="tpu_custom_call" | custom-call | flops 4194304 | bytes 6291456 | tf_op jit(solution)/shard_map/pallas_call | solution.py:251
  201.6 4.3 %all-to-all-done.3.mine_ref = bf16[8,144,256]{2,1,0:T(8,128)(2,1)S(1)} async-done(((bf16[8,144,256]{2,1,0:T(8,128)(2,1)}), bf16[8,144,256]{2,1,0:T(8,128)(2,1)S(1)}, u32[]{:S(2)}, u32[]{:S(2)}) %all-to-all-start.3) | async-done | bytes 589856 | tf_op jit(solution)/shard_map/all_to_all | solution.py:38
  205.9 1.8 add_convert_fusion
  207.8 0.9 collective-permute-start.10
  208.8 1.3 collective-permute-start.9
  210.0 0.1 collective-permute-start.8
  210.2 1.5 convert_add_fusion
  211.8 1.3 collective-permute-start.7
  213.1 3.9 %collective-permute-done.10 = bf16[128,1024]{1,0:T(8,128)(2,1)S(1)} collective-permute-done((bf16[128,1024]{1,0:T(8,128)(2,1)S(1)}, bf16[128,1024]{1,0:T(8,128)(2,1)S(1)}, u32[]{:S(2)}, u32[]{:S(2)}) %collective-permute-start.10) | collective-permute-done | bytes 262176 | tf_op jit(solution)/shard_map/ppermute | solution.py:34
  217.0 2.2 collective-permute-done.9
  219.1 2.7 %collective-permute-done.8 = bf16[128,1024]{1,0:T(8,128)(2,1)S(1)} collective-permute-done((bf16[128,1024]{1,0:T(8,128)(2,1)S(1)}, bf16[128,1024]{1,0:T(8,128)(2,1)S(1)}, u32[]{:S(2)}, u32[]{:S(2)}) %collective-permute-start.8) | collective-permute-done | bytes 262176 | tf_op jit(solution)/shard_map/ppermute | solution.py:34
  221.9 0.3 fusion.23
  222.2 1.2 fusion.11
  223.4 0.8 copy-done.8
  224.2 3.8 %shard_map.267 = (f32[128,3072]{1,0:T(8,128)}, f32[128,1024]{1,0:T(8,128)}, f32[1,128]{1,0:T(1,128)}, f32[1,128]{1,0:T(1,128)}, f32[1,384]{1,0:T(1,128)}) custom-call(s32[1]{0:T(128)} %bitcast.31.f_ref, s32[1]{0:T(128)} %bitcast.22.core_ref, bf16[8,144,256]{2,1,0:T(8,128)(2,1)} %copy-done.5, bf16[8,144,256]{2,1,0:T(8,128)(2,1)} %copy-done.8, ...), custom_call_target="tpu_custom_call" | custom-call | flops 3145728 | bytes 4718592 | tf_op jit(solution)/shard_map/pallas_call | solution.py:251
  228.1 1.3 reduce.9
  229.3 0.5 copy.66
  (93 shorter events, 1.5 us)
Async XLA Ops:
  7.2 14.5 %copy-start = (bf16[128,1024]{1,0:T(8,128)(2,1)S(1)}, bf16[128,1024]{1,0:T(8,128)(2,1)}, u32[]{:S(2)}) copy-start(bf16[128,1024]{1,0:T(8,128)(2,1)} %param.24) | copy-start | bytes 786436
  7.2 2.1 copy-start.4
  7.2 2.6 %copy-start.14 = (bf16[128]{0:T(256)(128)(2,1)S(1)}, bf16[128]{0:T(256)(128)(2,1)}, u32[]{:S(2)}) copy-start(bf16[128]{0:T(256)(128)(2,1)} %param.20) | copy-start | bytes 772
  7.2 2.7 %copy-start.15 = (bf16[128]{0:T(256)(128)(2,1)S(1)}, bf16[128]{0:T(256)(128)(2,1)}, u32[]{:S(2)}) copy-start(bf16[128]{0:T(256)(128)(2,1)} %param.21) | copy-start | bytes 772
  7.2 2.9 %copy-start.16 = (bf16[128]{0:T(256)(128)(2,1)S(1)}, bf16[128]{0:T(256)(128)(2,1)}, u32[]{:S(2)}) copy-start(bf16[128]{0:T(256)(128)(2,1)} %param.26) | copy-start | bytes 772
  7.2 3.0 %copy-start.17 = (bf16[128]{0:T(256)(128)(2,1)S(1)}, bf16[128]{0:T(256)(128)(2,1)}, u32[]{:S(2)}) copy-start(bf16[128]{0:T(256)(128)(2,1)} %param.27) | copy-start | bytes 772
  7.3 3.1 %copy-start.12 = (bf16[128]{0:T(256)(128)(2,1)S(1)}, bf16[128]{0:T(256)(128)(2,1)}, u32[]{:S(2)}) copy-start(bf16[128]{0:T(256)(128)(2,1)} %param.25) | copy-start | bytes 772
  7.3 3.3 %copy-start.13 = (bf16[128]{0:T(256)(128)(2,1)S(1)}, bf16[128]{0:T(256)(128)(2,1)}, u32[]{:S(2)}) copy-start(bf16[128]{0:T(256)(128)(2,1)} %param.31) | copy-start | bytes 772
  7.3 3.4 %copy-start.10 = (bf16[384]{0:T(512)(128)(2,1)S(1)}, bf16[384]{0:T(512)(128)(2,1)}, u32[]{:S(2)}) copy-start(bf16[384]{0:T(512)(128)(2,1)} %param.23) | copy-start | bytes 2308
  7.3 3.6 %copy-start.11 = (bf16[512]{0:T(512)(128)(2,1)S(1)}, bf16[512]{0:T(512)(128)(2,1)}, u32[]{:S(2)}) copy-start(bf16[512]{0:T(512)(128)(2,1)} %param.29) | copy-start | bytes 3076
  7.3 76.3 %all-gather.6.cloned.1.call-start = ((), (), s32[]{:S(2)}) async-start(), calls=%async_computation.4 | async-start | bytes 8912896 | tf_op jit(solution)/shard_map/all_gather | solution.py:407
  14.4 12.0 %copy-start.18 = (s32[1,128]{1,0:T(1,128)S(1)}, s32[1,128]{1,0:T(1,128)}, u32[]{:S(2)}) copy-start(s32[1,128]{1,0:T(1,128)} %param.19) | copy-start | bytes 1540
  14.4 53.8 %all-to-all-start = ((bf16[8,128,768]{2,1,0:T(8,128)(2,1)}), bf16[8,128,768]{2,1,0:T(8,128)(2,1)S(1)}, u32[]{:S(2)}, u32[]{:S(2)}) async-start(bf16[8,128,768]{2,1,0:T(8,128)(2,1)} %broadcast_in_dim.94), calls=%async_computation | async-start | bytes 3145728 | tf_op jit(solution)/shard_map/all_to_all | solution.py:417
  21.7 45.6 %collective-permute-start = (bf16[64,1024]{1,0:T(8,128)(2,1)S(1)}, bf16[64,1024]{1,0:T(8,128)(2,1)S(1)}, u32[]{:S(2)}, u32[]{:S(2)}) collective-permute-start(bf16[64,1024]{1,0:T(8,128)(2,1)S(1)} %constant_dynamic-slice_fusion.11), channel_id=1, source_target_pairs={{0,0},{1,16},{2,32},{3,48},{4,64},{5,80},{6,96},{7,112},{8,8},{9,2... | collective-permute-start | bytes 393224 | tf_op jit(solution)/shard_map/ppermute | solution.py:30
  73.5 24.8 %copy-start.2 = (bf16[8,32,1024]{2,1,0:T(8,128)(2,1)}, bf16[8,32,1024]{2,1,0:T(8,128)(2,1)S(1)}, u32[]{:S(2)}) copy-start(bf16[8,32,1024]{2,1,0:T(8,128)(2,1)S(1)} %pad_maximum_fusion.2) | copy-start | bytes 1572868
  98.2 37.1 %all-to-all-start.1 = ((bf16[8,144,512]{2,1,0:T(8,128)(2,1)}), bf16[8,144,512]{2,1,0:T(8,128)(2,1)S(1)}, u32[]{:S(2)}, u32[]{:S(2)}) async-start(bf16[8,144,512]{2,1,0:T(8,128)(2,1)} %get-tuple-element.63), calls=%async_computation.1 | async-start | bytes 2359296 | tf_op jit(solution)/shard_map/all_to_all | solution.py:448
  107.2 88.8 %all-gather.8.cloned.1.call-start = ((), (), s32[]{:S(2)}) async-start(), calls=%async_computation.5 | async-start | bytes 2506752 | tf_op jit(solution)/shard_map/all_gather | solution.py:459
  135.4 8.7 %collective-permute-start.1 = (bf16[2,8,128,1024]{3,2,1,0:T(8,128)(2,1)}, bf16[2,8,128,1024]{3,2,1,0:T(8,128)(2,1)}, u32[]{:S(2)}, u32[]{:S(2)}) collective-permute-start(bf16[2,8,128,1024]{3,2,1,0:T(8,128)(2,1)} %shard_map.265), channel_id=1, source_target_pairs={{8,0},{0,8},{24,16},{16,24},{40,32},{32,40},{56,48},{48,56},{72,64... | collective-permute-start | bytes 12582920 | tf_op jit(solution)/shard_map/ppermute | solution.py:34
  136.3 16.5 %all-to-all-start.2 = ((bf16[8,144,256]{2,1,0:T(8,128)(2,1)}), bf16[8,144,256]{2,1,0:T(8,128)(2,1)S(1)}, u32[]{:S(2)}, u32[]{:S(2)}) async-start(bf16[8,144,256]{2,1,0:T(8,128)(2,1)} %get-tuple-element.65), calls=%async_computation.2 | async-start | bytes 1179648 | tf_op jit(solution)/shard_map/all_to_all | solution.py:462
  144.1 8.8 %copy-start.3 = (bf16[1,128,1024]{2,1,0:T(8,128)(2,1)S(1)}, bf16[1,128,1024]{2,1,0:T(8,128)(2,1)}, u32[]{:S(2)}) copy-start(bf16[1,128,1024]{2,1,0:T(8,128)(2,1)} %param.16) | copy-start | bytes 786436
  152.8 53.1 %collective-permute-start.3 = (bf16[4,128,1024]{2,1,0:T(8,128)(2,1)}, bf16[4,128,1024]{2,1,0:T(8,128)(2,1)}, u32[]{:S(2)}, u32[]{:S(2)}) collective-permute-start(bf16[4,128,1024]{2,1,0:T(8,128)(2,1)} %get-tuple-element.75), channel_id=1, source_target_pairs={{16,0},{24,8},{0,16},{8,24},{48,32},{56,40},{32,48},{40,56},{80,64... | collective-permute-start | bytes 3145736 | tf_op jit(solution)/shard_map/ppermute | solution.py:34
  153.2 15.9 %collective-permute-start.2 = (bf16[144,64]{1,0:T(8,128)(2,1)S(1)}, bf16[144,64]{1,0:T(8,128)(2,1)S(1)}, u32[]{:S(2)}, u32[]{:S(2)}) collective-permute-start(bf16[144,64]{1,0:T(8,128)(2,1)S(1)} %slice.127), channel_id=1, source_target_pairs={{0,0},{1,16},{2,32},{3,48},{4,64},{5,80},{6,96},{7,112},{8,8},{9,2... | collective-permute-start | bytes 55304 | tf_op jit(solution)/shard_map/ppermute | solution.py:30
  165.9 35.7 %collective-permute-start.4 = (bf16[2,128,1024]{2,1,0:T(8,128)(2,1)}, bf16[2,128,1024]{2,1,0:T(8,128)(2,1)S(1)}, u32[]{:S(2)}, u32[]{:S(2)}) collective-permute-start(bf16[2,128,1024]{2,1,0:T(8,128)(2,1)} %get-tuple-element.76), channel_id=1, source_target_pairs={{0,32},{8,40},{16,48},{24,56},{32,64},{40,72},{48,80},{56,88},{64,... | collective-permute-start | bytes 1572872 | tf_op jit(solution)/shard_map/ppermute | solution.py:34
  166.2 35.4 %collective-permute-start.5 = (bf16[2,128,1024]{2,1,0:T(8,128)(2,1)}, bf16[2,128,1024]{2,1,0:T(8,128)(2,1)}, u32[]{:S(2)}, u32[]{:S(2)}) collective-permute-start(bf16[2,128,1024]{2,1,0:T(8,128)(2,1)} %get-tuple-element.77), channel_id=1, source_target_pairs={{0,64},{8,72},{16,80},{24,88},{32,96},{40,104},{48,112},{56,120},{... | collective-permute-start | bytes 1572872 | tf_op jit(solution)/shard_map/ppermute | solution.py:34
  166.2 35.4 %collective-permute-start.6 = (bf16[2,128,1024]{2,1,0:T(8,128)(2,1)}, bf16[2,128,1024]{2,1,0:T(8,128)(2,1)}, u32[]{:S(2)}, u32[]{:S(2)}) collective-permute-start(bf16[2,128,1024]{2,1,0:T(8,128)(2,1)} %get-tuple-element.78), channel_id=1, source_target_pairs={{0,96},{8,104},{16,112},{24,120},{32,0},{40,8},{48,16},{56,24},{64... | collective-permute-start | bytes 1572872 | tf_op jit(solution)/shard_map/ppermute | solution.py:34
  170.1 35.8 %all-to-all-start.3 = ((bf16[8,144,256]{2,1,0:T(8,128)(2,1)}), bf16[8,144,256]{2,1,0:T(8,128)(2,1)S(1)}, u32[]{:S(2)}, u32[]{:S(2)}) async-start(bf16[8,144,256]{2,1,0:T(8,128)(2,1)} %broadcast_in_dim.98), calls=%async_computation.3 | async-start | bytes 1179648 | tf_op jit(solution)/shard_map/all_to_all | solution.py:38
  195.7 10.2 %copy-start.6 = (bf16[4,128,1024]{2,1,0:T(8,128)(2,1)S(1)}, bf16[4,128,1024]{2,1,0:T(8,128)(2,1)}, u32[]{:S(2)}) copy-start(bf16[4,128,1024]{2,1,0:T(8,128)(2,1)} %get-tuple-element.82) | copy-start | bytes 3145732
  196.0 33.4 %copy-start.19 = (f32[128]{0:T(128)}, f32[128]{0:T(128)S(1)}, u32[]{:S(2)}) copy-start(f32[128]{0:T(128)S(1)} %slice_bitcast_fusion.5) | copy-start | bytes 1540
  201.5 8.6 %copy-start.9 = (bf16[2,128,1024]{2,1,0:T(8,128)(2,1)S(1)}, bf16[2,128,1024]{2,1,0:T(8,128)(2,1)}, u32[]{:S(2)}) copy-start(bf16[2,128,1024]{2,1,0:T(8,128)(2,1)} %get-tuple-element.73) | copy-start | bytes 1572868
  205.9 7.2 %copy-start.5 = (bf16[8,144,256]{2,1,0:T(8,128)(2,1)}, bf16[8,144,256]{2,1,0:T(8,128)(2,1)S(1)}, u32[]{:S(2)}) copy-start(bf16[8,144,256]{2,1,0:T(8,128)(2,1)S(1)} %all-to-all-done.3.mine_ref) | copy-start | bytes 1769476
  207.8 9.1 %collective-permute-start.10 = (bf16[128,1024]{1,0:T(8,128)(2,1)S(1)}, bf16[128,1024]{1,0:T(8,128)(2,1)S(1)}, u32[]{:S(2)}, u32[]{:S(2)}) collective-permute-start(bf16[128,1024]{1,0:T(8,128)(2,1)S(1)} %get-tuple-element.113), channel_id=1, source_target_pairs={{0,96},{8,104},{16,112},{24,120},{32,0},{40,8},{48,16},{56,24},{64... | collective-permute-start | bytes 786440 | tf_op jit(solution)/shard_map/ppermute | solution.py:34
  208.8 10.4 %collective-permute-start.9 = (bf16[128,1024]{1,0:T(8,128)(2,1)S(1)}, bf16[128,1024]{1,0:T(8,128)(2,1)S(1)}, u32[]{:S(2)}, u32[]{:S(2)}) collective-permute-start(bf16[128,1024]{1,0:T(8,128)(2,1)S(1)} %get-tuple-element.114), channel_id=1, source_target_pairs={{0,64},{8,72},{16,80},{24,88},{32,96},{40,104},{48,112},{56,120},{... | collective-permute-start | bytes 786440 | tf_op jit(solution)/shard_map/ppermute | solution.py:34
  210.0 12.2 %copy-start.7 = (bf16[1,128,1024]{2,1,0:T(8,128)(2,1)S(1)}, bf16[1,128,1024]{2,1,0:T(8,128)(2,1)}, u32[]{:S(2)}) copy-start(bf16[1,128,1024]{2,1,0:T(8,128)(2,1)} %param.17) | copy-start | bytes 786436
  210.0 11.8 %collective-permute-start.8 = (bf16[128,1024]{1,0:T(8,128)(2,1)S(1)}, bf16[128,1024]{1,0:T(8,128)(2,1)S(1)}, u32[]{:S(2)}, u32[]{:S(2)}) collective-permute-start(bf16[128,1024]{1,0:T(8,128)(2,1)S(1)} %get-tuple-element.112), channel_id=1, source_target_pairs={{0,32},{8,40},{16,48},{24,56},{32,64},{40,72},{48,80},{56,88},{64,... | collective-permute-start | bytes 786440 | tf_op jit(solution)/shard_map/ppermute | solution.py:34
  211.8 10.4 %collective-permute-start.7 = (bf16[128,1024]{1,0:T(8,128)(2,1)S(1)}, bf16[128,1024]{1,0:T(8,128)(2,1)S(1)}, u32[]{:S(2)}, u32[]{:S(2)}) collective-permute-start(bf16[128,1024]{1,0:T(8,128)(2,1)S(1)} %fusion.17), channel_id=1, source_target_pairs={{16,0},{24,8},{0,16},{8,24},{48,32},{56,40},{32,48},{40,56},{80,64... | collective-permute-start | bytes 786440 | tf_op jit(solution)/shard_map/ppermute | solution.py:34
  213.1 10.3 %collective-permute-start.11 = (bf16[8,144,256]{2,1,0:T(8,128)(2,1)S(1)}, bf16[8,144,256]{2,1,0:T(8,128)(2,1)S(1)}, u32[]{:S(2)}, u32[]{:S(2)}) collective-permute-start(bf16[8,144,256]{2,1,0:T(8,128)(2,1)S(1)} %all-to-all-done.3.mine_ref), channel_id=1, source_target_pairs={{8,0},{0,8},{24,16},{16,24},{40,32},{32,40},{56,48},{48,56},{72,64... | collective-permute-start | bytes 1769480 | tf_op jit(solution)/shard_map/ppermute | solution.py:34
  222.2 7.7 %copy-start.1 = (bf16[128,1024]{1,0:T(8,128)(2,1)S(1)}, bf16[128,1024]{1,0:T(8,128)(2,1)}, u32[]{:S(2)}) copy-start(bf16[128,1024]{1,0:T(8,128)(2,1)} %param.24) | copy-start | bytes 786436
  223.4 0.8 copy-start.8
Sparse Core Ops, SparseCore 0:
  10.4 73.0 all-gather.5
  136.4 47.0 all-gather.7
